TPU v7x, 1024 devices: a whole 4x4x32 slice. The times are simulated.
1024 devices in a mesh: dp: 32 (over z_hi, y, core), section: 4 (over x), mp: 8 (over z_lo).
Axes of the slice: x: 4, y: 4, z: 32 (z_hi: 4, z_lo: 8; z = z_hi * 8 + z_lo), core: 2. Of those that a mesh axis runs over, the one named last changes fastest.
Arguments:
- queries: bfloat16 [4, 64, 128, 4096], P('section', 'dp', None, 'mp'), may hold values from -72 to 72
- latents: bfloat16 [64, 192, 1536], P('dp', None, ('section', 'mp')), may hold values from -6 to 6
- kv_weight: bfloat16 [4, 1536, 2, 4096], P('section', None, None, 'mp'), may hold values from -0.15625 to 0.15625
- token_image: int32 [64, 128], P('dp'), may hold values from 0 to 2
- image_counts: int32 [64], P('dp'), may hold values from 1 to 3, as said below
- out_grad: bfloat16 [4, 64, 128, 4096], P('section', 'dp', None, 'mp'), may hold values from -6 to 6
Outputs:
- attended: bfloat16 [4, 64, 128, 4096], P('section', 'dp', None, 'mp')
- kv_grad: float32 [4, 1536, 2, 4096], P('section', 'dp', None, 'mp')
- latent_grad: float32 [64, 192, 1536], P('dp', None, ('section', 'mp'))
Inputs may be any that keep to these rules, and one draw needn't show every extreme that they name: `image_counts`: every value is at most 3, and the first sample has 3 images.
All inputs are finite; a program needn't handle non-finite values.
Results may differ from a plain program's by a relative error of at most 0.022.
Values may be sent and summed in bfloat16 or wider, within the bound.
No kernel may reach another device: no remote copies, remote signals or barrier semaphores. Data moves between devices by JAX's collectives and lax.ppermute only.
A program may use at most 32 MiB of HBM per device.

v0:
```python
import jax
import jax.numpy as jnp
from jax import lax
from jax.sharding import PartitionSpec as P

HEAD = 128
LATENTS = 64


def attend(query_rows, kv_rounded, token_rows, count_rows, grad_rows):
    samples, text_len, width = query_rows.shape
    key_count = kv_rounded.shape[1]
    scale = HEAD ** (-0.5)
    query_heads = query_rows.reshape(samples, text_len, -1, HEAD)
    key_heads = kv_rounded[:, :, 0].reshape(samples, key_count, -1, HEAD)
    value_heads = kv_rounded[:, :, 1].reshape(samples, key_count, -1, HEAD)
    grad_heads = grad_rows.reshape(samples, text_len, -1, HEAD)
    image_of = jnp.arange(key_count) // LATENTS
    allowed = (image_of[None, None, :] == token_rows[:, :, None]) & (
        image_of[None, None, :] < count_rows[:, None, None]
    )
    allowed = allowed[:, None]
    scores = (
        jnp.einsum("bthe,brhe->bhtr", query_heads, key_heads, preferred_element_type=jnp.float32)
        * scale
    )
    row_top = jnp.max(jnp.where(allowed, scores, -1e30), axis=-1, keepdims=True)
    expval = jnp.exp(jnp.where(allowed, scores - row_top, -jnp.inf))
    totals = jnp.sum(expval, axis=-1, keepdims=True)
    attn_prob = expval / jnp.where(totals > 0, totals, 1.0)
    prob_bf = attn_prob.astype(jnp.bfloat16)
    output = jnp.einsum("bhtr,brhe->bthe", prob_bf, value_heads, preferred_element_type=jnp.float32)
    output = output.reshape(samples, text_len, width).astype(jnp.bfloat16)
    dprob = jnp.einsum(
        "bthe,brhe->bhtr", grad_heads, value_heads, preferred_element_type=jnp.float32
    )
    dscore = (
        attn_prob * (dprob - jnp.sum(dprob * attn_prob, axis=-1, keepdims=True)) * scale
    ).astype(jnp.bfloat16)
    dkeys = jnp.einsum("bhtr,bthe->brhe", dscore, query_heads, preferred_element_type=jnp.float32)
    dvalues = jnp.einsum("bhtr,bthe->brhe", prob_bf, grad_heads, preferred_element_type=jnp.float32)
    dkv = jnp.stack(
        [dkeys.reshape(samples, key_count, width), dvalues.reshape(samples, key_count, width)],
        axis=2,
    )
    return (output, dkv.astype(jnp.bfloat16))


def body(queries, latents, kv_weight, token_image, image_counts, out_grad):
    gathered = lax.all_gather(latents, ("section", "mp"), axis=2, tiled=True)
    samples, key_count, width = gathered.shape
    local_features = kv_weight.shape[-1]
    weights = kv_weight.reshape(width, 2 * local_features)
    flat_lat = gathered.reshape(samples * key_count, width)
    kv_rounded = jnp.dot(flat_lat, weights, preferred_element_type=jnp.float32).astype(jnp.bfloat16)
    kv_rounded = kv_rounded.reshape(samples, key_count, 2, local_features)
    attended, dkv = attend(queries[0], kv_rounded, token_image, image_counts, out_grad[0])
    dflat = dkv.reshape(samples * key_count, 2 * local_features)
    kv_grad = lax.psum_scatter(
        lax.dot_general(
            flat_lat, dflat, (((0,), (0,)), ((), ())), preferred_element_type=jnp.float32
        ).astype(jnp.bfloat16),
        "dp",
        scatter_dimension=0,
        tiled=True,
    ).astype(jnp.float32)
    lat_term = lax.dot_general(
        dflat, weights, (((1,), (1,)), ((), ())), preferred_element_type=jnp.float32
    )
    latent_grad = lax.psum_scatter(lat_term, ("section", "mp"), scatter_dimension=1, tiled=True)
    return (
        attended[None],
        kv_grad.reshape(1, -1, 2, local_features),
        latent_grad.reshape(samples, key_count, -1),
    )


def solution(mesh):
    return jax.shard_map(
        body,
        mesh=mesh,
        in_specs=(
            P("section", "dp", None, "mp"),
            P("dp", None, ("section", "mp")),
            P("section", None, None, "mp"),
            P("dp", None),
            P("dp"),
            P("section", "dp", None, "mp"),
        ),
        out_specs=(
            P("section", "dp", None, "mp"),
            P("section", "dp", None, "mp"),
            P("dp", None, ("section", "mp")),
        ),
        check_vma=False,
    )
```

profile of v0, /device:TPU:2, one launch (start us, length us, event | category | flops | bytes accessed | tf_op | source)
XLA Modules:
  0.0 747.0 jit_solution(11988488989839320579)
XLA Ops:
  7.2 1.5 copy.47
  8.7 1.0 reshape_squeeze.14
  9.8 1.7 reshape_squeeze.15
  11.5 2.8 copy.70
  14.5 221.6 %all-gather.2.cloned.1.call-done = bf16[2,192,1536]{1,0,2:T(2,128)(2,1)} async-done(((bf16[2,192,48]{1,0,2:T(2,128)(2,1)}), bf16[2,192,1536]{1,0,2:T(2,128)(2,1)}) %all-gather.2.cloned.1.call-update) | async-done | bytes 1179664 | tf_op jit(solution)/shard_map/all_gather | solution.py:50
  236.1 4.9 copy.48
  241.0 3.6 convolution_convert_fusion.1
  244.6 2.6 reshape.88
  247.2 3.4 slice_reduce_fusion
  250.6 0.3 fusion.5
  250.9 0.3 fusion.44
  251.2 0.3 convolution_bitcast_fusion
  251.5 1.2 fusion.13
  252.7 1.3 copy.59
  254.0 0.9 stack_reshape.9
  254.9 1.2 fusion.14
  256.1 2.2 copy.57
  258.3 1.9 stack_reshape.8
  260.2 1.2 pad_maximum_fusion
  261.4 0.8 copy.60
  262.4 0.9 copy-done.4
  263.3 3.2 fusion.45
  266.7 3.3 fusion.2
  270.1 2.9 copy.64
  273.0 2.0 convolution_convert_fusion.3
  275.0 0.9 copy.61
  275.9 243.9 %reduce-scatter.5.cloned.1.call-done = f32[384,48]{0,1:T(8,128)} async-done(((f32[384,1536]{0,1:T(8,128)}), f32[384,48]{0,1:T(8,128)}) %reduce-scatter.5.cloned.1.call-update) | async-done | bytes 73744 | tf_op jit(solution)/shard_map/reduce_scatter | solution.py:70
  519.8 1.0 reshape.91
  520.8 0.6 copy.63
  521.5 217.1 %reduce-scatter.7.cloned.1.call-done = bf16[48,1024]{1,0:T(8,128)(2,1)} async-done(((bf16[1536,1024]{1,0:T(8,128)(2,1)}), bf16[48,1024]{1,0:T(8,128)(2,1)}) %reduce-scatter.7.cloned.1.call-update) | async-done | bytes 98320
  738.6 1.1 copy.65
  739.7 0.8 copy.62
  (26 shorter events, 0.7 us)
Async XLA Ops:
  7.2 228.9 %all-gather.2.cloned.1.call-start = ((), (), s32[]{:S(2)}) async-start(), calls=%async_computation.2 | async-start | bytes 1622016 | tf_op jit(solution)/shard_map/all_gather | solution.py:50
  8.7 511.1 %reduce-scatter.5.cloned.1.call-start = ((), (), s32[]{:S(2)}) async-start(), calls=%async_computation.3 | async-start | bytes 2433024 | tf_op jit(solution)/shard_map/reduce_scatter | solution.py:70
  11.5 2.8 copy-start.7
  11.5 2.9 copy-start.6
  14.3 226.7 %copy-start = (bf16[192,8,2,512]{3,1,2,0:T(8,128)(2,1)}, bf16[192,8,2,512]{3,1,2,0:T(8,128)(2,1)S(1)}, u32[]{:S(2)}) copy-start(bf16[192,8,2,512]{3,1,2,0:T(8,128)(2,1)S(1)} %copy.70) | copy-start | bytes 9437188
  14.5 237.0 %copy-start.5 = (pred[2,128,192]{1,2,0:T(8,128)(4,1)}, pred[2,128,192]{1,2,0:T(8,128)(4,1)S(1)}, u32[]{:S(2)}) copy-start(pred[2,128,192]{1,2,0:T(8,128)(4,1)S(1)} %compare_and_fusion) | copy-start | bytes 147460
  244.6 6.7 copy-start.3
  250.9 1.9 copy-start.2
  256.1 7.2 copy-start.1
  262.4 0.9 copy-start.4
  266.5 472.1 %reduce-scatter.7.cloned.1.call-start = ((), (), s32[]{:S(2)}) async-start(), calls=%async_computation.4 | async-start | bytes 3244032
Sparse Core Ops, SparseCore 0:
  11.2 224.8 all-gather.1
  266.6 253.1 reduce-scatter.4
  525.5 213.0 reduce-scatter.6
where the time goes:
time: 748 us; the launch traced here: 747 us
  waiting for transfers between devices  683 us (91%)
  local copies, waits for them, and re-layouts  33.3 us (4%)
  matrix products  15.1 us (2%)
  between operations  13.9 us (2%)
    reduce_scatter x1, waiting for transfers between devices, body(): lax.psum_scatter(lat_term, ('section', 'mp'), scatter_dimension=1, tiled=...  244 us
    all_gather x1, waiting for transfers between devices, body(): gathered = lax.all_gather(latents, ('section', 'mp'), axis=2, tiled=True)  222 us
    unnamed x4, waiting for transfers between devices  217 us
  transfers between devices with their start and end apart: 3, of which 3 were waited for; matrix products, arithmetic and copies ran while one was open for 2% of the time, Pallas kernels for 0%

commit v1 on v0

--- a/solution.py
+++ b/solution.py
@@ -1,10 +1,15 @@
 import jax
 import jax.numpy as jnp
 from jax import lax
-from jax.sharding import PartitionSpec as P
+from jax.sharding import Mesh, PartitionSpec as P
 
 HEAD = 128
 LATENTS = 64
+SIZES = (("zh", 4), ("y", 4), ("core", 2), ("section", 4), ("mp", 8))
+AXES = tuple(name for name, _ in SIZES)
+SIZE = dict(SIZES)
+DP = ("zh", "y", "core")
+f32, bf16 = jnp.float32, jnp.bfloat16
 
 
 def attend(query_rows, kv_rounded, token_rows, count_rows, grad_rows):
@@ -46,51 +51,125 @@
     return (output, dkv.astype(jnp.bfloat16))
 
 
+def shift(x, axis, step):
+    n = SIZE[axis]
+    return lax.ppermute(x, axis, [(i, (i + step) % n) for i in range(n)])
+
+
+def swap(x, axis, bit):
+    return lax.ppermute(x, axis, [(i, i ^ bit) for i in range(SIZE[axis])])
+
+
+def pick(x, index, axis=0):
+    return lax.dynamic_index_in_dim(x, index, axis, keepdims=False)
+
+
+def gather_latents(own):
+    mp, section = lax.axis_index("mp"), lax.axis_index("section")
+    block = own
+    for bit in (4, 2, 1):
+        other = swap(block, "mp", bit)
+        upper = (mp // bit) % 2 == 1
+        block = jnp.where(
+            upper, jnp.concatenate([other, block]), jnp.concatenate([block, other])
+        )
+    parts = [block] + [shift(block, "section", k) for k in (1, 2, 3)]
+    descending = jnp.stack(parts[::-1] + parts[::-1])
+    ordered = lax.dynamic_slice_in_dim(descending, (3 - section) % 4, 4, 0)
+    depth, rows = own.shape
+    ordered = ordered.reshape(4, 2, 2, 2, depth, rows).transpose(0, 3, 2, 1, 4, 5)
+    return ordered.reshape(32 * depth, rows)
+
+
+def scatter_direct(x, axis):
+    n, me = SIZE[axis], lax.axis_index(axis)
+    sent = [shift(pick(x, (me + k) % n).astype(bf16), axis, k) for k in range(1, n)]
+    total = pick(x, me).astype(f32)
+    for part in sent:
+        total = total + part.astype(f32)
+    return total
+
+
+def scatter_halving(x):
+    mp = lax.axis_index("mp")
+    x = x.reshape((2, 2, 2) + x.shape[1:])
+    for bit in (1, 2, 4):
+        mine = (mp // bit) % 2
+        last = {1: 2, 2: 1, 4: 0}[bit]
+        x = pick(x, mine, last) + swap(
+            pick(x, 1 - mine, last).astype(bf16), "mp", bit
+        ).astype(f32)
+    return x
+
+
+def scatter_zh(x):
+    me = lax.axis_index("zh")
+    half = x.shape[-1] // 2
+    far = pick(x, (me + 2) % 4)
+    after, before = pick(x, (me + 1) % 4), pick(x, (me + 3) % 4)
+    from_after = shift(far[:, :half].astype(bf16), "zh", 3)
+    from_before = shift(far[:, half:].astype(bf16), "zh", 1)
+    to_before = jnp.concatenate(
+        [before[:, :half] + from_after.astype(f32), before[:, half:]], axis=1
+    ).astype(bf16)
+    to_after = jnp.concatenate(
+        [after[:, :half], after[:, half:] + from_before.astype(f32)], axis=1
+    ).astype(bf16)
+    return pick(x, me) + shift(to_before, "zh", 3).astype(f32) + shift(to_after, "zh", 1).astype(f32)
+
+
 def body(queries, latents, kv_weight, token_image, image_counts, out_grad):
-    gathered = lax.all_gather(latents, ("section", "mp"), axis=2, tiled=True)
-    samples, key_count, width = gathered.shape
+    samples, key_count, depth = latents.shape
+    rows = samples * key_count
     local_features = kv_weight.shape[-1]
-    weights = kv_weight.reshape(width, 2 * local_features)
-    flat_lat = gathered.reshape(samples * key_count, width)
-    kv_rounded = jnp.dot(flat_lat, weights, preferred_element_type=jnp.float32).astype(jnp.bfloat16)
+    weights = kv_weight.reshape(-1, 2 * local_features)
+    width = weights.shape[0]
+    lat_t = gather_latents(latents.reshape(rows, depth).T)
+    kv_rounded = lax.dot_general(
+        lat_t, weights, (((0,), (0,)), ((), ())), preferred_element_type=f32
+    ).astype(bf16)
     kv_rounded = kv_rounded.reshape(samples, key_count, 2, local_features)
     attended, dkv = attend(queries[0], kv_rounded, token_image, image_counts, out_grad[0])
-    dflat = dkv.reshape(samples * key_count, 2 * local_features)
-    kv_grad = lax.psum_scatter(
-        lax.dot_general(
-            flat_lat, dflat, (((0,), (0,)), ((), ())), preferred_element_type=jnp.float32
-        ).astype(jnp.bfloat16),
-        "dp",
-        scatter_dimension=0,
-        tiled=True,
-    ).astype(jnp.float32)
+    dflat = dkv.reshape(rows, 2 * local_features)
+
+    core = lax.axis_index("core")
+    grad_term = jnp.dot(lat_t, dflat, preferred_element_type=f32).astype(bf16)
+    grad_term = grad_term.reshape(4, 4, 2, depth, 2 * local_features)
+    grad_sum = pick(grad_term, core, 2).astype(f32) + swap(
+        pick(grad_term, 1 - core, 2), "core", 1
+    ).astype(f32)
+    grad_sum = scatter_direct(grad_sum.transpose(1, 0, 2, 3).astype(bf16), "y")
+    kv_grad = scatter_zh(grad_sum)
+
     lat_term = lax.dot_general(
-        dflat, weights, (((1,), (1,)), ((), ())), preferred_element_type=jnp.float32
-    )
-    latent_grad = lax.psum_scatter(lat_term, ("section", "mp"), scatter_dimension=1, tiled=True)
+        weights, dflat, (((1,), (1,)), ((), ())), preferred_element_type=f32
+    ).astype(bf16)
+    lat_sum = scatter_direct(lat_term.reshape(4, 8, depth, rows), "section")
+    latent_grad = scatter_halving(lat_sum)
     return (
         attended[None],
-        kv_grad.reshape(1, -1, 2, local_features),
-        latent_grad.reshape(samples, key_count, -1),
+        kv_grad.reshape(1, depth, 2, local_features),
+        latent_grad.T.reshape(samples, key_count, depth),
     )
 
 
 def solution(mesh):
+    fine = Mesh(mesh.devices.reshape([n for _, n in SIZES]), AXES)
     return jax.shard_map(
         body,
-        mesh=mesh,
+        mesh=fine,
         in_specs=(
-            P("section", "dp", None, "mp"),
-            P("dp", None, ("section", "mp")),
+            P("section", DP, None, "mp"),
+            P(DP, None, ("section", "mp")),
             P("section", None, None, "mp"),
-            P("dp", None),
-            P("dp"),
-            P("section", "dp", None, "mp"),
+            P(DP, None),
+            P(DP),
+            P("section", DP, None, "mp"),
         ),
         out_specs=(
-            P("section", "dp", None, "mp"),
-            P("section", "dp", None, "mp"),
-            P("dp", None, ("section", "mp")),
+            P("section", DP, None, "mp"),
+            P("section", DP, None, "mp"),
+            P(DP, None, ("section", "mp")),
         ),
         check_vma=False,
     )

time: 748 us -> 215 us (0.29)
  the two profiles are of different devices: /device:TPU:2 before, /device:TPU:16 now
where the time goes in v1:
time: 215 us; the launch traced here: 214 us
  starting transfers between devices  96.8 us (45%)
  waiting for transfers between devices  62.2 us (29%)
  local copies, waits for them, and re-layouts  32.2 us (15%)
  matrix products  11.7 us (5%)
  other arithmetic  9.36 us (4%)
    ppermute x13, starting transfers between devices, shift(): return lax.ppermute(x, axis, [(i, (i + step) % n) for i in range(n)])  68 us
    ppermute x13, waiting for transfers between devices, shift(): return lax.ppermute(x, axis, [(i, (i + step) % n) for i in range(n)])  47 us
    ppermute x7, starting transfers between devices, swap(): return lax.ppermute(x, axis, [(i, i ^ bit) for i in range(SIZE[axis])])  28.7 us
    ppermute x7, waiting for transfers between devices, swap(): return lax.ppermute(x, axis, [(i, i ^ bit) for i in range(SIZE[axis])])  15.2 us
    unnamed x27, local copies, waits for them, and re-layouts  13.2 us
  transfers between devices with their start and end apart: 20, of which 12 were waited for; matrix products, arithmetic and copies ran while one was open for 12% of the time, Pallas kernels for 0%

profile of v1, /device:TPU:16, one launch (start us, length us, event | category | flops | bytes accessed | tf_op | source)
XLA Modules:
  0.0 213.7 jit_solution(1506788051529564462)
XLA Ops:
  1.6 9.1 %collective-permute-start = (bf16[48,384]{1,0:T(8,128)(2,1)S(1)}, bf16[48,384]{1,0:T(8,128)(2,1)S(1)}, u32[]{:S(2)}, u32[]{:S(2)}) collective-permute-start(bf16[48,384]{1,0:T(8,128)(2,1)S(1)} %bitcast.144), channel_id=1, source_target_pairs={{0,4},{1,5},{2,6},{3,7},{4,0},{5,1},{6,2},{7,3},{8,12},{9,13},{10,... | collective-permute-start | bytes 110600 | tf_op jit(solution)/shard_map/ppermute | solution.py:60
  12.6 5.2 %collective-permute-start.1 = (bf16[96,384]{1,0:T(8,128)(2,1)S(1)}, bf16[96,384]{1,0:T(8,128)(2,1)S(1)}, u32[]{:S(2)}, u32[]{:S(2)}) collective-permute-start(bf16[96,384]{1,0:T(8,128)(2,1)S(1)} %maximum_select_fusion.3), channel_id=1, source_target_pairs={{0,2},{1,3},{2,0},{3,1},{4,6},{5,7},{6,4},{7,5},{8,10},{9,11},{10,... | collective-permute-start | bytes 221192 | tf_op jit(solution)/shard_map/ppermute | solution.py:60
  17.8 3.9 %collective-permute-done.1 = bf16[96,384]{1,0:T(8,128)(2,1)S(1)} collective-permute-done((bf16[96,384]{1,0:T(8,128)(2,1)S(1)}, bf16[96,384]{1,0:T(8,128)(2,1)S(1)}, u32[]{:S(2)}, u32[]{:S(2)}) %collective-permute-start.1) | collective-permute-done | bytes 73760 | tf_op jit(solution)/shard_map/ppermute | solution.py:60
  21.7 2.2 %collective-permute-start.2 = (bf16[192,384]{1,0:T(8,128)(2,1)S(1)}, bf16[192,384]{1,0:T(8,128)(2,1)S(1)}, u32[]{:S(2)}, u32[]{:S(2)}) collective-permute-start(bf16[192,384]{1,0:T(8,128)(2,1)S(1)} %maximum_select_fusion.2), channel_id=1, source_target_pairs={{0,1},{1,0},{2,3},{3,2},{4,5},{5,4},{6,7},{7,6},{8,9},{9,8},{10,11... | collective-permute-start | bytes 442376 | tf_op jit(solution)/shard_map/ppermute | solution.py:60
  24.0 4.8 %collective-permute-done.2 = bf16[192,384]{1,0:T(8,128)(2,1)S(1)} collective-permute-done((bf16[192,384]{1,0:T(8,128)(2,1)S(1)}, bf16[192,384]{1,0:T(8,128)(2,1)S(1)}, u32[]{:S(2)}, u32[]{:S(2)}) %collective-permute-start.2) | collective-permute-done | bytes 147488 | tf_op jit(solution)/shard_map/ppermute | solution.py:60
  29.6 4.7 %collective-permute-start.3 = (bf16[384,384]{1,0:T(8,128)(2,1)}, bf16[384,384]{1,0:T(8,128)(2,1)}, u32[]{:S(2)}, u32[]{:S(2)}) collective-permute-start(bf16[384,384]{1,0:T(8,128)(2,1)} %maximum_select_fusion), channel_id=1, source_target_pairs={{0,24},{8,0},{16,8},{24,16},{1,25},{9,1},{17,9},{25,17},{2,26},{10... | collective-permute-start | bytes 884744 | tf_op jit(solution)/shard_map/ppermute | solution.py:56
  35.0 2.7 %collective-permute-start.4 = (bf16[384,384]{1,0:T(8,128)(2,1)}, bf16[384,384]{1,0:T(8,128)(2,1)}, u32[]{:S(2)}, u32[]{:S(2)}) collective-permute-start(bf16[384,384]{1,0:T(8,128)(2,1)} %maximum_select_fusion), channel_id=1, source_target_pairs={{0,16},{8,24},{16,0},{24,8},{1,17},{9,25},{17,1},{25,9},{2,18},{10... | collective-permute-start | bytes 884744 | tf_op jit(solution)/shard_map/ppermute | solution.py:56
  38.6 2.7 %copy.53 = bf16[192,8,2,512]{3,1,2,0:T(8,128)(2,1)S(1)} copy(bf16[192,8,2,512]{3,2,1,0:T(2,128)(2,1)} %bitcast.127) | data formatting | bytes 6291456
  44.9 2.8 %collective-permute-start.5 = (bf16[384,384]{1,0:T(8,128)(2,1)}, bf16[384,384]{1,0:T(8,128)(2,1)S(1)}, u32[]{:S(2)}, u32[]{:S(2)}) collective-permute-start(bf16[384,384]{1,0:T(8,128)(2,1)} %maximum_select_fusion), channel_id=1, source_target_pairs={{0,8},{8,16},{16,24},{24,0},{1,9},{9,17},{17,25},{25,1},{2,10},{10... | collective-permute-start | bytes 884744 | tf_op jit(solution)/shard_map/ppermute | solution.py:56
  49.8 5.2 %collective-permute-done.5 = bf16[384,384]{1,0:T(8,128)(2,1)S(1)} collective-permute-done((bf16[384,384]{1,0:T(8,128)(2,1)}, bf16[384,384]{1,0:T(8,128)(2,1)S(1)}, u32[]{:S(2)}, u32[]{:S(2)}) %collective-permute-start.5) | collective-permute-done | bytes 294944 | tf_op jit(solution)/shard_map/ppermute | solution.py:56
  58.6 2.3 %convolution_convert_fusion.2 = bf16[384,1024]{1,0:T(8,128)(2,1)} fusion(bf16[1536,384]{1,0:T(8,128)(2,1)S(1)} %bitcast.139, bf16[1536,1024]{1,0:T(8,128)(2,1)S(1)} %bitcast.130), kind=kOutput, calls=%fused_computation.8 | convolution fusion | flops 1208352768 | bytes 5111808 | tf_op jit(solution)/shard_map/dot_general | solution.py:128
  61.0 2.6 %reshape.223 = bf16[2,192,2,512]{3,2,1,0:T(2,128)(2,1)S(1)} reshape(bf16[384,1024]{1,0:T(8,128)(2,1)} %convolution_convert_fusion.2) | data formatting | bytes 1572864 | tf_op jit(solution)/shard_map/reshape | solution.py:131
  63.6 3.4 %slice_reduce_fusion = (bf16[2,192,512]{2,1,0:T(8,128)(2,1)S(1)}, bf16[2,192,512]{2,1,0:T(8,128)(2,1)S(1)}) fusion(bf16[2,192,2,512]{3,2,1,0:T(2,128)(2,1)S(1)} %reshape.223), kind=kLoop, calls=%fused_computation.27 | loop fusion | bytes 1572864 | tf_op jit(solution)/shard_map/slice | solution.py:20
  81.5 2.5 %fusion.3 = bf16[1536,384]{0,1:T(8,128)(2,1)} fusion(bf16[384,1024]{1,0:T(8,128)(2,1)S(1)} %bitcast.142, bf16[1536,1024]{1,0:T(8,128)(2,1)S(1)} %bitcast.131), kind=kOutput, calls=%fused_computation.6 | convolution fusion | flops 1208549376 | bytes 5111808 | tf_op jit(solution)/shard_map/dot_general | solution.py:144
  87.7 3.4 %collective-permute-start.15 = (bf16[8,48,384]{2,1,0:T(8,128)(2,1)S(1)}, bf16[8,48,384]{2,1,0:T(8,128)(2,1)}, u32[]{:S(2)}, u32[]{:S(2)}) collective-permute-start(bf16[8,48,384]{2,1,0:T(8,128)(2,1)S(1)} %get-tuple-element.19), channel_id=1, source_target_pairs={{0,16},{8,24},{16,0},{24,8},{1,17},{9,25},{17,1},{25,9},{2,18},{10... | collective-permute-start | bytes 884744 | tf_op jit(solution)/shard_map/ppermute | solution.py:56
  91.1 4.5 %collective-permute-start.16 = (bf16[8,48,384]{2,1,0:T(8,128)(2,1)S(1)}, bf16[8,48,384]{2,1,0:T(8,128)(2,1)}, u32[]{:S(2)}, u32[]{:S(2)}) collective-permute-start(bf16[8,48,384]{2,1,0:T(8,128)(2,1)S(1)} %get-tuple-element.18), channel_id=1, source_target_pairs={{0,24},{8,0},{16,8},{24,16},{1,25},{9,1},{17,9},{25,17},{2,26},{10... | collective-permute-start | bytes 884744 | tf_op jit(solution)/shard_map/ppermute | solution.py:56
  95.7 8.9 %collective-permute-done.14 = bf16[8,48,384]{2,1,0:T(8,128)(2,1)S(1)} collective-permute-done((bf16[8,48,384]{2,1,0:T(8,128)(2,1)S(1)}, bf16[8,48,384]{2,1,0:T(8,128)(2,1)S(1)}, u32[]{:S(2)}, u32[]{:S(2)}) %collective-permute-start.14) | collective-permute-done | bytes 294944 | tf_op jit(solution)/shard_map/ppermute | solution.py:56
  104.6 2.6 %collective-permute-done.16 = bf16[8,48,384]{2,1,0:T(8,128)(2,1)} collective-permute-done((bf16[8,48,384]{2,1,0:T(8,128)(2,1)S(1)}, bf16[8,48,384]{2,1,0:T(8,128)(2,1)}, u32[]{:S(2)}, u32[]{:S(2)}) %collective-permute-start.16) | collective-permute-done | bytes 294944 | tf_op jit(solution)/shard_map/ppermute | solution.py:56
  108.5 2.2 %collective-permute-start.17 = (bf16[2,2,48,384]{3,2,1,0:T(8,128)(2,1)S(1)}, bf16[2,2,48,384]{3,2,1,0:T(8,128)(2,1)S(1)}, u32[]{:S(2)}, u32[]{:S(2)}) collective-permute-start(bf16[2,2,48,384]{3,2,1,0:T(8,128)(2,1)S(1)} %fusion.39), channel_id=1, source_target_pairs={{0,1},{1,0},{2,3},{3,2},{4,5},{5,4},{6,7},{7,6},{8,9},{9,8},{10,11... | collective-permute-start | bytes 442376 | tf_op jit(solution)/shard_map/ppermute | solution.py:60
  110.8 4.7 %collective-permute-done.17 = bf16[2,2,48,384]{3,2,1,0:T(8,128)(2,1)S(1)} collective-permute-done((bf16[2,2,48,384]{3,2,1,0:T(8,128)(2,1)S(1)}, bf16[2,2,48,384]{3,2,1,0:T(8,128)(2,1)S(1)}, u32[]{:S(2)}, u32[]{:S(2)}) %collective-permute-start.17) | collective-permute-done | bytes 147488 | tf_op jit(solution)/shard_map/ppermute | solution.py:60
  115.6 3.8 %collective-permute-start.18 = (bf16[2,48,384]{2,1,0:T(8,128)(2,1)S(1)}, bf16[2,48,384]{2,1,0:T(8,128)(2,1)}, u32[]{:S(2)}, u32[]{:S(2)}) collective-permute-start(bf16[2,48,384]{2,1,0:T(8,128)(2,1)S(1)} %fusion.43), channel_id=1, source_target_pairs={{0,2},{1,3},{2,0},{3,1},{4,6},{5,7},{6,4},{7,5},{8,10},{9,11},{10,... | collective-permute-start | bytes 221192 | tf_op jit(solution)/shard_map/ppermute | solution.py:60
  119.4 2.7 %fusion.2 = bf16[4,4,48,1024]{3,2,1,0:T(8,128)(2,1)S(1)} fusion(bf16[4,4,48,1024]{3,2,1,0:T(8,128)(2,1)} %collective-permute-done.6, bf16[4,4,2,48,1024]{4,3,2,1,0:T(8,128)(2,1)} %bitcast.129, s32[]{:T(128)S(6)} %select_n.230), kind=kLoop, calls=%fused_computation.4 | loop fusion | flops 3145728 | bytes 4718596 | tf_op jit(solution)/shard_map/convert_element_type | solution.py:141
  123.1 3.2 %collective-permute-start.7 = (bf16[4,48,1024]{2,1,0:T(8,128)(2,1)}, bf16[4,48,1024]{2,1,0:T(8,128)(2,1)}, u32[]{:S(2)}, u32[]{:S(2)}) collective-permute-start(bf16[4,48,1024]{2,1,0:T(8,128)(2,1)} %get-tuple-element.14), channel_id=1, source_target_pairs={{0,64},{64,128},{128,192},{192,0},{1,65},{65,129},{129,193},{193,1... | collective-permute-start | bytes 1179656 | tf_op jit(solution)/shard_map/ppermute | solution.py:56
  126.3 6.5 %collective-permute-start.8 = (bf16[4,48,1024]{2,1,0:T(8,128)(2,1)}, bf16[4,48,1024]{2,1,0:T(8,128)(2,1)}, u32[]{:S(2)}, u32[]{:S(2)}) collective-permute-start(bf16[4,48,1024]{2,1,0:T(8,128)(2,1)} %get-tuple-element.16), channel_id=1, source_target_pairs={{0,128},{64,192},{128,0},{192,64},{1,129},{65,193},{129,1},{193,65... | collective-permute-start | bytes 1179656 | tf_op jit(solution)/shard_map/ppermute | solution.py:56
  132.8 4.5 %collective-permute-start.9 = (bf16[4,48,1024]{2,1,0:T(8,128)(2,1)S(1)}, bf16[4,48,1024]{2,1,0:T(8,128)(2,1)}, u32[]{:S(2)}, u32[]{:S(2)}) collective-permute-start(bf16[4,48,1024]{2,1,0:T(8,128)(2,1)S(1)} %get-tuple-element.15), channel_id=1, source_target_pairs={{0,192},{64,0},{128,64},{192,128},{1,193},{65,1},{129,65},{193,129... | collective-permute-start | bytes 1179656 | tf_op jit(solution)/shard_map/ppermute | solution.py:56
  142.2 4.1 %collective-permute-start.19 = (bf16[48,384]{1,0:T(8,128)(2,1)S(1)}, bf16[48,384]{1,0:T(8,128)(2,1)S(1)}, u32[]{:S(2)}, u32[]{:S(2)}) collective-permute-start(bf16[48,384]{1,0:T(8,128)(2,1)S(1)} %fusion.47), channel_id=1, source_target_pairs={{0,4},{1,5},{2,6},{3,7},{4,0},{5,1},{6,2},{7,3},{8,12},{9,13},{10,... | collective-permute-start | bytes 110600 | tf_op jit(solution)/shard_map/ppermute | solution.py:60
  147.2 2.8 %collective-permute-done.9 = bf16[4,48,1024]{2,1,0:T(8,128)(2,1)} collective-permute-done((bf16[4,48,1024]{2,1,0:T(8,128)(2,1)S(1)}, bf16[4,48,1024]{2,1,0:T(8,128)(2,1)}, u32[]{:S(2)}, u32[]{:S(2)}) %collective-permute-start.9) | collective-permute-done | bytes 393248 | tf_op jit(solution)/shard_map/ppermute | solution.py:56
  151.5 16.9 %collective-permute-start.10 = (bf16[48,512]{1,0:T(8,128)(2,1)S(1)}, bf16[48,512]{1,0:T(8,128)(2,1)S(1)}, u32[]{:S(2)}, u32[]{:S(2)}) collective-permute-start(bf16[48,512]{1,0:T(8,128)(2,1)S(1)} %get-tuple-element.22), channel_id=1, source_target_pairs={{0,768},{256,0},{512,256},{768,512},{1,769},{257,1},{513,257},{769... | collective-permute-start | bytes 147464 | tf_op jit(solution)/shard_map/ppermute | solution.py:56
  170.4 6.4 %collective-permute-done.10 = bf16[48,512]{1,0:T(8,128)(2,1)S(1)} collective-permute-done((bf16[48,512]{1,0:T(8,128)(2,1)S(1)}, bf16[48,512]{1,0:T(8,128)(2,1)S(1)}, u32[]{:S(2)}, u32[]{:S(2)}) %collective-permute-start.10) | collective-permute-done | bytes 49184 | tf_op jit(solution)/shard_map/ppermute | solution.py:56
  176.9 13.1 %collective-permute-start.11 = (bf16[48,1024]{1,0:T(8,128)(2,1)S(1)}, bf16[48,1024]{1,0:T(8,128)(2,1)S(1)}, u32[]{:S(2)}, u32[]{:S(2)}) collective-permute-start(bf16[48,1024]{1,0:T(8,128)(2,1)S(1)} %pad_maximum_fusion.1), channel_id=1, source_target_pairs={{0,768},{256,0},{512,256},{768,512},{1,769},{257,1},{513,257},{769... | collective-permute-start | bytes 294920 | tf_op jit(solution)/shard_map/ppermute | solution.py:56
  192.7 7.2 %collective-permute-done.11 = bf16[48,1024]{1,0:T(8,128)(2,1)S(1)} collective-permute-done((bf16[48,1024]{1,0:T(8,128)(2,1)S(1)}, bf16[48,1024]{1,0:T(8,128)(2,1)S(1)}, u32[]{:S(2)}, u32[]{:S(2)}) %collective-permute-start.11) | collective-permute-done | bytes 98336 | tf_op jit(solution)/shard_map/ppermute | solution.py:56
  200.0 12.9 %collective-permute-done.13 = bf16[48,1024]{1,0:T(8,128)(2,1)S(1)} collective-permute-done((bf16[48,1024]{1,0:T(8,128)(2,1)S(1)}, bf16[48,1024]{1,0:T(8,128)(2,1)S(1)}, u32[]{:S(2)}, u32[]{:S(2)}) %collective-permute-start.13) | collective-permute-done | bytes 98336 | tf_op jit(solution)/shard_map/ppermute | solution.py:56
  (91 shorter events, 47.7 us)
Async XLA Ops:
  1.6 11.0 %collective-permute-start = (bf16[48,384]{1,0:T(8,128)(2,1)S(1)}, bf16[48,384]{1,0:T(8,128)(2,1)S(1)}, u32[]{:S(2)}, u32[]{:S(2)}) collective-permute-start(bf16[48,384]{1,0:T(8,128)(2,1)S(1)} %bitcast.144), channel_id=1, source_target_pairs={{0,4},{1,5},{2,6},{3,7},{4,0},{5,1},{6,2},{7,3},{8,12},{9,13},{10,... | collective-permute-start | bytes 110600 | tf_op jit(solution)/shard_map/ppermute | solution.py:60
  12.6 9.1 %collective-permute-start.1 = (bf16[96,384]{1,0:T(8,128)(2,1)S(1)}, bf16[96,384]{1,0:T(8,128)(2,1)S(1)}, u32[]{:S(2)}, u32[]{:S(2)}) collective-permute-start(bf16[96,384]{1,0:T(8,128)(2,1)S(1)} %maximum_select_fusion.3), channel_id=1, source_target_pairs={{0,2},{1,3},{2,0},{3,1},{4,6},{5,7},{6,4},{7,5},{8,10},{9,11},{10,... | collective-permute-start | bytes 221192 | tf_op jit(solution)/shard_map/ppermute | solution.py:60
  21.7 7.0 %collective-permute-start.2 = (bf16[192,384]{1,0:T(8,128)(2,1)S(1)}, bf16[192,384]{1,0:T(8,128)(2,1)S(1)}, u32[]{:S(2)}, u32[]{:S(2)}) collective-permute-start(bf16[192,384]{1,0:T(8,128)(2,1)S(1)} %maximum_select_fusion.2), channel_id=1, source_target_pairs={{0,1},{1,0},{2,3},{3,2},{4,5},{5,4},{6,7},{7,6},{8,9},{9,8},{10,11... | collective-permute-start | bytes 442376 | tf_op jit(solution)/shard_map/ppermute | solution.py:60
  29.6 18.2 %collective-permute-start.3 = (bf16[384,384]{1,0:T(8,128)(2,1)}, bf16[384,384]{1,0:T(8,128)(2,1)}, u32[]{:S(2)}, u32[]{:S(2)}) collective-permute-start(bf16[384,384]{1,0:T(8,128)(2,1)} %maximum_select_fusion), channel_id=1, source_target_pairs={{0,24},{8,0},{16,8},{24,16},{1,25},{9,1},{17,9},{25,17},{2,26},{10... | collective-permute-start | bytes 884744 | tf_op jit(solution)/shard_map/ppermute | solution.py:56
  35.0 13.8 %collective-permute-start.4 = (bf16[384,384]{1,0:T(8,128)(2,1)}, bf16[384,384]{1,0:T(8,128)(2,1)}, u32[]{:S(2)}, u32[]{:S(2)}) collective-permute-start(bf16[384,384]{1,0:T(8,128)(2,1)} %maximum_select_fusion), channel_id=1, source_target_pairs={{0,16},{8,24},{16,0},{24,8},{1,17},{9,25},{17,1},{25,9},{2,18},{10... | collective-permute-start | bytes 884744 | tf_op jit(solution)/shard_map/ppermute | solution.py:56
  38.5 29.4 %copy-start.7 = (pred[2,128,192]{1,2,0:T(8,128)(4,1)}, pred[2,128,192]{1,2,0:T(8,128)(4,1)S(1)}, u32[]{:S(2)}) copy-start(pred[2,128,192]{1,2,0:T(8,128)(4,1)S(1)} %compare_and_fusion) | copy-start | bytes 147460
  41.3 16.3 %copy-start.1 = (bf16[192,8,2,512]{3,1,2,0:T(8,128)(2,1)}, bf16[192,8,2,512]{3,1,2,0:T(8,128)(2,1)S(1)}, u32[]{:S(2)}) copy-start(bf16[192,8,2,512]{3,1,2,0:T(8,128)(2,1)S(1)} %copy.53) | copy-start | bytes 9437188
  44.9 10.0 %collective-permute-start.5 = (bf16[384,384]{1,0:T(8,128)(2,1)}, bf16[384,384]{1,0:T(8,128)(2,1)S(1)}, u32[]{:S(2)}, u32[]{:S(2)}) collective-permute-start(bf16[384,384]{1,0:T(8,128)(2,1)} %maximum_select_fusion), channel_id=1, source_target_pairs={{0,8},{8,16},{16,24},{24,0},{1,9},{9,17},{17,25},{25,1},{2,10},{10... | collective-permute-start | bytes 884744 | tf_op jit(solution)/shard_map/ppermute | solution.py:56
  57.6 1.0 copy-start.3
  61.0 6.0 %copy-start.5 = (bf16[2,128,4,128]{3,2,1,0:T(4,128)(2,1)S(1)}, bf16[2,128,4,128]{3,2,1,0:T(4,128)(2,1)}, u32[]{:S(2)}) copy-start(bf16[2,128,4,128]{3,2,1,0:T(4,128)(2,1)} %reshape_squeeze.14) | copy-start | bytes 786436
  63.6 4.1 %copy-start.6 = (bf16[2,128,4,128]{3,2,1,0:T(4,128)(2,1)S(1)}, bf16[2,128,4,128]{3,2,1,0:T(4,128)(2,1)}, u32[]{:S(2)}) copy-start(bf16[2,128,4,128]{3,2,1,0:T(4,128)(2,1)} %reshape_squeeze.15) | copy-start | bytes 786436
  73.2 1.3 copy-start.4
  76.3 1.7 copy-start
  76.3 5.2 %copy-start.2 = (bf16[192,8,2,512]{3,1,2,0:T(8,128)(2,1)S(1)}, bf16[192,8,2,512]{3,1,2,0:T(8,128)(2,1)}, u32[]{:S(2)}) copy-start(bf16[192,8,2,512]{3,1,2,0:T(8,128)(2,1)} %copy-done.1) | copy-start | bytes 9437188
  79.4 40.0 %collective-permute-start.6 = (bf16[4,4,48,1024]{3,2,1,0:T(8,128)(2,1)}, bf16[4,4,48,1024]{3,2,1,0:T(8,128)(2,1)}, u32[]{:S(2)}, u32[]{:S(2)}) collective-permute-start(bf16[4,4,48,1024]{3,2,1,0:T(8,128)(2,1)} %dynamic-slice_bitcast_fusion), channel_id=1, source_target_pairs={{0,32},{32,0},{1,33},{33,1},{2,34},{34,2},{3,35},{35,3},{4,36},{36... | collective-permute-start | bytes 4718600 | tf_op jit(solution)/shard_map/ppermute | solution.py:60
  85.8 18.8 %collective-permute-start.14 = (bf16[8,48,384]{2,1,0:T(8,128)(2,1)S(1)}, bf16[8,48,384]{2,1,0:T(8,128)(2,1)S(1)}, u32[]{:S(2)}, u32[]{:S(2)}) collective-permute-start(bf16[8,48,384]{2,1,0:T(8,128)(2,1)S(1)} %get-tuple-element.17), channel_id=1, source_target_pairs={{0,8},{8,16},{16,24},{24,0},{1,9},{9,17},{17,25},{25,1},{2,10},{10... | collective-permute-start | bytes 884744 | tf_op jit(solution)/shard_map/ppermute | solution.py:56
  87.7 16.9 %collective-permute-start.15 = (bf16[8,48,384]{2,1,0:T(8,128)(2,1)S(1)}, bf16[8,48,384]{2,1,0:T(8,128)(2,1)}, u32[]{:S(2)}, u32[]{:S(2)}) collective-permute-start(bf16[8,48,384]{2,1,0:T(8,128)(2,1)S(1)} %get-tuple-element.19), channel_id=1, source_target_pairs={{0,16},{8,24},{16,0},{24,8},{1,17},{9,25},{17,1},{25,9},{2,18},{10... | collective-permute-start | bytes 884744 | tf_op jit(solution)/shard_map/ppermute | solution.py:56
  91.1 16.1 %collective-permute-start.16 = (bf16[8,48,384]{2,1,0:T(8,128)(2,1)S(1)}, bf16[8,48,384]{2,1,0:T(8,128)(2,1)}, u32[]{:S(2)}, u32[]{:S(2)}) collective-permute-start(bf16[8,48,384]{2,1,0:T(8,128)(2,1)S(1)} %get-tuple-element.18), channel_id=1, source_target_pairs={{0,24},{8,0},{16,8},{24,16},{1,25},{9,1},{17,9},{25,17},{2,26},{10... | collective-permute-start | bytes 884744 | tf_op jit(solution)/shard_map/ppermute | solution.py:56
  108.5 7.0 %collective-permute-start.17 = (bf16[2,2,48,384]{3,2,1,0:T(8,128)(2,1)S(1)}, bf16[2,2,48,384]{3,2,1,0:T(8,128)(2,1)S(1)}, u32[]{:S(2)}, u32[]{:S(2)}) collective-permute-start(bf16[2,2,48,384]{3,2,1,0:T(8,128)(2,1)S(1)} %fusion.39), channel_id=1, source_target_pairs={{0,1},{1,0},{2,3},{3,2},{4,5},{5,4},{6,7},{7,6},{8,9},{9,8},{10,11... | collective-permute-start | bytes 442376 | tf_op jit(solution)/shard_map/ppermute | solution.py:60
  115.6 25.7 %collective-permute-start.18 = (bf16[2,48,384]{2,1,0:T(8,128)(2,1)S(1)}, bf16[2,48,384]{2,1,0:T(8,128)(2,1)}, u32[]{:S(2)}, u32[]{:S(2)}) collective-permute-start(bf16[2,48,384]{2,1,0:T(8,128)(2,1)S(1)} %fusion.43), channel_id=1, source_target_pairs={{0,2},{1,3},{2,0},{3,1},{4,6},{5,7},{6,4},{7,5},{8,10},{9,11},{10,... | collective-permute-start | bytes 221192 | tf_op jit(solution)/shard_map/ppermute | solution.py:60
  123.1 23.2 %collective-permute-start.7 = (bf16[4,48,1024]{2,1,0:T(8,128)(2,1)}, bf16[4,48,1024]{2,1,0:T(8,128)(2,1)}, u32[]{:S(2)}, u32[]{:S(2)}) collective-permute-start(bf16[4,48,1024]{2,1,0:T(8,128)(2,1)} %get-tuple-element.14), channel_id=1, source_target_pairs={{0,64},{64,128},{128,192},{192,0},{1,65},{65,129},{129,193},{193,1... | collective-permute-start | bytes 1179656 | tf_op jit(solution)/shard_map/ppermute | solution.py:56
  126.3 20.9 %collective-permute-start.8 = (bf16[4,48,1024]{2,1,0:T(8,128)(2,1)}, bf16[4,48,1024]{2,1,0:T(8,128)(2,1)}, u32[]{:S(2)}, u32[]{:S(2)}) collective-permute-start(bf16[4,48,1024]{2,1,0:T(8,128)(2,1)} %get-tuple-element.16), channel_id=1, source_target_pairs={{0,128},{64,192},{128,0},{192,64},{1,129},{65,193},{129,1},{193,65... | collective-permute-start | bytes 1179656 | tf_op jit(solution)/shard_map/ppermute | solution.py:56
  132.8 17.2 %collective-permute-start.9 = (bf16[4,48,1024]{2,1,0:T(8,128)(2,1)S(1)}, bf16[4,48,1024]{2,1,0:T(8,128)(2,1)}, u32[]{:S(2)}, u32[]{:S(2)}) collective-permute-start(bf16[4,48,1024]{2,1,0:T(8,128)(2,1)S(1)} %get-tuple-element.15), channel_id=1, source_target_pairs={{0,192},{64,0},{128,64},{192,128},{1,193},{65,1},{129,65},{193,129... | collective-permute-start | bytes 1179656 | tf_op jit(solution)/shard_map/ppermute | solution.py:56
  142.2 49.7 %collective-permute-start.19 = (bf16[48,384]{1,0:T(8,128)(2,1)S(1)}, bf16[48,384]{1,0:T(8,128)(2,1)S(1)}, u32[]{:S(2)}, u32[]{:S(2)}) collective-permute-start(bf16[48,384]{1,0:T(8,128)(2,1)S(1)} %fusion.47), channel_id=1, source_target_pairs={{0,4},{1,5},{2,6},{3,7},{4,0},{5,1},{6,2},{7,3},{8,12},{9,13},{10,... | collective-permute-start | bytes 110600 | tf_op jit(solution)/shard_map/ppermute | solution.py:60
  151.5 25.3 %collective-permute-start.10 = (bf16[48,512]{1,0:T(8,128)(2,1)S(1)}, bf16[48,512]{1,0:T(8,128)(2,1)S(1)}, u32[]{:S(2)}, u32[]{:S(2)}) collective-permute-start(bf16[48,512]{1,0:T(8,128)(2,1)S(1)} %get-tuple-element.22), channel_id=1, source_target_pairs={{0,768},{256,0},{512,256},{768,512},{1,769},{257,1},{513,257},{769... | collective-permute-start | bytes 147464 | tf_op jit(solution)/shard_map/ppermute | solution.py:56
  168.5 21.5 %collective-permute-start.12 = (bf16[48,512]{1,0:T(8,128)(2,1)S(1)}, bf16[48,512]{1,0:T(8,128)(2,1)S(1)}, u32[]{:S(2)}, u32[]{:S(2)}) collective-permute-start(bf16[48,512]{1,0:T(8,128)(2,1)S(1)} %get-tuple-element.23), channel_id=1, source_target_pairs={{0,256},{256,512},{512,768},{768,0},{1,257},{257,513},{513,769},{7... | collective-permute-start | bytes 147464 | tf_op jit(solution)/shard_map/ppermute | solution.py:56
  176.9 23.1 %collective-permute-start.11 = (bf16[48,1024]{1,0:T(8,128)(2,1)S(1)}, bf16[48,1024]{1,0:T(8,128)(2,1)S(1)}, u32[]{:S(2)}, u32[]{:S(2)}) collective-permute-start(bf16[48,1024]{1,0:T(8,128)(2,1)S(1)} %pad_maximum_fusion.1), channel_id=1, source_target_pairs={{0,768},{256,0},{512,256},{768,512},{1,769},{257,1},{513,257},{769... | collective-permute-start | bytes 294920 | tf_op jit(solution)/shard_map/ppermute | solution.py:56
  190.0 22.9 %collective-permute-start.13 = (bf16[48,1024]{1,0:T(8,128)(2,1)S(1)}, bf16[48,1024]{1,0:T(8,128)(2,1)S(1)}, u32[]{:S(2)}, u32[]{:S(2)}) collective-permute-start(bf16[48,1024]{1,0:T(8,128)(2,1)S(1)} %pad_maximum_fusion.2), channel_id=1, source_target_pairs={{0,256},{256,512},{512,768},{768,0},{1,257},{257,513},{513,769},{7... | collective-permute-start | bytes 294920 | tf_op jit(solution)/shard_map/ppermute | solution.py:56

commit v2 on v1

--- a/solution.py
+++ b/solution.py
@@ -51,13 +51,27 @@
     return (output, dkv.astype(jnp.bfloat16))
 
 
-def shift(x, axis, step):
-    n = SIZE[axis]
-    return lax.ppermute(x, axis, [(i, (i + step) % n) for i in range(n)])
+def swap(x, axis, bit):
+    return lax.ppermute(x, axis, [(i, i ^ bit) for i in range(SIZE[axis])])
 
 
-def swap(x, axis, bit):
-    return lax.ppermute(x, axis, [(i, i ^ bit) for i in range(SIZE[axis])])
+PARITY = {"y": "core", "section": "core", "zh": "mp"}
+
+
+def pairing(axis, first):
+    odd = lax.axis_index(PARITY[axis]) % 2
+    return 1 + 2 * odd if first else 3 - 2 * odd
+
+
+def paired(x, axis, first):
+    axes = tuple(name for name in AXES if name in (axis, PARITY[axis]))
+    pairs = []
+    for at in range(SIZE[axes[0]] * SIZE[axes[1]]):
+        place = dict(zip(axes, divmod(at, SIZE[axes[1]])))
+        odd = place[PARITY[axis]] % 2
+        place[axis] ^= 1 + 2 * odd if first else 3 - 2 * odd
+        pairs.append((at, place[axes[0]] * SIZE[axes[1]] + place[axes[1]]))
+    return lax.ppermute(x, axes, pairs)
 
 
 def pick(x, index, axis=0):
@@ -73,49 +87,35 @@
         block = jnp.where(
             upper, jnp.concatenate([other, block]), jnp.concatenate([block, other])
         )
-    parts = [block] + [shift(block, "section", k) for k in (1, 2, 3)]
-    descending = jnp.stack(parts[::-1] + parts[::-1])
-    ordered = lax.dynamic_slice_in_dim(descending, (3 - section) % 4, 4, 0)
+    second = paired(block, "section", False)
+    pair = jnp.stack([block, second])
+    far = paired(pair, "section", True)
+    parts = jnp.concatenate([pair, far])
+    a = pairing("section", True)
     depth, rows = own.shape
-    ordered = ordered.reshape(4, 2, 2, 2, depth, rows).transpose(0, 3, 2, 1, 4, 5)
+    ordered = []
+    for s in range(4):
+        x = s ^ section
+        place = jnp.where(x == 0, 0, jnp.where(x == 2, 3, jnp.where(x == a, 2, 1)))
+        ordered.append(pick(parts, place))
+    ordered = jnp.stack(ordered).reshape(4, 2, 2, 2, depth, rows).transpose(0, 3, 2, 1, 4, 5)
     return ordered.reshape(32 * depth, rows)
 
 
-def scatter_direct(x, axis):
-    n, me = SIZE[axis], lax.axis_index(axis)
-    sent = [shift(pick(x, (me + k) % n).astype(bf16), axis, k) for k in range(1, n)]
-    total = pick(x, me).astype(f32)
-    for part in sent:
-        total = total + part.astype(f32)
-    return total
+def halve_first(x, axis):
+    me, a, b = lax.axis_index(axis), pairing(axis, True), pairing(axis, False)
+    send = jnp.stack([pick(x, me ^ a), pick(x, me ^ 2)]).astype(bf16)
+    got = paired(send, axis, True).astype(f32)
+    return pick(x, me).astype(f32) + got[0], pick(x, me ^ b).astype(f32) + got[1]
 
 
-def scatter_halving(x):
-    mp = lax.axis_index("mp")
-    x = x.reshape((2, 2, 2) + x.shape[1:])
-    for bit in (1, 2, 4):
-        mine = (mp // bit) % 2
-        last = {1: 2, 2: 1, 4: 0}[bit]
-        x = pick(x, mine, last) + swap(
-            pick(x, 1 - mine, last).astype(bf16), "mp", bit
-        ).astype(f32)
-    return x
+def halve_second(mine, other, axis):
+    return mine + paired(other.astype(bf16), axis, False).astype(f32)
 
 
-def scatter_zh(x):
-    me = lax.axis_index("zh")
-    half = x.shape[-1] // 2
-    far = pick(x, (me + 2) % 4)
-    after, before = pick(x, (me + 1) % 4), pick(x, (me + 3) % 4)
-    from_after = shift(far[:, :half].astype(bf16), "zh", 3)
-    from_before = shift(far[:, half:].astype(bf16), "zh", 1)
-    to_before = jnp.concatenate(
-        [before[:, :half] + from_after.astype(f32), before[:, half:]], axis=1
-    ).astype(bf16)
-    to_after = jnp.concatenate(
-        [after[:, :half], after[:, half:] + from_before.astype(f32)], axis=1
-    ).astype(bf16)
-    return pick(x, me) + shift(to_before, "zh", 3).astype(f32) + shift(to_after, "zh", 1).astype(f32)
+def halve_mp(x, bit):
+    mine = (lax.axis_index("mp") // bit) % 2
+    return pick(x, mine).astype(f32) + swap(pick(x, 1 - mine).astype(bf16), "mp", bit).astype(f32)
 
 
 def body(queries, latents, kv_weight, token_image, image_counts, out_grad):
@@ -134,18 +134,28 @@
 
     core = lax.axis_index("core")
     grad_term = jnp.dot(lat_t, dflat, preferred_element_type=f32).astype(bf16)
-    grad_term = grad_term.reshape(4, 4, 2, depth, 2 * local_features)
-    grad_sum = pick(grad_term, core, 2).astype(f32) + swap(
-        pick(grad_term, 1 - core, 2), "core", 1
-    ).astype(f32)
-    grad_sum = scatter_direct(grad_sum.transpose(1, 0, 2, 3).astype(bf16), "y")
-    kv_grad = scatter_zh(grad_sum)
-
+    grad_term = grad_term.reshape(4, 4, 2, depth, 2 * local_features).transpose(2, 1, 0, 3, 4)
     lat_term = lax.dot_general(
         weights, dflat, (((1,), (1,)), ((), ())), preferred_element_type=f32
     ).astype(bf16)
-    lat_sum = scatter_direct(lat_term.reshape(4, 8, depth, rows), "section")
-    latent_grad = scatter_halving(lat_sum)
+    lat_term = lat_term.reshape(4, 2, 2, 2, depth, rows).transpose(0, 3, 2, 1, 4, 5)
+
+    grad_sum = pick(grad_term, core).astype(f32) + swap(
+        pick(grad_term, 1 - core), "core", 1
+    ).astype(f32)
+    lat_mine, lat_other = halve_first(lat_term, "section")
+    grad_sum, lat_mine, lat_other = lax.optimization_barrier((grad_sum, lat_mine, lat_other))
+    mine, other = halve_first(grad_sum, "y")
+    lat_sum = halve_second(lat_mine, lat_other, "section")
+    mine, other, lat_sum = lax.optimization_barrier((mine, other, lat_sum))
+    grad_sum = halve_second(mine, other, "y")
+    lat_sum = halve_mp(lat_sum, 1)
+    grad_sum, lat_sum = lax.optimization_barrier((grad_sum, lat_sum))
+    mine, other = halve_first(grad_sum, "zh")
+    lat_sum = halve_mp(lat_sum, 2)
+    lat_sum = halve_mp(lat_sum, 4)
+    kv_grad = halve_second(mine, other, "zh")
+    latent_grad = lat_sum
     return (
         attended[None],
         kv_grad.reshape(1, depth, 2, local_features),

time: 215 us -> 196 us (0.912)
  the two profiles are of different devices: /device:TPU:16 before, /device:TPU:93 now
where the time goes in v2:
time: 196 us; the launch traced here: 195 us
  starting transfers between devices  102 us (52%)
  waiting for transfers between devices  41.4 us (21%)
  local copies, waits for them, and re-layouts  21.4 us (11%)
  other arithmetic  16.9 us (9%)
  matrix products  11.9 us (6%)
    ppermute x8, starting transfers between devices, paired(): return lax.ppermute(x, axes, pairs)  64 us
    ppermute x7, starting transfers between devices, swap(): return lax.ppermute(x, axis, [(i, i ^ bit) for i in range(SIZE[axis])])  37.7 us
    ppermute x8, waiting for transfers between devices, paired(): return lax.ppermute(x, axes, pairs)  33.6 us
    unnamed x39, local copies, waits for them, and re-layouts  8.83 us
    ppermute x7, waiting for transfers between devices, swap(): return lax.ppermute(x, axis, [(i, i ^ bit) for i in range(SIZE[axis])])  7.85 us
  transfers between devices with their start and end apart: 15, of which 10 were waited for; matrix products, arithmetic and copies ran while one was open for 11% of the time, Pallas kernels for 0%

profile of v2, /device:TPU:93, one launch (start us, length us, event | category | flops | bytes accessed | tf_op | source)
XLA Modules:
  0.0 194.7 jit_solution(11993456932985432017)
XLA Ops:
  1.6 8.8 %collective-permute-start = (bf16[48,384]{1,0:T(8,128)(2,1)S(1)}, bf16[48,384]{1,0:T(8,128)(2,1)S(1)}, u32[]{:S(2)}, u32[]{:S(2)}) collective-permute-start(bf16[48,384]{1,0:T(8,128)(2,1)S(1)} %bitcast.135), channel_id=1, source_target_pairs={{0,4},{1,5},{2,6},{3,7},{4,0},{5,1},{6,2},{7,3},{8,12},{9,13},{10,... | collective-permute-start | bytes 110600 | tf_op jit(solution)/shard_map/ppermute | solution.py:55
  11.7 1.9 collective-permute-start.1
  13.7 4.0 %collective-permute-done.1 = bf16[96,384]{1,0:T(8,128)(2,1)S(1)} collective-permute-done((bf16[96,384]{1,0:T(8,128)(2,1)S(1)}, bf16[96,384]{1,0:T(8,128)(2,1)S(1)}, u32[]{:S(2)}, u32[]{:S(2)}) %collective-permute-start.1) | collective-permute-done | bytes 73760 | tf_op jit(solution)/shard_map/ppermute | solution.py:55
  17.8 4.4 %collective-permute-start.2 = (bf16[192,384]{1,0:T(8,128)(2,1)S(1)}, bf16[192,384]{1,0:T(8,128)(2,1)S(1)}, u32[]{:S(2)}, u32[]{:S(2)}) collective-permute-start(bf16[192,384]{1,0:T(8,128)(2,1)S(1)} %maximum_select_fusion.2), channel_id=1, source_target_pairs={{0,1},{1,0},{2,3},{3,2},{4,5},{5,4},{6,7},{7,6},{8,9},{9,8},{10,11... | collective-permute-start | bytes 442376 | tf_op jit(solution)/shard_map/ppermute | solution.py:55
  22.2 2.5 %collective-permute-done.2 = bf16[192,384]{1,0:T(8,128)(2,1)S(1)} collective-permute-done((bf16[192,384]{1,0:T(8,128)(2,1)S(1)}, bf16[192,384]{1,0:T(8,128)(2,1)S(1)}, u32[]{:S(2)}, u32[]{:S(2)}) %collective-permute-start.2) | collective-permute-done | bytes 147488 | tf_op jit(solution)/shard_map/ppermute | solution.py:55
  24.8 3.1 %collective-permute-start.3 = (bf16[384,384]{1,0:T(8,128)(2,1)S(1)}, bf16[384,384]{1,0:T(8,128)(2,1)S(1)}, u32[]{:S(2)}, u32[]{:S(2)}) collective-permute-start(bf16[384,384]{1,0:T(8,128)(2,1)S(1)} %maximum_select_fusion.1), channel_id=1, source_target_pairs={{0,24},{8,16},{16,8},{24,0},{32,40},{40,32},{48,56},{56,48},{1,25}... | collective-permute-start | bytes 884744 | tf_op jit(solution)/shard_map/ppermute | solution.py:74
  29.1 3.4 %collective-permute-done.3 = bf16[384,384]{1,0:T(8,128)(2,1)S(1)} collective-permute-done((bf16[384,384]{1,0:T(8,128)(2,1)S(1)}, bf16[384,384]{1,0:T(8,128)(2,1)S(1)}, u32[]{:S(2)}, u32[]{:S(2)}) %collective-permute-start.3) | collective-permute-done | bytes 294944 | tf_op jit(solution)/shard_map/ppermute | solution.py:74
  34.1 2.2 %collective-permute-start.4 = (bf16[2,384,384]{2,1,0:T(8,128)(2,1)}, bf16[2,384,384]{2,1,0:T(8,128)(2,1)}, u32[]{:S(2)}, u32[]{:S(2)}) collective-permute-start(bf16[2,384,384]{2,1,0:T(8,128)(2,1)} %pad_maximum_fusion.4), channel_id=1, source_target_pairs={{0,8},{8,0},{16,24},{24,16},{32,56},{40,48},{48,40},{56,32},{1,9},... | collective-permute-start | bytes 1769480 | tf_op jit(solution)/shard_map/ppermute | solution.py:74
  36.3 1.7 reshape_squeeze.14
  38.1 1.7 reshape_squeeze.15
  39.8 2.5 %copy.74 = bf16[192,8,2,512]{3,1,2,0:T(8,128)(2,1)} copy(bf16[192,8,2,512]{3,2,1,0:T(2,128)(2,1)S(1)} %bitcast.120) | data formatting | bytes 6291456
  42.5 2.8 %collective-permute-done.4 = bf16[2,384,384]{2,1,0:T(8,128)(2,1)} collective-permute-done((bf16[2,384,384]{2,1,0:T(8,128)(2,1)}, bf16[2,384,384]{2,1,0:T(8,128)(2,1)}, u32[]{:S(2)}, u32[]{:S(2)}) %collective-permute-start.4) | collective-permute-done | bytes 589856 | tf_op jit(solution)/shard_map/ppermute | solution.py:74
  50.7 3.4 %slice_reduce_fusion = (bf16[2,192,512]{2,1,0:T(8,128)(2,1)S(1)}, bf16[2,192,512]{2,1,0:T(8,128)(2,1)S(1)}) fusion(bf16[2,192,2,512]{3,2,1,0:T(2,128)(2,1)S(1)} %reshape.220), kind=kLoop, calls=%fused_computation.33 | loop fusion | bytes 1572864 | tf_op jit(solution)/shard_map/slice | solution.py:20
  57.7 2.3 %fusion.14 = bf16[2,192,4,128]{3,1,2,0:T(8,128)(2,1)S(1)} fusion(f32[2,4,128,192]{2,3,1,0:T(8,128)} %convolution_bitcast_fusion, bf16[2,128,4,128]{3,2,1,0:T(4,128)(2,1)S(1)} %copy-done.11, f32[2,4,128,192]{2,3,1,0:T(8,128)} %get-tuple-element.41, f32[2,4,128]{2,1,0:T(4,128)S(1)} %compare_select_fusion), kind=kOutput, calls=%fused_computation.22 | convolution fusion | flops 51905728 | bytes 2232320 | tf_op jit(solution)/shard_map/bhtr,bthe->brhe/dot_general | solution.py:45
  61.5 1.8 convolution_convert_fusion
  65.0 7.7 %collective-permute-start.5 = (bf16[4,4,48,1024]{3,2,0,1:T(8,128)(2,1)S(1)}, bf16[4,4,48,1024]{3,2,0,1:T(8,128)(2,1)}, u32[]{:S(2)}, u32[]{:S(2)}) collective-permute-start(bf16[4,4,48,1024]{3,2,0,1:T(8,128)(2,1)S(1)} %dynamic-slice_bitcast_fusion), channel_id=1, source_target_pairs={{0,32},{32,0},{1,33},{33,1},{2,34},{34,2},{3,35},{35,3},{4,36},{36... | collective-permute-start | bytes 4718600 | tf_op jit(solution)/shard_map/ppermute | solution.py:55
  72.8 2.5 %fusion.2 = bf16[1536,384]{0,1:T(8,128)(2,1)} fusion(bf16[384,1024]{1,0:T(8,128)(2,1)S(1)} %bitcast.132, bf16[1536,1024]{1,0:T(8,128)(2,1)S(1)} %bitcast.122), kind=kOutput, calls=%fused_computation.5 | convolution fusion | flops 1208549376 | bytes 5111808 | tf_op jit(solution)/shard_map/dot_general | solution.py:138
  77.9 1.9 collective-permute-start.6
  79.9 9.3 %collective-permute-done.6 = bf16[2,2,2,2,48,384]{5,4,1,2,3,0:T(8,128)(2,1)} collective-permute-done((bf16[2,2,2,2,48,384]{5,4,1,2,3,0:T(8,128)(2,1)}, bf16[2,2,2,2,48,384]{5,4,1,2,3,0:T(8,128)(2,1)}, u32[]{:S(2)}, u32[]{:S(2)}) %collective-permute-start.6) | collective-permute-done | bytes 589856 | tf_op jit(solution)/shard_map/ppermute | solution.py:74
  92.1 2.0 %bitcast_add_fusion = f32[4,4,48,1024]{3,2,0,1:T(8,128)S(1)} fusion(bf16[4,4,48,1024]{3,2,0,1:T(8,128)(2,1)} %collective-permute-done.5, bf16[4,4,2,48,1024]{4,3,2,1,0:T(8,128)(2,1)S(1)} %bitcast.125, s32[]{:T(128)S(6)} %select_n.257), kind=kLoop, calls=%fused_computation.3 | loop fusion | flops 2359296 | bytes 6291460 | tf_op jit(solution)/shard_map/add | solution.py:143
  95.2 10.8 %collective-permute-start.7 = (bf16[2,4,48,1024]{3,2,1,0:T(8,128)(2,1)}, bf16[2,4,48,1024]{3,2,1,0:T(8,128)(2,1)}, u32[]{:S(2)}, u32[]{:S(2)}) collective-permute-start(bf16[2,4,48,1024]{3,2,1,0:T(8,128)(2,1)} %pad_maximum_fusion.3), channel_id=1, source_target_pairs={{0,64},{32,224},{64,0},{96,160},{128,192},{160,96},{192,128},{224,... | collective-permute-start | bytes 2359304 | tf_op jit(solution)/shard_map/ppermute | solution.py:74
  106.1 4.2 %collective-permute-start.8 = (bf16[2,2,2,48,384]{4,3,0,1,2:T(8,128)(2,1)}, bf16[2,2,2,48,384]{4,3,0,1,2:T(8,128)(2,1)}, u32[]{:S(2)}, u32[]{:S(2)}) collective-permute-start(bf16[2,2,2,48,384]{4,3,0,1,2:T(8,128)(2,1)} %fusion.21), channel_id=1, source_target_pairs={{0,24},{8,16},{16,8},{24,0},{32,40},{40,32},{48,56},{56,48},{1,25}... | collective-permute-start | bytes 884744 | tf_op jit(solution)/shard_map/ppermute | solution.py:74
  110.4 4.3 %collective-permute-done.8 = bf16[2,2,2,48,384]{4,3,0,1,2:T(8,128)(2,1)} collective-permute-done((bf16[2,2,2,48,384]{4,3,0,1,2:T(8,128)(2,1)}, bf16[2,2,2,48,384]{4,3,0,1,2:T(8,128)(2,1)}, u32[]{:S(2)}, u32[]{:S(2)}) %collective-permute-start.8) | collective-permute-done | bytes 294944 | tf_op jit(solution)/shard_map/ppermute | solution.py:74
  119.4 2.1 %collective-permute-start.10 = (bf16[2,2,48,384]{3,2,1,0:T(8,128)(2,1)S(1)}, bf16[2,2,48,384]{3,2,1,0:T(8,128)(2,1)S(1)}, u32[]{:S(2)}, u32[]{:S(2)}) collective-permute-start(bf16[2,2,48,384]{3,2,1,0:T(8,128)(2,1)S(1)} %copy_bitcast_fusion), channel_id=1, source_target_pairs={{0,1},{1,0},{2,3},{3,2},{4,5},{5,4},{6,7},{7,6},{8,9},{9,8},{10,11... | collective-permute-start | bytes 442376 | tf_op jit(solution)/shard_map/ppermute | solution.py:55
  121.4 1.9 collective-permute-start.9
  123.4 2.0 %convolution_convert_fusion.4 = bf16[2,4,128,128]{3,2,1,0:T(8,128)(2,1)S(1)} fusion(f32[2,4,128]{2,1,0:T(4,128)S(1)} %compare_select_fusion, f32[2,4,128,192]{2,3,1,0:T(8,128)} %copy-done.4, pred[2,128,192]{1,2,0:T(8,128)(4,1)} %copy-done.14, bf16[2,192,512]{2,1,0:T(8,128)(2,1)S(1)} %get-tuple-element.29), kind=kOutput, calls=%fused_computation.23 | convolution fusion | flops 51446976 | bytes 1495040 | tf_op jit(solution)/shard_map/bhtr,brhe->bthe/dot_general | solution.py:37
  126.3 4.2 %collective-permute-done.9 = bf16[4,48,1024]{2,1,0:T(8,128)(2,1)S(1)} collective-permute-done((bf16[4,48,1024]{2,1,0:T(8,128)(2,1)}, bf16[4,48,1024]{2,1,0:T(8,128)(2,1)S(1)}, u32[]{:S(2)}, u32[]{:S(2)}) %collective-permute-start.9) | collective-permute-done | bytes 393248 | tf_op jit(solution)/shard_map/ppermute | solution.py:74
  130.6 4.3 %collective-permute-start.13 = (bf16[2,48,384]{2,1,0:T(8,128)(2,1)S(1)}, bf16[2,48,384]{2,1,0:T(8,128)(2,1)S(1)}, u32[]{:S(2)}, u32[]{:S(2)}) collective-permute-start(bf16[2,48,384]{2,1,0:T(8,128)(2,1)S(1)} %fusion.42), channel_id=1, source_target_pairs={{0,2},{1,3},{2,0},{3,1},{4,6},{5,7},{6,4},{7,5},{8,10},{9,11},{10,... | collective-permute-start | bytes 221192 | tf_op jit(solution)/shard_map/ppermute | solution.py:55
  134.9 8.2 %collective-permute-start.11 = (bf16[2,48,1024]{2,1,0:T(8,128)(2,1)S(1)}, bf16[2,48,1024]{2,1,0:T(8,128)(2,1)S(1)}, u32[]{:S(2)}, u32[]{:S(2)}) collective-permute-start(bf16[2,48,1024]{2,1,0:T(8,128)(2,1)S(1)} %pad_maximum_fusion.6), channel_id=1, source_target_pairs={{0,256},{1,769},{2,258},{3,771},{4,260},{5,773},{6,262},{7,775},{2... | collective-permute-start | bytes 589832 | tf_op jit(solution)/shard_map/ppermute | solution.py:74
  143.2 8.5 %collective-permute-start.14 = (bf16[48,384]{1,0:T(8,128)(2,1)S(1)}, bf16[48,384]{1,0:T(8,128)(2,1)S(1)}, u32[]{:S(2)}, u32[]{:S(2)}) collective-permute-start(bf16[48,384]{1,0:T(8,128)(2,1)S(1)} %fusion.44), channel_id=1, source_target_pairs={{0,4},{1,5},{2,6},{3,7},{4,0},{5,1},{6,2},{7,3},{8,12},{9,13},{10,... | collective-permute-start | bytes 110600 | tf_op jit(solution)/shard_map/ppermute | solution.py:55
  153.2 31.8 %collective-permute-start.12 = (bf16[48,1024]{1,0:T(8,128)(2,1)S(1)}, bf16[48,1024]{1,0:T(8,128)(2,1)S(1)}, u32[]{:S(2)}, u32[]{:S(2)}) collective-permute-start(bf16[48,1024]{1,0:T(8,128)(2,1)S(1)} %fusion.41), channel_id=1, source_target_pairs={{0,768},{1,257},{2,770},{3,259},{4,772},{5,261},{6,774},{7,263},{2... | collective-permute-start | bytes 294920 | tf_op jit(solution)/shard_map/ppermute | solution.py:74
  185.8 8.1 %collective-permute-done.12 = bf16[48,1024]{1,0:T(8,128)(2,1)S(1)} collective-permute-done((bf16[48,1024]{1,0:T(8,128)(2,1)S(1)}, bf16[48,1024]{1,0:T(8,128)(2,1)S(1)}, u32[]{:S(2)}, u32[]{:S(2)}) %collective-permute-start.12) | collective-permute-done | bytes 98336 | tf_op jit(solution)/shard_map/ppermute | solution.py:74
  (98 shorter events, 33.0 us)
Async XLA Ops:
  1.6 10.2 %collective-permute-start = (bf16[48,384]{1,0:T(8,128)(2,1)S(1)}, bf16[48,384]{1,0:T(8,128)(2,1)S(1)}, u32[]{:S(2)}, u32[]{:S(2)}) collective-permute-start(bf16[48,384]{1,0:T(8,128)(2,1)S(1)} %bitcast.135), channel_id=1, source_target_pairs={{0,4},{1,5},{2,6},{3,7},{4,0},{5,1},{6,2},{7,3},{8,12},{9,13},{10,... | collective-permute-start | bytes 110600 | tf_op jit(solution)/shard_map/ppermute | solution.py:55
  11.7 6.0 %collective-permute-start.1 = (bf16[96,384]{1,0:T(8,128)(2,1)S(1)}, bf16[96,384]{1,0:T(8,128)(2,1)S(1)}, u32[]{:S(2)}, u32[]{:S(2)}) collective-permute-start(bf16[96,384]{1,0:T(8,128)(2,1)S(1)} %maximum_select_fusion.3), channel_id=1, source_target_pairs={{0,2},{1,3},{2,0},{3,1},{4,6},{5,7},{6,4},{7,5},{8,10},{9,11},{10,... | collective-permute-start | bytes 221192 | tf_op jit(solution)/shard_map/ppermute | solution.py:55
  17.8 10.1 %copy-start.9 = (bf16[192,384]{1,0:T(8,128)(2,1)}, bf16[192,384]{1,0:T(8,128)(2,1)S(1)}, u32[]{:S(2)}) copy-start(bf16[192,384]{1,0:T(8,128)(2,1)S(1)} %maximum_select_fusion.2) | copy-start | bytes 442372
  17.8 6.9 %collective-permute-start.2 = (bf16[192,384]{1,0:T(8,128)(2,1)S(1)}, bf16[192,384]{1,0:T(8,128)(2,1)S(1)}, u32[]{:S(2)}, u32[]{:S(2)}) collective-permute-start(bf16[192,384]{1,0:T(8,128)(2,1)S(1)} %maximum_select_fusion.2), channel_id=1, source_target_pairs={{0,1},{1,0},{2,3},{3,2},{4,5},{5,4},{6,7},{7,6},{8,9},{9,8},{10,11... | collective-permute-start | bytes 442376 | tf_op jit(solution)/shard_map/ppermute | solution.py:55
  24.7 3.2 %copy-start.13 = (bf16[192,384]{1,0:T(8,128)(2,1)}, bf16[192,384]{1,0:T(8,128)(2,1)S(1)}, u32[]{:S(2)}) copy-start(bf16[192,384]{1,0:T(8,128)(2,1)S(1)} %collective-permute-done.2) | copy-start | bytes 442372
  24.7 15.1 %copy-start = (bf16[1,1536,2,512]{3,2,1,0:T(2,128)(2,1)S(1)}, bf16[1,1536,2,512]{3,2,1,0:T(2,128)(2,1)}, u32[]{:S(2)}) copy-start(bf16[1,1536,2,512]{3,2,1,0:T(2,128)(2,1)} %param.8) | copy-start | bytes 9437188
  24.8 7.7 %collective-permute-start.3 = (bf16[384,384]{1,0:T(8,128)(2,1)S(1)}, bf16[384,384]{1,0:T(8,128)(2,1)S(1)}, u32[]{:S(2)}, u32[]{:S(2)}) collective-permute-start(bf16[384,384]{1,0:T(8,128)(2,1)S(1)} %maximum_select_fusion.1), channel_id=1, source_target_pairs={{0,24},{8,16},{16,8},{24,0},{32,40},{40,32},{48,56},{56,48},{1,25}... | collective-permute-start | bytes 884744 | tf_op jit(solution)/shard_map/ppermute | solution.py:74
  32.5 0.7 copy-start.10
  34.1 11.2 %collective-permute-start.4 = (bf16[2,384,384]{2,1,0:T(8,128)(2,1)}, bf16[2,384,384]{2,1,0:T(8,128)(2,1)}, u32[]{:S(2)}, u32[]{:S(2)}) collective-permute-start(bf16[2,384,384]{2,1,0:T(8,128)(2,1)} %pad_maximum_fusion.4), channel_id=1, source_target_pairs={{0,8},{8,0},{16,24},{24,16},{32,56},{40,48},{48,40},{56,32},{1,9},... | collective-permute-start | bytes 1769480 | tf_op jit(solution)/shard_map/ppermute | solution.py:74
  39.8 2.5 %copy-start.16 = (s32[2]{0:T(128)S(1)}, s32[2]{0:T(128)}, u32[]{:S(2)}) copy-start(s32[2]{0:T(128)} %param.10) | copy-start | bytes 28
  39.8 2.6 %copy-start.15 = (s32[2,128]{1,0:T(2,128)S(1)}, s32[2,128]{1,0:T(2,128)}, u32[]{:S(2)}) copy-start(s32[2,128]{1,0:T(2,128)} %param.9) | copy-start | bytes 3076
  42.5 14.3 %copy-start.14 = (pred[2,128,192]{1,2,0:T(8,128)(4,1)}, pred[2,128,192]{1,2,0:T(8,128)(4,1)S(1)}, u32[]{:S(2)}) copy-start(pred[2,128,192]{1,2,0:T(8,128)(4,1)S(1)} %compare_and_fusion) | copy-start | bytes 147460
  46.8 1.9 copy-start.1
  50.7 3.4 %copy-start.11 = (bf16[2,128,4,128]{3,2,1,0:T(4,128)(2,1)S(1)}, bf16[2,128,4,128]{3,2,1,0:T(4,128)(2,1)}, u32[]{:S(2)}) copy-start(bf16[2,128,4,128]{3,2,1,0:T(4,128)(2,1)} %reshape_squeeze.14) | copy-start | bytes 786436
  54.1 1.5 copy-start.12
  54.4 2.8 %copy-start.4 = (f32[2,4,128,192]{2,3,1,0:T(8,128)}, f32[2,4,128,192]{2,3,1,0:T(8,128)S(1)}, u32[]{:S(2)}) copy-start(f32[2,4,128,192]{2,3,1,0:T(8,128)S(1)} %fusion.5) | copy-start | bytes 2359300
  63.3 1.7 copy-start.5
  63.3 9.4 %copy-start.2 = (bf16[192,8,2,512]{3,1,2,0:T(8,128)(2,1)S(1)}, bf16[192,8,2,512]{3,1,2,0:T(8,128)(2,1)}, u32[]{:S(2)}) copy-start(bf16[192,8,2,512]{3,1,2,0:T(8,128)(2,1)} %copy.74) | copy-start | bytes 9437188
  65.0 27.1 %collective-permute-start.5 = (bf16[4,4,48,1024]{3,2,0,1:T(8,128)(2,1)S(1)}, bf16[4,4,48,1024]{3,2,0,1:T(8,128)(2,1)}, u32[]{:S(2)}, u32[]{:S(2)}) collective-permute-start(bf16[4,4,48,1024]{3,2,0,1:T(8,128)(2,1)S(1)} %dynamic-slice_bitcast_fusion), channel_id=1, source_target_pairs={{0,32},{32,0},{1,33},{33,1},{2,34},{34,2},{3,35},{35,3},{4,36},{36... | collective-permute-start | bytes 4718600 | tf_op jit(solution)/shard_map/ppermute | solution.py:55
  77.9 11.2 %collective-permute-start.6 = (bf16[2,2,2,2,48,384]{5,4,1,2,3,0:T(8,128)(2,1)}, bf16[2,2,2,2,48,384]{5,4,1,2,3,0:T(8,128)(2,1)}, u32[]{:S(2)}, u32[]{:S(2)}) collective-permute-start(bf16[2,2,2,2,48,384]{5,4,1,2,3,0:T(8,128)(2,1)} %pad_maximum_fusion.5), channel_id=1, source_target_pairs={{0,8},{8,0},{16,24},{24,16},{32,56},{40,48},{48,40},{56,32},{1,9},... | collective-permute-start | bytes 1769480 | tf_op jit(solution)/shard_map/ppermute | solution.py:74
  89.1 3.0 %copy-start.6 = (bf16[1536,1024]{1,0:T(8,128)(2,1)S(1)}, bf16[1536,1024]{1,0:T(8,128)(2,1)}, u32[]{:S(2)}) copy-start(bf16[1536,1024]{1,0:T(8,128)(2,1)} %copy-done.5) | copy-start | bytes 9437188
  95.2 20.7 %collective-permute-start.7 = (bf16[2,4,48,1024]{3,2,1,0:T(8,128)(2,1)}, bf16[2,4,48,1024]{3,2,1,0:T(8,128)(2,1)}, u32[]{:S(2)}, u32[]{:S(2)}) collective-permute-start(bf16[2,4,48,1024]{3,2,1,0:T(8,128)(2,1)} %pad_maximum_fusion.3), channel_id=1, source_target_pairs={{0,64},{32,224},{64,0},{96,160},{128,192},{160,96},{192,128},{224,... | collective-permute-start | bytes 2359304 | tf_op jit(solution)/shard_map/ppermute | solution.py:74
  106.1 8.7 %collective-permute-start.8 = (bf16[2,2,2,48,384]{4,3,0,1,2:T(8,128)(2,1)}, bf16[2,2,2,48,384]{4,3,0,1,2:T(8,128)(2,1)}, u32[]{:S(2)}, u32[]{:S(2)}) collective-permute-start(bf16[2,2,2,48,384]{4,3,0,1,2:T(8,128)(2,1)} %fusion.21), channel_id=1, source_target_pairs={{0,24},{8,16},{16,8},{24,0},{32,40},{40,32},{48,56},{56,48},{1,25}... | collective-permute-start | bytes 884744 | tf_op jit(solution)/shard_map/ppermute | solution.py:74
  116.0 3.4 %copy-start.7 = (f32[2,2,2,48,384]{4,3,0,1,2:T(8,128)}, f32[2,2,2,48,384]{4,3,0,1,2:T(8,128)S(1)}, u32[]{:S(2)}) copy-start(f32[2,2,2,48,384]{4,3,0,1,2:T(8,128)S(1)} %convert_add_fusion.1) | copy-start | bytes 1769476
  119.4 6.9 %copy-start.8 = (f32[2,2,2,48,384]{4,3,0,1,2:T(8,128)S(1)}, f32[2,2,2,48,384]{4,3,0,1,2:T(8,128)}, u32[]{:S(2)}) copy-start(f32[2,2,2,48,384]{4,3,0,1,2:T(8,128)} %copy-done.7) | copy-start | bytes 1769476
  119.4 6.9 %collective-permute-start.10 = (bf16[2,2,48,384]{3,2,1,0:T(8,128)(2,1)S(1)}, bf16[2,2,48,384]{3,2,1,0:T(8,128)(2,1)S(1)}, u32[]{:S(2)}, u32[]{:S(2)}) collective-permute-start(bf16[2,2,48,384]{3,2,1,0:T(8,128)(2,1)S(1)} %copy_bitcast_fusion), channel_id=1, source_target_pairs={{0,1},{1,0},{2,3},{3,2},{4,5},{5,4},{6,7},{7,6},{8,9},{9,8},{10,11... | collective-permute-start | bytes 442376 | tf_op jit(solution)/shard_map/ppermute | solution.py:55
  121.4 9.0 %collective-permute-start.9 = (bf16[4,48,1024]{2,1,0:T(8,128)(2,1)}, bf16[4,48,1024]{2,1,0:T(8,128)(2,1)S(1)}, u32[]{:S(2)}, u32[]{:S(2)}) collective-permute-start(bf16[4,48,1024]{2,1,0:T(8,128)(2,1)} %fusion.17), channel_id=1, source_target_pairs={{0,192},{32,96},{64,128},{96,32},{128,64},{160,224},{192,0},{224,1... | collective-permute-start | bytes 1179656 | tf_op jit(solution)/shard_map/ppermute | solution.py:74
  125.4 5.1 %copy-start.3 = (f32[4,48,1024]{2,1,0:T(8,128)S(1)}, f32[4,48,1024]{2,1,0:T(8,128)}, u32[]{:S(2)}) copy-start(f32[4,48,1024]{2,1,0:T(8,128)} %fusion.18) | copy-start | bytes 2359300
  130.6 12.5 %collective-permute-start.13 = (bf16[2,48,384]{2,1,0:T(8,128)(2,1)S(1)}, bf16[2,48,384]{2,1,0:T(8,128)(2,1)S(1)}, u32[]{:S(2)}, u32[]{:S(2)}) collective-permute-start(bf16[2,48,384]{2,1,0:T(8,128)(2,1)S(1)} %fusion.42), channel_id=1, source_target_pairs={{0,2},{1,3},{2,0},{3,1},{4,6},{5,7},{6,4},{7,5},{8,10},{9,11},{10,... | collective-permute-start | bytes 221192 | tf_op jit(solution)/shard_map/ppermute | solution.py:55
  134.9 18.2 %collective-permute-start.11 = (bf16[2,48,1024]{2,1,0:T(8,128)(2,1)S(1)}, bf16[2,48,1024]{2,1,0:T(8,128)(2,1)S(1)}, u32[]{:S(2)}, u32[]{:S(2)}) collective-permute-start(bf16[2,48,1024]{2,1,0:T(8,128)(2,1)S(1)} %pad_maximum_fusion.6), channel_id=1, source_target_pairs={{0,256},{1,769},{2,258},{3,771},{4,260},{5,773},{6,262},{7,775},{2... | collective-permute-start | bytes 589832 | tf_op jit(solution)/shard_map/ppermute | solution.py:74
  143.2 41.8 %collective-permute-start.14 = (bf16[48,384]{1,0:T(8,128)(2,1)S(1)}, bf16[48,384]{1,0:T(8,128)(2,1)S(1)}, u32[]{:S(2)}, u32[]{:S(2)}) collective-permute-start(bf16[48,384]{1,0:T(8,128)(2,1)S(1)} %fusion.44), channel_id=1, source_target_pairs={{0,4},{1,5},{2,6},{3,7},{4,0},{5,1},{6,2},{7,3},{8,12},{9,13},{10,... | collective-permute-start | bytes 110600 | tf_op jit(solution)/shard_map/ppermute | solution.py:55
  153.2 40.6 %collective-permute-start.12 = (bf16[48,1024]{1,0:T(8,128)(2,1)S(1)}, bf16[48,1024]{1,0:T(8,128)(2,1)S(1)}, u32[]{:S(2)}, u32[]{:S(2)}) collective-permute-start(bf16[48,1024]{1,0:T(8,128)(2,1)S(1)} %fusion.41), channel_id=1, source_target_pairs={{0,768},{1,257},{2,770},{3,259},{4,772},{5,261},{6,774},{7,263},{2... | collective-permute-start | bytes 294920 | tf_op jit(solution)/shard_map/ppermute | solution.py:74

commit v3 on v0

v3 whole, which is shorter than its diff:
```python
import functools

import jax
import jax.numpy as jnp
from jax import lax
from jax.experimental import pallas as pl
from jax.experimental.pallas import tpu as pltpu
from jax.sharding import Mesh, PartitionSpec as P

HEAD = 128
LATENTS = 64
SIZES = (("zh", 4), ("y", 4), ("core", 2), ("section", 4), ("mp", 8))
AXES = tuple(name for name, _ in SIZES)
SIZE = dict(SIZES)
DP = ("zh", "y", "core")
f32, bf16 = jnp.float32, jnp.bfloat16
VMEM = pl.BlockSpec(memory_space=pltpu.VMEM)
SMEM = pl.BlockSpec(memory_space=pltpu.SMEM)
TRANS_A = (((0,), (0,)), ((), ()))
TRANS_B = (((1,), (1,)), ((), ()))


def dot(a, b, dims=(((1,), (0,)), ((), ()))):
    return lax.dot_general(a, b, dims, preferred_element_type=f32)


PARITY = {"y": "core", "section": "core", "zh": "mp"}


def relative(axis):
    me, odd = lax.axis_index(axis), lax.axis_index(PARITY[axis]) % 2
    return [me, me ^ (3 - 2 * odd), me ^ (1 + 2 * odd), me ^ 2]


def paired(x, axis, first):
    axes = tuple(name for name in AXES if name in (axis, PARITY[axis]))
    pairs = []
    for at in range(SIZE[axes[0]] * SIZE[axes[1]]):
        place = dict(zip(axes, divmod(at, SIZE[axes[1]])))
        odd = place[PARITY[axis]] % 2
        place[axis] ^= 1 + 2 * odd if first else 3 - 2 * odd
        pairs.append((at, place[axes[0]] * SIZE[axes[1]] + place[axes[1]]))
    return lax.ppermute(x, axes, pairs)


def swap(x, axis, bit):
    return lax.ppermute(x, axis, [(i, i ^ bit) for i in range(SIZE[axis])])


def gather_latents(own):
    block = own
    for axis in ("mp", "section"):
        copies = jnp.broadcast_to(block, (SIZE[axis],) + block.shape)
        block = lax.all_to_all(copies, axis, 0, 0, tiled=True)
        block = block.reshape((-1,) + block.shape[2:])
    return block


def attend_kernel(keys, counts, lat, weight, query, grad, token, attended, dflat, kv):
    samples, _, width = query.shape
    scale = HEAD ** (-0.5)
    kv[...] = dot(lat[...], weight[...], TRANS_A).astype(bf16)
    image_of = lax.broadcasted_iota(jnp.int32, (keys, query.shape[1]), 0) // LATENTS
    for b in range(samples):
        rows = slice(b * keys, (b + 1) * keys)
        allowed = (image_of == token[b]) & (image_of < counts[b])
        for h in range(width // HEAD):
            low = slice(h * HEAD, (h + 1) * HEAD)
            high = slice(width + h * HEAD, width + (h + 1) * HEAD)
            k, v, q, g = kv[rows, low], kv[rows, high], query[b, :, low], grad[b, :, low]
            scores = dot(k, q, TRANS_B) * scale
            top = jnp.max(jnp.where(allowed, scores, -1e30), axis=0, keepdims=True)
            expval = jnp.where(allowed, jnp.exp(scores - top), 0.0)
            total = jnp.sum(expval, axis=0, keepdims=True)
            prob = expval / jnp.where(total > 0, total, 1.0)
            prob_bf = prob.astype(bf16)
            attended[b, :, low] = dot(prob_bf, v, TRANS_A).astype(bf16)
            dprob = dot(v, g, TRANS_B)
            dscore = prob * (dprob - jnp.sum(dprob * prob, axis=0, keepdims=True)) * scale
            dflat[rows, low] = dot(dscore.astype(bf16), q).astype(bf16)
            dflat[rows, high] = dot(prob_bf, g).astype(bf16)


def latent_kernel(depth, order, place, weight, dflat, out):
    chunk = out.shape[1]
    for i in range(out.shape[0]):
        start = pl.multiple_of(order[i] * chunk, 128)
        term = dot(weight[pl.ds(start, chunk), :], dflat[...], TRANS_B).astype(out.dtype)
        for m in range(chunk // depth):
            at = pl.multiple_of(place[m] * depth, 16)
            out[i, pl.ds(at, depth), :] = term[m * depth : (m + 1) * depth]


def weight_kernel(depth, blocks, lat, dflat, out, picked):
    for i in range(picked.shape[0] // depth):
        start = pl.multiple_of(blocks[i] * depth, 16)
        picked[i * depth : (i + 1) * depth, :] = lat[pl.ds(start, depth), :]
    out[...] = dot(picked[...], dflat[...]).astype(out.dtype)


def call(kernel, specs, shapes, scratch, flops, *args):
    size = sum(a.size * a.dtype.itemsize for a in args)
    return pl.pallas_call(
        kernel,
        out_shape=shapes,
        in_specs=specs,
        out_specs=jax.tree.map(lambda _: VMEM, shapes),
        scratch_shapes=scratch,
        compiler_params=pltpu.CompilerParams(vmem_limit_bytes=40 << 20),
        cost_estimate=pl.CostEstimate(flops=flops, bytes_accessed=size, transcendentals=0),
    )(*args)


def body(queries, latents, kv_weight, token_image, image_counts, out_grad):
    samples, keys, depth = latents.shape
    rows = samples * keys
    _, width, _, local = kv_weight.shape
    weight = kv_weight.reshape(width, 2 * local)
    core, mp = lax.axis_index("core"), lax.axis_index("mp")
    lat = gather_latents(latents.reshape(rows, depth).T)

    attended, dflat = call(
        functools.partial(attend_kernel, keys),
        [SMEM] + [VMEM] * 5,
        (
            jax.ShapeDtypeStruct(queries.shape[1:], bf16),
            jax.ShapeDtypeStruct((rows, 2 * local), bf16),
        ),
        [pltpu.VMEM((rows, 2 * local), bf16)],
        2 * rows * width * 2 * local,
        image_counts,
        lat,
        weight,
        queries[0],
        out_grad[0],
        token_image.reshape(samples, 1, -1),
    )

    to = jnp.arange(8, dtype=jnp.int32) ^ mp
    place = (to % 2) * 4 + (to // 2 % 2) * 2 + to // 4
    order = jnp.stack(relative("section")).astype(jnp.int32)

    def latent_terms(sections, dtype):
        return call(
            functools.partial(latent_kernel, depth),
            [SMEM, SMEM, VMEM, VMEM],
            jax.ShapeDtypeStruct((2, width // 4, rows), dtype),
            [],
            width * rows * 2 * local,
            sections,
            place,
            weight,
            dflat,
        )

    def weight_terms(at_core, ys, dtype, dflat):
        zs = jnp.stack(relative("zh"))
        blocks = (zs[None, :] * 8 + jnp.stack(ys)[:, None] * 2 + at_core).reshape(-1)
        return call(
            functools.partial(weight_kernel, depth),
            [SMEM, VMEM, VMEM],
            jax.ShapeDtypeStruct((width // 2, 2 * local), dtype),
            [pltpu.VMEM((width // 2, rows), bf16)],
            width * rows * 2 * local,
            blocks.astype(jnp.int32),
            lat,
            dflat,
        ).reshape(4, 4, depth, 2 * local)

    mine, second, first, both = relative("y")
    lat_send = latent_terms(order[2:], bf16)
    lat_send, dflat_next = lax.optimization_barrier((lat_send, dflat))
    grad_send = weight_terms(1 - core, [mine, first, second, both], bf16, dflat_next)
    lat_keep = latent_terms(order[:2], f32)
    grad_keep = weight_terms(core, [mine, second, first, both], f32, dflat)

    grad = grad_keep + swap(grad_send, "core", 1).astype(f32)
    lat_sum = lat_keep + paired(lat_send, "section", True).astype(f32)
    grad, lat_sum = lax.optimization_barrier((grad, lat_sum))

    grad = grad[:2] + paired(grad[2:].astype(bf16), "y", True).astype(f32)
    lat_sum = lat_sum[0] + paired(lat_sum[1].astype(bf16), "section", False).astype(f32)
    grad, lat_sum = lax.optimization_barrier((grad, lat_sum))

    grad = grad[0] + paired(grad[1].astype(bf16), "y", False).astype(f32)
    lat_sum = lat_sum.reshape(8, depth, rows)
    lat_sum = lat_sum[:4] + swap(lat_sum[4:].astype(bf16), "mp", 1).astype(f32)
    grad, lat_sum = lax.optimization_barrier((grad, lat_sum))

    grad = grad[:2] + paired(grad[2:].astype(bf16), "zh", True).astype(f32)
    lat_sum = lat_sum[:2] + swap(lat_sum[2:].astype(bf16), "mp", 2).astype(f32)
    lat_sum = lat_sum[0] + swap(lat_sum[1].astype(bf16), "mp", 4).astype(f32)
    kv_grad = grad[0] + paired(grad[1].astype(bf16), "zh", False).astype(f32)
    return (
        attended[None],
        kv_grad.reshape(1, depth, 2, local),
        lat_sum.T.reshape(samples, keys, depth),
    )


def solution(mesh):
    fine = Mesh(mesh.devices.reshape([n for _, n in SIZES]), AXES)
    return jax.shard_map(
        body,
        mesh=fine,
        in_specs=(
            P("section", DP, None, "mp"),
            P(DP, None, ("section", "mp")),
            P("section", None, None, "mp"),
            P(DP, None),
            P(DP),
            P("section", DP, None, "mp"),
        ),
        out_specs=(
            P("section", DP, None, "mp"),
            P("section", DP, None, "mp"),
            P(DP, None, ("section", "mp")),
        ),
        check_vma=False,
    )
```

time: 748 us -> 171 us (0.23)
  the two profiles are of different devices: /device:TPU:2 before, /device:TPU:112 now
where the time goes in v3:
time: 171 us; the launch traced here: 170 us
  starting transfers between devices  62.1 us (36%)
  waiting for transfers between devices  50.9 us (30%)
  blocking collectives  27.2 us (16%)
  Pallas kernels  15.7 us (9%)
  local copies, waits for them, and re-layouts  9.05 us (5%)
  other arithmetic  4.08 us (2%)
    ppermute x6, starting transfers between devices, paired(): return lax.ppermute(x, axes, pairs)  42.9 us
    ppermute x6, waiting for transfers between devices, paired(): return lax.ppermute(x, axes, pairs)  35.2 us
    all_to_all x1, blocking collectives, gather_latents(): block = lax.all_to_all(copies, axis, 0, 0, tiled=True)  27.2 us
    pallas_call x5, Pallas kernels, call(): pl.pallas_call(kernel, out_shape=shapes, in_specs=specs, out_specs=jax.tr...  15.7 us
    ppermute x4, starting transfers between devices, swap(): return lax.ppermute(x, axis, [(i, i ^ bit) for i in range(SIZE[axis])])  14.9 us
    all_to_all x1, waiting for transfers between devices, gather_latents(): block = lax.all_to_all(copies, axis, 0, 0, tiled=True)  10.8 us
    unnamed x17, local copies, waits for them, and re-layouts  6.37 us
    ppermute x4, waiting for transfers between devices, swap(): return lax.ppermute(x, axis, [(i, i ^ bit) for i in range(SIZE[axis])])  4.92 us
  transfers between devices with their start and end apart: 11, of which 7 were waited for; matrix products, arithmetic and copies ran while one was open for 3% of the time, Pallas kernels for 2%

profile of v3, /device:TPU:112, one launch (start us, length us, event | category | flops | bytes accessed | tf_op | source)
XLA Modules:
  0.0 169.9 jit_solution(10390385377190749434)
XLA Ops:
  0.6 0.8 copy.9
  1.6 27.2 %all_to_all.10 = bf16[8,48,384]{2,1,0:T(8,128)(2,1)S(1)} all-to-all(bf16[8,48,384]{2,1,0:T(8,128)(2,1)S(1)} %broadcast_in_dim.6), channel_id=1, replica_groups=mesh['zh'=4,'y'=4,'core'=2,'section'=4,'mp'=8] {'mp'}, dimensions={0} | all-to-all | bytes 589824 | tf_op jit(solution)/shard_map/all_to_all | solution.py:54
  28.8 1.1 broadcast_in_dim.14
  30.0 4.3 %all-to-all-start.1 = ((bf16[4,384,384]{2,1,0:T(8,128)(2,1)}), bf16[4,384,384]{2,1,0:T(8,128)(2,1)}, u32[]{:S(2)}, u32[]{:S(2)}) async-start(bf16[4,384,384]{2,1,0:T(8,128)(2,1)} %broadcast_in_dim.14), calls=%async_computation.1 | async-start | bytes 2359296 | tf_op jit(solution)/shard_map/all_to_all | solution.py:54
  34.6 2.8 %copy.11 = bf16[192,8,2,512]{3,1,2,0:T(8,128)(2,1)S(1)} copy(bf16[192,8,2,512]{3,2,1,0:T(2,128)(2,1)} %bitcast.61) | data formatting | bytes 6291456
  37.5 10.8 %all-to-all-done.1 = bf16[4,384,384]{2,1,0:T(8,128)(2,1)} async-done(((bf16[4,384,384]{2,1,0:T(8,128)(2,1)}), bf16[4,384,384]{2,1,0:T(8,128)(2,1)}, u32[]{:S(2)}, u32[]{:S(2)}) %all-to-all-start.1) | async-done | bytes 1179680 | tf_op jit(solution)/shard_map/all_to_all | solution.py:54
  48.3 0.9 copy-done.4
  49.2 6.0 %shard_map.85 = (bf16[2,128,512]{2,1,0:T(8,128)(2,1)}, bf16[384,1024]{1,0:T(8,128)(2,1)S(1)}) custom-call(s32[2]{0:T(128)S(1)} %copy-done.6, bf16[1536,384]{1,0:T(8,128)(2,1)} %bitcast.2.lat, bf16[1536,1024]{1,0:T(8,128)(2,1)S(1)} %bitcast.54, bf16[2,128,512]{2,1,0:T(8,128)(2,1)S(1)} %bitcast.58, bf16[2,128,512]{2,1,0:T(8,128)(2,1)S(1)} %bitcast.59, ...), custom_call_target="tpu_custom_call" | custom-call | flops 1207959552 | bytes 4850696 | tf_op jit(solution)/shard_map/pallas_call | solution.py:103
  55.3 2.4 %shard_map.87 = bf16[2,384,384]{2,1,0:T(8,128)(2,1)} custom-call(s32[2]{0:T(128)S(1)} %pad_add_fusion.order, s32[8]{0:T(128)S(1)} %fusion.9.place, bf16[1536,1024]{1,0:T(8,128)(2,1)S(1)} %bitcast.55, bf16[384,1024]{1,0:T(8,128)(2,1)S(1)} %get-tuple-element.15.dflat), custom_call_target="tpu_custom_call" | custom-call | flops 603979776 | bytes 3932200 | tf_op jit(solution)/shard_map/pallas_call | solution.py:103
  57.7 3.4 %shard_map.88 = bf16[768,1024]{1,0:T(8,128)(2,1)} custom-call(s32[16]{0:T(128)S(1)} %add.127.blocks, bf16[1536,384]{1,0:T(8,128)(2,1)} %bitcast.2.lat, bf16[384,1024]{1,0:T(8,128)(2,1)S(1)} %get-tuple-element.15.dflat), custom_call_target="tpu_custom_call" | custom-call | flops 603979776 | bytes 1966144 | tf_op jit(solution)/shard_map/pallas_call | solution.py:103
  61.1 1.9 %collective-permute-start = (bf16[4,4,48,1024]{3,2,1,0:T(8,128)(2,1)}, bf16[4,4,48,1024]{3,2,1,0:T(8,128)(2,1)}, u32[]{:S(2)}, u32[]{:S(2)}) collective-permute-start(bf16[4,4,48,1024]{3,2,1,0:T(8,128)(2,1)} %bitcast.18), channel_id=1, source_target_pairs={{0,32},{32,0},{1,33},{33,1},{2,34},{34,2},{3,35},{35,3},{4,36},{36... | collective-permute-start | bytes 4718600 | tf_op jit(solution)/shard_map/ppermute | solution.py:47
  63.0 2.5 %collective-permute-start.1 = (bf16[2,384,384]{2,1,0:T(8,128)(2,1)}, bf16[2,384,384]{2,1,0:T(8,128)(2,1)}, u32[]{:S(2)}, u32[]{:S(2)}) collective-permute-start(bf16[2,384,384]{2,1,0:T(8,128)(2,1)} %shard_map.87), channel_id=1, source_target_pairs={{0,8},{8,0},{16,24},{24,16},{32,56},{40,48},{48,40},{56,32},{1,9},... | collective-permute-start | bytes 1769480 | tf_op jit(solution)/shard_map/ppermute | solution.py:43
  65.7 1.1 copy-done.1
  66.8 1.5 shard_map.89
  68.3 2.3 %shard_map.86 = f32[768,1024]{1,0:T(8,128)S(1)} custom-call(s32[16]{0:T(128)S(1)} %add.122.blocks, bf16[1536,384]{1,0:T(8,128)(2,1)} %bitcast.2.lat, bf16[384,1024]{1,0:T(8,128)(2,1)S(1)} %copy-done.2), custom_call_target="tpu_custom_call" | custom-call | flops 603979776 | bytes 1966144 | tf_op jit(solution)/shard_map/pallas_call | solution.py:103
  70.6 4.5 %collective-permute-done.1 = bf16[2,384,384]{2,1,0:T(8,128)(2,1)} collective-permute-done((bf16[2,384,384]{2,1,0:T(8,128)(2,1)}, bf16[2,384,384]{2,1,0:T(8,128)(2,1)}, u32[]{:S(2)}, u32[]{:S(2)}) %collective-permute-start.1) | collective-permute-done | bytes 589856 | tf_op jit(solution)/shard_map/ppermute | solution.py:43
  75.1 1.2 convert_add_fusion.2
  76.3 1.9 %convert_add_fusion = f32[4,4,48,1024]{3,2,1,0:T(8,128)S(1)} fusion(f32[4,4,48,1024]{3,2,1,0:T(8,128)S(1)} %bitcast.57, bf16[4,4,48,1024]{3,2,1,0:T(8,128)(2,1)} %collective-permute-done), kind=kLoop, calls=%fused_computation | loop fusion | flops 1572864 | bytes 7864320 | tf_op jit(solution)/shard_map/add | solution.py:177
  78.4 3.2 %collective-permute-start.2 = (bf16[2,4,48,1024]{3,2,1,0:T(8,128)(2,1)S(1)}, bf16[2,4,48,1024]{3,2,1,0:T(8,128)(2,1)S(1)}, u32[]{:S(2)}, u32[]{:S(2)}) collective-permute-start(bf16[2,4,48,1024]{3,2,1,0:T(8,128)(2,1)S(1)} %slice.120), channel_id=1, source_target_pairs={{0,64},{32,224},{64,0},{96,160},{128,192},{160,96},{192,128},{224,... | collective-permute-start | bytes 2359304 | tf_op jit(solution)/shard_map/ppermute | solution.py:43
  81.6 3.1 %collective-permute-start.3 = (bf16[384,384]{1,0:T(8,128)(2,1)S(1)}, bf16[384,384]{1,0:T(8,128)(2,1)S(1)}, u32[]{:S(2)}, u32[]{:S(2)}) collective-permute-start(bf16[384,384]{1,0:T(8,128)(2,1)S(1)} %fusion.1), channel_id=1, source_target_pairs={{0,24},{8,16},{16,8},{24,0},{32,40},{40,32},{48,56},{56,48},{1,25}... | collective-permute-start | bytes 884744 | tf_op jit(solution)/shard_map/ppermute | solution.py:43
  84.7 6.7 %collective-permute-done.3 = bf16[384,384]{1,0:T(8,128)(2,1)S(1)} collective-permute-done((bf16[384,384]{1,0:T(8,128)(2,1)S(1)}, bf16[384,384]{1,0:T(8,128)(2,1)S(1)}, u32[]{:S(2)}, u32[]{:S(2)}) %collective-permute-start.3) | collective-permute-done | bytes 294944 | tf_op jit(solution)/shard_map/ppermute | solution.py:43
  91.5 0.7 collective-permute-done.2
  92.5 2.4 %collective-permute-start.4 = (bf16[4,48,1024]{2,1,0:T(8,128)(2,1)S(1)}, bf16[4,48,1024]{2,1,0:T(8,128)(2,1)S(1)}, u32[]{:S(2)}, u32[]{:S(2)}) collective-permute-start(bf16[4,48,1024]{2,1,0:T(8,128)(2,1)S(1)} %fusion), channel_id=1, source_target_pairs={{0,192},{32,96},{64,128},{96,32},{128,64},{160,224},{192,0},{224,1... | collective-permute-start | bytes 1179656 | tf_op jit(solution)/shard_map/ppermute | solution.py:43
  94.9 3.5 %collective-permute-start.5 = (bf16[4,48,384]{2,1,0:T(8,128)(2,1)S(1)}, bf16[4,48,384]{2,1,0:T(8,128)(2,1)S(1)}, u32[]{:S(2)}, u32[]{:S(2)}) collective-permute-start(bf16[4,48,384]{2,1,0:T(8,128)(2,1)S(1)} %bitcast.64), channel_id=1, source_target_pairs={{0,1},{1,0},{2,3},{3,2},{4,5},{5,4},{6,7},{7,6},{8,9},{9,8},{10,11... | collective-permute-start | bytes 442376 | tf_op jit(solution)/shard_map/ppermute | solution.py:47
  98.4 4.9 %collective-permute-done.5 = bf16[4,48,384]{2,1,0:T(8,128)(2,1)S(1)} collective-permute-done((bf16[4,48,384]{2,1,0:T(8,128)(2,1)S(1)}, bf16[4,48,384]{2,1,0:T(8,128)(2,1)S(1)}, u32[]{:S(2)}, u32[]{:S(2)}) %collective-permute-start.5) | collective-permute-done | bytes 147488 | tf_op jit(solution)/shard_map/ppermute | solution.py:47
  103.5 5.9 %collective-permute-start.8 = (bf16[2,48,384]{2,1,0:T(8,128)(2,1)S(1)}, bf16[2,48,384]{2,1,0:T(8,128)(2,1)S(1)}, u32[]{:S(2)}, u32[]{:S(2)}) collective-permute-start(bf16[2,48,384]{2,1,0:T(8,128)(2,1)S(1)} %slice.123), channel_id=1, source_target_pairs={{0,2},{1,3},{2,0},{3,1},{4,6},{5,7},{6,4},{7,5},{8,10},{9,11},{10,... | collective-permute-start | bytes 221192 | tf_op jit(solution)/shard_map/ppermute | solution.py:47
  109.4 15.5 %collective-permute-start.6 = (bf16[2,48,1024]{2,1,0:T(8,128)(2,1)S(1)}, bf16[2,48,1024]{2,1,0:T(8,128)(2,1)S(1)}, u32[]{:S(2)}, u32[]{:S(2)}) collective-permute-start(bf16[2,48,1024]{2,1,0:T(8,128)(2,1)S(1)} %slice.121), channel_id=1, source_target_pairs={{0,256},{1,769},{2,258},{3,771},{4,260},{5,773},{6,262},{7,775},{2... | collective-permute-start | bytes 589832 | tf_op jit(solution)/shard_map/ppermute | solution.py:43
  125.0 3.7 %collective-permute-start.9 = (bf16[48,384]{1,0:T(8,128)(2,1)S(1)}, bf16[48,384]{1,0:T(8,128)(2,1)S(1)}, u32[]{:S(2)}, u32[]{:S(2)}) collective-permute-start(bf16[48,384]{1,0:T(8,128)(2,1)S(1)} %fusion.6), channel_id=1, source_target_pairs={{0,4},{1,5},{2,6},{3,7},{4,0},{5,1},{6,2},{7,3},{8,12},{9,13},{10,... | collective-permute-start | bytes 110600 | tf_op jit(solution)/shard_map/ppermute | solution.py:47
  128.7 14.6 %collective-permute-done.6 = bf16[2,48,1024]{2,1,0:T(8,128)(2,1)S(1)} collective-permute-done((bf16[2,48,1024]{2,1,0:T(8,128)(2,1)S(1)}, bf16[2,48,1024]{2,1,0:T(8,128)(2,1)S(1)}, u32[]{:S(2)}, u32[]{:S(2)}) %collective-permute-start.6) | collective-permute-done | bytes 196640 | tf_op jit(solution)/shard_map/ppermute | solution.py:43
  143.4 16.3 %collective-permute-start.7 = (bf16[48,1024]{1,0:T(8,128)(2,1)S(1)}, bf16[48,1024]{1,0:T(8,128)(2,1)S(1)}, u32[]{:S(2)}, u32[]{:S(2)}) collective-permute-start(bf16[48,1024]{1,0:T(8,128)(2,1)S(1)} %fusion.3), channel_id=1, source_target_pairs={{0,768},{1,257},{2,770},{3,259},{4,772},{5,261},{6,774},{7,263},{2... | collective-permute-start | bytes 294920 | tf_op jit(solution)/shard_map/ppermute | solution.py:43
  160.5 8.6 %collective-permute-done.7 = bf16[48,1024]{1,0:T(8,128)(2,1)S(1)} collective-permute-done((bf16[48,1024]{1,0:T(8,128)(2,1)S(1)}, bf16[48,1024]{1,0:T(8,128)(2,1)S(1)}, u32[]{:S(2)}, u32[]{:S(2)}) %collective-permute-start.7) | collective-permute-done | bytes 98336 | tf_op jit(solution)/shard_map/ppermute | solution.py:43
  169.1 0.8 reshape.162
  (45 shorter events, 2.4 us)
Async XLA Ops:
  30.0 18.3 %all-to-all-start.1 = ((bf16[4,384,384]{2,1,0:T(8,128)(2,1)}), bf16[4,384,384]{2,1,0:T(8,128)(2,1)}, u32[]{:S(2)}, u32[]{:S(2)}) async-start(bf16[4,384,384]{2,1,0:T(8,128)(2,1)} %broadcast_in_dim.14), calls=%async_computation.1 | async-start | bytes 2359296 | tf_op jit(solution)/shard_map/all_to_all | solution.py:54
  34.6 13.7 %copy-start.3 = (bf16[1,2,128,512]{3,2,1,0:T(8,128)(2,1)S(1)}, bf16[1,2,128,512]{3,2,1,0:T(8,128)(2,1)}, u32[]{:S(2)}) copy-start(bf16[1,2,128,512]{3,2,1,0:T(8,128)(2,1)} %param.6) | copy-start | bytes 786436
  34.6 13.7 %copy-start.5 = (s32[2,128]{1,0:T(2,128)S(1)}, s32[2,128]{1,0:T(2,128)}, u32[]{:S(2)}) copy-start(s32[2,128]{1,0:T(2,128)} %param.9) | copy-start | bytes 3076
  34.6 13.7 %copy-start.6 = (s32[2]{0:T(128)S(1)}, s32[2]{0:T(128)}, u32[]{:S(2)}) copy-start(s32[2]{0:T(128)} %counts.1) | copy-start | bytes 28
  48.3 1.0 copy-start.4
  55.3 2.4 %copy-start = (bf16[384,1024]{1,0:T(8,128)(2,1)}, bf16[384,1024]{1,0:T(8,128)(2,1)S(1)}, u32[]{:S(2)}) copy-start(bf16[384,1024]{1,0:T(8,128)(2,1)S(1)} %get-tuple-element.15.dflat) | copy-start | bytes 2359300
  61.1 15.2 %collective-permute-start = (bf16[4,4,48,1024]{3,2,1,0:T(8,128)(2,1)}, bf16[4,4,48,1024]{3,2,1,0:T(8,128)(2,1)}, u32[]{:S(2)}, u32[]{:S(2)}) collective-permute-start(bf16[4,4,48,1024]{3,2,1,0:T(8,128)(2,1)} %bitcast.18), channel_id=1, source_target_pairs={{0,32},{32,0},{1,33},{33,1},{2,34},{34,2},{3,35},{35,3},{4,36},{36... | collective-permute-start | bytes 4718600 | tf_op jit(solution)/shard_map/ppermute | solution.py:47
  63.0 12.1 %collective-permute-start.1 = (bf16[2,384,384]{2,1,0:T(8,128)(2,1)}, bf16[2,384,384]{2,1,0:T(8,128)(2,1)}, u32[]{:S(2)}, u32[]{:S(2)}) collective-permute-start(bf16[2,384,384]{2,1,0:T(8,128)(2,1)} %shard_map.87), channel_id=1, source_target_pairs={{0,8},{8,0},{16,24},{24,16},{32,56},{40,48},{48,40},{56,32},{1,9},... | collective-permute-start | bytes 1769480 | tf_op jit(solution)/shard_map/ppermute | solution.py:43
  65.7 1.1 copy-start.1
  66.8 1.5 copy-start.2
  78.4 13.9 %collective-permute-start.2 = (bf16[2,4,48,1024]{3,2,1,0:T(8,128)(2,1)S(1)}, bf16[2,4,48,1024]{3,2,1,0:T(8,128)(2,1)S(1)}, u32[]{:S(2)}, u32[]{:S(2)}) collective-permute-start(bf16[2,4,48,1024]{3,2,1,0:T(8,128)(2,1)S(1)} %slice.120), channel_id=1, source_target_pairs={{0,64},{32,224},{64,0},{96,160},{128,192},{160,96},{192,128},{224,... | collective-permute-start | bytes 2359304 | tf_op jit(solution)/shard_map/ppermute | solution.py:43
  81.6 9.8 %collective-permute-start.3 = (bf16[384,384]{1,0:T(8,128)(2,1)S(1)}, bf16[384,384]{1,0:T(8,128)(2,1)S(1)}, u32[]{:S(2)}, u32[]{:S(2)}) collective-permute-start(bf16[384,384]{1,0:T(8,128)(2,1)S(1)} %fusion.1), channel_id=1, source_target_pairs={{0,24},{8,16},{16,8},{24,0},{32,40},{40,32},{48,56},{56,48},{1,25}... | collective-permute-start | bytes 884744 | tf_op jit(solution)/shard_map/ppermute | solution.py:43
  92.5 10.8 %collective-permute-start.4 = (bf16[4,48,1024]{2,1,0:T(8,128)(2,1)S(1)}, bf16[4,48,1024]{2,1,0:T(8,128)(2,1)S(1)}, u32[]{:S(2)}, u32[]{:S(2)}) collective-permute-start(bf16[4,48,1024]{2,1,0:T(8,128)(2,1)S(1)} %fusion), channel_id=1, source_target_pairs={{0,192},{32,96},{64,128},{96,32},{128,64},{160,224},{192,0},{224,1... | collective-permute-start | bytes 1179656 | tf_op jit(solution)/shard_map/ppermute | solution.py:43
  94.9 8.4 %collective-permute-start.5 = (bf16[4,48,384]{2,1,0:T(8,128)(2,1)S(1)}, bf16[4,48,384]{2,1,0:T(8,128)(2,1)S(1)}, u32[]{:S(2)}, u32[]{:S(2)}) collective-permute-start(bf16[4,48,384]{2,1,0:T(8,128)(2,1)S(1)} %bitcast.64), channel_id=1, source_target_pairs={{0,1},{1,0},{2,3},{3,2},{4,5},{5,4},{6,7},{7,6},{8,9},{9,8},{10,11... | collective-permute-start | bytes 442376 | tf_op jit(solution)/shard_map/ppermute | solution.py:47
  103.5 21.4 %collective-permute-start.8 = (bf16[2,48,384]{2,1,0:T(8,128)(2,1)S(1)}, bf16[2,48,384]{2,1,0:T(8,128)(2,1)S(1)}, u32[]{:S(2)}, u32[]{:S(2)}) collective-permute-start(bf16[2,48,384]{2,1,0:T(8,128)(2,1)S(1)} %slice.123), channel_id=1, source_target_pairs={{0,2},{1,3},{2,0},{3,1},{4,6},{5,7},{6,4},{7,5},{8,10},{9,11},{10,... | collective-permute-start | bytes 221192 | tf_op jit(solution)/shard_map/ppermute | solution.py:47
  109.4 33.9 %collective-permute-start.6 = (bf16[2,48,1024]{2,1,0:T(8,128)(2,1)S(1)}, bf16[2,48,1024]{2,1,0:T(8,128)(2,1)S(1)}, u32[]{:S(2)}, u32[]{:S(2)}) collective-permute-start(bf16[2,48,1024]{2,1,0:T(8,128)(2,1)S(1)} %slice.121), channel_id=1, source_target_pairs={{0,256},{1,769},{2,258},{3,771},{4,260},{5,773},{6,262},{7,775},{2... | collective-permute-start | bytes 589832 | tf_op jit(solution)/shard_map/ppermute | solution.py:43
  125.0 34.7 %collective-permute-start.9 = (bf16[48,384]{1,0:T(8,128)(2,1)S(1)}, bf16[48,384]{1,0:T(8,128)(2,1)S(1)}, u32[]{:S(2)}, u32[]{:S(2)}) collective-permute-start(bf16[48,384]{1,0:T(8,128)(2,1)S(1)} %fusion.6), channel_id=1, source_target_pairs={{0,4},{1,5},{2,6},{3,7},{4,0},{5,1},{6,2},{7,3},{8,12},{9,13},{10,... | collective-permute-start | bytes 110600 | tf_op jit(solution)/shard_map/ppermute | solution.py:47
  143.4 25.7 %collective-permute-start.7 = (bf16[48,1024]{1,0:T(8,128)(2,1)S(1)}, bf16[48,1024]{1,0:T(8,128)(2,1)S(1)}, u32[]{:S(2)}, u32[]{:S(2)}) collective-permute-start(bf16[48,1024]{1,0:T(8,128)(2,1)S(1)} %fusion.3), channel_id=1, source_target_pairs={{0,768},{1,257},{2,770},{3,259},{4,772},{5,261},{6,774},{7,263},{2... | collective-permute-start | bytes 294920 | tf_op jit(solution)/shard_map/ppermute | solution.py:43

commit v4 on v3

--- a/solution.py
+++ b/solution.py
@@ -81,21 +81,33 @@
             dflat[rows, high] = dot(prob_bf, g).astype(bf16)
 
 
-def latent_kernel(depth, order, place, weight, dflat, out):
-    chunk = out.shape[1]
-    for i in range(out.shape[0]):
-        start = pl.multiple_of(order[i] * chunk, 128)
-        term = dot(weight[pl.ds(start, chunk), :], dflat[...], TRANS_B).astype(out.dtype)
-        for m in range(chunk // depth):
-            at = pl.multiple_of(place[m] * depth, 16)
-            out[i, pl.ds(at, depth), :] = term[m * depth : (m + 1) * depth]
-
-
-def weight_kernel(depth, blocks, lat, dflat, out, picked):
+def latent_kernel(weight, dflat, after, out):
+    out[...] = dot(weight[...], dflat[...], TRANS_B).astype(bf16)
+
+
+def pick_blocks(depth, blocks, lat, picked):
     for i in range(picked.shape[0] // depth):
         start = pl.multiple_of(blocks[i] * depth, 16)
         picked[i * depth : (i + 1) * depth, :] = lat[pl.ds(start, depth), :]
-    out[...] = dot(picked[...], dflat[...]).astype(out.dtype)
+
+
+def send_kernel(depth, blocks, lat, dflat, out, picked):
+    pick_blocks(depth, blocks, lat, picked)
+    out[...] = dot(picked[...], dflat[...]).astype(bf16)
+
+
+def keep_kernel(depth, blocks, lat, dflat, other, keep, send, picked):
+    pick_blocks(depth, blocks, lat, picked)
+    half = keep.shape[0]
+    keep[...] = dot(picked[:half], dflat[...]) + other[:half].astype(f32)
+    send[...] = (dot(picked[half:], dflat[...]) + other[half:].astype(f32)).astype(bf16)
+
+
+def sum_kernel(parts, after, out):
+    total = parts[0].astype(f32)
+    for i in range(1, parts.shape[0]):
+        total += parts[i].astype(f32)
+    out[...] = total.astype(bf16)
 
 
 def call(kernel, specs, shapes, scratch, flops, *args):
@@ -106,7 +118,7 @@
         in_specs=specs,
         out_specs=jax.tree.map(lambda _: VMEM, shapes),
         scratch_shapes=scratch,
-        compiler_params=pltpu.CompilerParams(vmem_limit_bytes=40 << 20),
+        compiler_params=pltpu.CompilerParams(vmem_limit_bytes=16 << 20),
         cost_estimate=pl.CostEstimate(flops=flops, bytes_accessed=size, transcendentals=0),
     )(*args)
 
@@ -116,7 +128,7 @@
     rows = samples * keys
     _, width, _, local = kv_weight.shape
     weight = kv_weight.reshape(width, 2 * local)
-    core, mp = lax.axis_index("core"), lax.axis_index("mp")
+    core = lax.axis_index("core")
     lat = gather_latents(latents.reshape(rows, depth).T)
 
     attended, dflat = call(
@@ -136,60 +148,65 @@
         token_image.reshape(samples, 1, -1),
     )
 
-    to = jnp.arange(8, dtype=jnp.int32) ^ mp
-    place = (to % 2) * 4 + (to // 2 % 2) * 2 + to // 4
-    order = jnp.stack(relative("section")).astype(jnp.int32)
-
-    def latent_terms(sections, dtype):
-        return call(
-            functools.partial(latent_kernel, depth),
-            [SMEM, SMEM, VMEM, VMEM],
-            jax.ShapeDtypeStruct((2, width // 4, rows), dtype),
-            [],
-            width * rows * 2 * local,
-            sections,
-            place,
-            weight,
-            dflat,
-        )
-
-    def weight_terms(at_core, ys, dtype, dflat):
-        zs = jnp.stack(relative("zh"))
-        blocks = (zs[None, :] * 8 + jnp.stack(ys)[:, None] * 2 + at_core).reshape(-1)
-        return call(
-            functools.partial(weight_kernel, depth),
-            [SMEM, VMEM, VMEM],
-            jax.ShapeDtypeStruct((width // 2, 2 * local), dtype),
-            [pltpu.VMEM((width // 2, rows), bf16)],
-            width * rows * 2 * local,
-            blocks.astype(jnp.int32),
-            lat,
-            dflat,
-        ).reshape(4, 4, depth, 2 * local)
+    half, cols = width // 4, 2 * local
+    zs = jnp.stack(relative("zh"))
+
+    def blocks(at_core, ys):
+        return (zs[None, :] * 8 + jnp.stack(ys)[:, None] * 2 + at_core).reshape(-1).astype(jnp.int32)
 
     mine, second, first, both = relative("y")
-    lat_send = latent_terms(order[2:], bf16)
-    lat_send, dflat_next = lax.optimization_barrier((lat_send, dflat))
-    grad_send = weight_terms(1 - core, [mine, first, second, both], bf16, dflat_next)
-    lat_keep = latent_terms(order[:2], f32)
-    grad_keep = weight_terms(core, [mine, second, first, both], f32, dflat)
-
-    grad = grad_keep + swap(grad_send, "core", 1).astype(f32)
-    lat_sum = lat_keep + paired(lat_send, "section", True).astype(f32)
+    picked = [pltpu.VMEM((2 * half, rows), bf16)]
+    grad_send = call(
+        functools.partial(send_kernel, depth),
+        [SMEM, VMEM, VMEM],
+        jax.ShapeDtypeStruct((2 * half, cols), bf16),
+        picked,
+        width * rows * cols,
+        blocks(1 - core, [mine, first, second, both]),
+        lat,
+        dflat,
+    )
+    lat_term = call(
+        latent_kernel,
+        [VMEM, VMEM, pl.BlockSpec(memory_space=pl.ANY)],
+        jax.ShapeDtypeStruct((width, rows), bf16),
+        [],
+        2 * width * rows * cols,
+        weight,
+        dflat,
+        grad_send,
+    )
+    keep, send = call(
+        functools.partial(keep_kernel, depth),
+        [SMEM, VMEM, VMEM, VMEM],
+        (jax.ShapeDtypeStruct((half, cols), f32), jax.ShapeDtypeStruct((half, cols), bf16)),
+        picked,
+        width * rows * cols,
+        blocks(core, [mine, second, first, both]),
+        lat,
+        dflat,
+        swap(grad_send, "core", 1),
+    )
+
+    lat_parts = lax.all_to_all(lat_term.reshape(4, half, rows), "section", 0, 0, tiled=True)
+    lat_sum = call(
+        sum_kernel,
+        [VMEM, pl.BlockSpec(memory_space=pl.ANY)],
+        jax.ShapeDtypeStruct((half, rows), bf16),
+        [],
+        4 * half * rows,
+        lat_parts,
+        send,
+    )
+    lat_parts = lax.all_to_all(lat_sum.reshape(8, depth, rows), "mp", 0, 0, tiled=True)
+
+    grad = (keep + paired(send, "y", True).astype(f32)).reshape(2, -1, cols)
+    grad = grad[0] + paired(grad[1].astype(bf16), "y", False).astype(f32)
+    grad = grad.reshape(2, -1, cols)
+    grad = grad[0] + paired(grad[1].astype(bf16), "zh", True).astype(f32)
+    lat_sum = jnp.sum(lat_parts.astype(f32), axis=0)
     grad, lat_sum = lax.optimization_barrier((grad, lat_sum))
-
-    grad = grad[:2] + paired(grad[2:].astype(bf16), "y", True).astype(f32)
-    lat_sum = lat_sum[0] + paired(lat_sum[1].astype(bf16), "section", False).astype(f32)
-    grad, lat_sum = lax.optimization_barrier((grad, lat_sum))
-
-    grad = grad[0] + paired(grad[1].astype(bf16), "y", False).astype(f32)
-    lat_sum = lat_sum.reshape(8, depth, rows)
-    lat_sum = lat_sum[:4] + swap(lat_sum[4:].astype(bf16), "mp", 1).astype(f32)
-    grad, lat_sum = lax.optimization_barrier((grad, lat_sum))
-
-    grad = grad[:2] + paired(grad[2:].astype(bf16), "zh", True).astype(f32)
-    lat_sum = lat_sum[:2] + swap(lat_sum[2:].astype(bf16), "mp", 2).astype(f32)
-    lat_sum = lat_sum[0] + swap(lat_sum[1].astype(bf16), "mp", 4).astype(f32)
+    grad = grad.reshape(2, -1, cols)
     kv_grad = grad[0] + paired(grad[1].astype(bf16), "zh", False).astype(f32)
     return (
         attended[None],

time: 171 us -> 165 us (0.965)
  the two profiles are of different devices: /device:TPU:112 before, /device:TPU:9 now
where the time goes in v4:
time: 165 us; the launch traced here: 164 us
  waiting for transfers between devices  65.4 us (40%)
  starting transfers between devices  43.8 us (27%)
  blocking collectives  28.4 us (17%)
  Pallas kernels  16.1 us (10%)
  local copies, waits for them, and re-layouts  8.79 us (5%)
    ppermute x4, waiting for transfers between devices, paired(): return lax.ppermute(x, axes, pairs)  46.1 us
    all_to_all x1, blocking collectives, gather_latents(): block = lax.all_to_all(copies, axis, 0, 0, tiled=True)  28.4 us
    ppermute x4, starting transfers between devices, paired(): return lax.ppermute(x, axes, pairs)  22.5 us
    pallas_call x5, Pallas kernels, call(): pl.pallas_call(kernel, out_shape=shapes, in_specs=specs, out_specs=jax.tr...  16.1 us
    all_to_all x1, waiting for transfers between devices, body(): lax.all_to_all(lat_term.reshape(4, half, rows), 'section', 0, 0, tiled=True)  9.68 us
    all_to_all x1, waiting for transfers between devices, gather_latents(): block = lax.all_to_all(copies, axis, 0, 0, tiled=True)  9.55 us
    ppermute x1, starting transfers between devices, swap(): return lax.ppermute(x, axis, [(i, i ^ bit) for i in range(SIZE[axis])])  6.73 us
    all_to_all x1, starting transfers between devices, body(): lax.all_to_all(lat_sum.reshape(8, depth, rows), 'mp', 0, 0, tiled=True)  6.69 us
  transfers between devices with their start and end apart: 8, of which 5 were waited for; matrix products, arithmetic and copies ran while one was open for 3% of the time, Pallas kernels for 4%

profile of v4, /device:TPU:9, one launch (start us, length us, event | category | flops | bytes accessed | tf_op | source)
XLA Modules:
  0.0 164.0 jit_solution(13349835092990165563)
XLA Ops:
  0.6 0.8 copy.9
  1.5 0.1 reshape.162
  1.6 28.4 %all_to_all.20 = bf16[8,48,384]{2,1,0:T(8,128)(2,1)S(1)} all-to-all(bf16[8,48,384]{2,1,0:T(8,128)(2,1)S(1)} %broadcast_in_dim.6), channel_id=1, replica_groups=mesh['zh'=4,'y'=4,'core'=2,'section'=4,'mp'=8] {'mp'}, dimensions={0} | all-to-all | bytes 589824 | tf_op jit(solution)/shard_map/all_to_all | solution.py:54
  30.0 1.2 broadcast_in_dim.14
  31.1 4.3 %all-to-all-start.1 = ((bf16[4,384,384]{2,1,0:T(8,128)(2,1)}), bf16[4,384,384]{2,1,0:T(8,128)(2,1)}, u32[]{:S(2)}, u32[]{:S(2)}) async-start(bf16[4,384,384]{2,1,0:T(8,128)(2,1)} %broadcast_in_dim.14), calls=%async_computation.1 | async-start | bytes 2359296 | tf_op jit(solution)/shard_map/all_to_all | solution.py:54
  35.7 0.1 add.87.blocks
  35.8 2.8 %copy.11 = bf16[192,8,2,512]{3,1,2,0:T(8,128)(2,1)S(1)} copy(bf16[192,8,2,512]{3,2,1,0:T(2,128)(2,1)} %bitcast.31) | data formatting | bytes 6291456
  38.6 9.5 %all-to-all-done.1 = bf16[4,384,384]{2,1,0:T(8,128)(2,1)} async-done(((bf16[4,384,384]{2,1,0:T(8,128)(2,1)}), bf16[4,384,384]{2,1,0:T(8,128)(2,1)}, u32[]{:S(2)}, u32[]{:S(2)}) %all-to-all-start.1) | async-done | bytes 1179680 | tf_op jit(solution)/shard_map/all_to_all | solution.py:54
  48.1 0.9 copy-done.4
  49.1 6.1 %shard_map.85 = (bf16[2,128,512]{2,1,0:T(8,128)(2,1)}, bf16[384,1024]{1,0:T(8,128)(2,1)S(1)}) custom-call(s32[2]{0:T(128)S(1)} %copy-done.6, bf16[1536,384]{1,0:T(8,128)(2,1)} %bitcast.2.lat, bf16[1536,1024]{1,0:T(8,128)(2,1)S(1)} %bitcast.25, bf16[2,128,512]{2,1,0:T(8,128)(2,1)S(1)} %bitcast.28, bf16[2,128,512]{2,1,0:T(8,128)(2,1)S(1)} %bitcast.29, ...), custom_call_target="tpu_custom_call" | custom-call | flops 1207959552 | bytes 4850696 | tf_op jit(solution)/shard_map/pallas_call | solution.py:115
  55.1 3.7 %shard_map.86.after = bf16[768,1024]{1,0:T(8,128)(2,1)} custom-call(s32[16]{0:T(128)S(1)} %add.87.blocks, bf16[1536,384]{1,0:T(8,128)(2,1)} %bitcast.2.lat, bf16[384,1024]{1,0:T(8,128)(2,1)S(1)} %get-tuple-element.10.dflat), custom_call_target="tpu_custom_call" | custom-call | flops 603979776 | bytes 1966144 | tf_op jit(solution)/shard_map/pallas_call | solution.py:115
  58.8 6.7 %collective-permute-start = (bf16[768,1024]{1,0:T(8,128)(2,1)}, bf16[768,1024]{1,0:T(8,128)(2,1)}, u32[]{:S(2)}, u32[]{:S(2)}) collective-permute-start(bf16[768,1024]{1,0:T(8,128)(2,1)} %shard_map.86.after), channel_id=1, source_target_pairs={{0,32},{32,0},{1,33},{33,1},{2,34},{34,2},{3,35},{35,3},{4,36},{36... | collective-permute-start | bytes 4718600 | tf_op jit(solution)/shard_map/ppermute | solution.py:47
  65.5 1.8 %shard_map.88 = bf16[1536,384]{1,0:T(8,128)(2,1)S(1)} custom-call(bf16[1536,1024]{1,0:T(8,128)(2,1)S(1)} %bitcast.26, bf16[384,1024]{1,0:T(8,128)(2,1)S(1)} %get-tuple-element.10.dflat, bf16[768,1024]{1,0:T(8,128)(2,1)} %shard_map.86.after), custom_call_target="tpu_custom_call" | custom-call | flops 1207959552 | bytes 5505024 | tf_op jit(solution)/shard_map/pallas_call | solution.py:115
  67.4 1.1 copy-done.2
  68.5 3.7 %all-to-all-start.2 = ((bf16[4,384,384]{2,1,0:T(8,128)(2,1)}), bf16[4,384,384]{2,1,0:T(8,128)(2,1)S(1)}, u32[]{:S(2)}, u32[]{:S(2)}) async-start(bf16[4,384,384]{2,1,0:T(8,128)(2,1)} %bitcast.27), calls=%async_computation.2 | async-start | bytes 2359296 | tf_op jit(solution)/shard_map/all_to_all | solution.py:191
  72.1 0.1 add.82.blocks
  72.2 3.7 %shard_map.87 = (f32[384,1024]{1,0:T(8,128)S(1)}, bf16[384,1024]{1,0:T(8,128)(2,1)}) custom-call(s32[16]{0:T(128)S(1)} %add.82.blocks, bf16[1536,384]{1,0:T(8,128)(2,1)} %bitcast.2.lat, bf16[384,1024]{1,0:T(8,128)(2,1)S(1)} %copy-done.1, bf16[768,1024]{1,0:T(8,128)(2,1)} %collective-permute-done.other), custom_call_target="tpu_custom_call" | custom-call | flops 603979776 | bytes 3539008 | tf_op jit(solution)/shard_map/pallas_call | solution.py:115
  75.9 3.2 %collective-permute-start.1 = (bf16[384,1024]{1,0:T(8,128)(2,1)}, bf16[384,1024]{1,0:T(8,128)(2,1)S(1)}, u32[]{:S(2)}, u32[]{:S(2)}) collective-permute-start(bf16[384,1024]{1,0:T(8,128)(2,1)} %get-tuple-element.12.after), channel_id=1, source_target_pairs={{0,64},{32,224},{64,0},{96,160},{128,192},{160,96},{192,128},{224,... | collective-permute-start | bytes 2359304 | tf_op jit(solution)/shard_map/ppermute | solution.py:43
  79.1 9.7 %all-to-all-done.2.parts = bf16[4,384,384]{2,1,0:T(8,128)(2,1)S(1)} async-done(((bf16[4,384,384]{2,1,0:T(8,128)(2,1)}), bf16[4,384,384]{2,1,0:T(8,128)(2,1)S(1)}, u32[]{:S(2)}, u32[]{:S(2)}) %all-to-all-start.2) | async-done | bytes 1179680 | tf_op jit(solution)/shard_map/all_to_all | solution.py:191
  88.7 0.9 shard_map.89
  89.6 6.7 %all-to-all-start.3 = ((bf16[8,48,384]{2,1,0:T(8,128)(2,1)}), bf16[8,48,384]{2,1,0:T(8,128)(2,1)S(1)}, u32[]{:S(2)}, u32[]{:S(2)}) async-start(bf16[8,48,384]{2,1,0:T(8,128)(2,1)} %bitcast.16), calls=%async_computation.3 | async-start | bytes 589824 | tf_op jit(solution)/shard_map/all_to_all | solution.py:201
  96.3 0.2 convert_add_fusion
  96.6 1.9 %collective-permute-start.2 = (bf16[192,1024]{1,0:T(8,128)(2,1)S(1)}, bf16[192,1024]{1,0:T(8,128)(2,1)S(1)}, u32[]{:S(2)}, u32[]{:S(2)}) collective-permute-start(bf16[192,1024]{1,0:T(8,128)(2,1)S(1)} %slice.44), channel_id=1, source_target_pairs={{0,192},{32,96},{64,128},{96,32},{128,64},{160,224},{192,0},{224,1... | collective-permute-start | bytes 1179656 | tf_op jit(solution)/shard_map/ppermute | solution.py:43
  98.5 6.9 %collective-permute-done.2 = bf16[192,1024]{1,0:T(8,128)(2,1)S(1)} collective-permute-done((bf16[192,1024]{1,0:T(8,128)(2,1)S(1)}, bf16[192,1024]{1,0:T(8,128)(2,1)S(1)}, u32[]{:S(2)}, u32[]{:S(2)}) %collective-permute-start.2) | collective-permute-done | bytes 393248 | tf_op jit(solution)/shard_map/ppermute | solution.py:43
  105.4 0.1 slice_add_fusion
  105.6 15.4 %collective-permute-start.3 = (bf16[96,1024]{1,0:T(8,128)(2,1)S(1)}, bf16[96,1024]{1,0:T(8,128)(2,1)S(1)}, u32[]{:S(2)}, u32[]{:S(2)}) collective-permute-start(bf16[96,1024]{1,0:T(8,128)(2,1)S(1)} %slice.45), channel_id=1, source_target_pairs={{0,256},{1,769},{2,258},{3,771},{4,260},{5,773},{6,262},{7,775},{2... | collective-permute-start | bytes 589832 | tf_op jit(solution)/shard_map/ppermute | solution.py:43
  121.0 21.2 %collective-permute-done.3 = bf16[96,1024]{1,0:T(8,128)(2,1)S(1)} collective-permute-done((bf16[96,1024]{1,0:T(8,128)(2,1)S(1)}, bf16[96,1024]{1,0:T(8,128)(2,1)S(1)}, u32[]{:S(2)}, u32[]{:S(2)}) %collective-permute-start.3) | collective-permute-done | bytes 196640 | tf_op jit(solution)/shard_map/ppermute | solution.py:43
  142.4 1.9 %collective-permute-start.4 = (bf16[48,1024]{1,0:T(8,128)(2,1)S(1)}, bf16[48,1024]{1,0:T(8,128)(2,1)S(1)}, u32[]{:S(2)}, u32[]{:S(2)}) collective-permute-start(bf16[48,1024]{1,0:T(8,128)(2,1)S(1)} %slice.46), channel_id=1, source_target_pairs={{0,768},{1,257},{2,770},{3,259},{4,772},{5,261},{6,774},{7,263},{2... | collective-permute-start | bytes 294920 | tf_op jit(solution)/shard_map/ppermute | solution.py:43
  144.3 0.1 reshape.170
  144.4 0.6 copy.10
  145.1 18.0 %collective-permute-done.4 = bf16[48,1024]{1,0:T(8,128)(2,1)S(1)} collective-permute-done((bf16[48,1024]{1,0:T(8,128)(2,1)S(1)}, bf16[48,1024]{1,0:T(8,128)(2,1)S(1)}, u32[]{:S(2)}, u32[]{:S(2)}) %collective-permute-start.4) | collective-permute-done | bytes 98336 | tf_op jit(solution)/shard_map/ppermute | solution.py:43
  163.1 0.8 reshape.169
  (25 shorter events, 0.5 us)
Async XLA Ops:
  31.1 17.0 %all-to-all-start.1 = ((bf16[4,384,384]{2,1,0:T(8,128)(2,1)}), bf16[4,384,384]{2,1,0:T(8,128)(2,1)}, u32[]{:S(2)}, u32[]{:S(2)}) async-start(bf16[4,384,384]{2,1,0:T(8,128)(2,1)} %broadcast_in_dim.14), calls=%async_computation.1 | async-start | bytes 2359296 | tf_op jit(solution)/shard_map/all_to_all | solution.py:54
  35.8 12.3 %copy-start.3 = (bf16[1,2,128,512]{3,2,1,0:T(8,128)(2,1)S(1)}, bf16[1,2,128,512]{3,2,1,0:T(8,128)(2,1)}, u32[]{:S(2)}) copy-start(bf16[1,2,128,512]{3,2,1,0:T(8,128)(2,1)} %param.6) | copy-start | bytes 786436
  35.8 12.3 %copy-start.5 = (s32[2,128]{1,0:T(2,128)S(1)}, s32[2,128]{1,0:T(2,128)}, u32[]{:S(2)}) copy-start(s32[2,128]{1,0:T(2,128)} %param.9) | copy-start | bytes 3076
  35.8 12.4 %copy-start.6 = (s32[2]{0:T(128)S(1)}, s32[2]{0:T(128)}, u32[]{:S(2)}) copy-start(s32[2]{0:T(128)} %counts.1) | copy-start | bytes 28
  48.1 1.0 copy-start.4
  55.1 10.4 %copy-start = (bf16[384,1024]{1,0:T(8,128)(2,1)}, bf16[384,1024]{1,0:T(8,128)(2,1)S(1)}, u32[]{:S(2)}) copy-start(bf16[384,1024]{1,0:T(8,128)(2,1)S(1)} %get-tuple-element.10.dflat) | copy-start | bytes 2359300
  58.8 13.4 %collective-permute-start = (bf16[768,1024]{1,0:T(8,128)(2,1)}, bf16[768,1024]{1,0:T(8,128)(2,1)}, u32[]{:S(2)}, u32[]{:S(2)}) collective-permute-start(bf16[768,1024]{1,0:T(8,128)(2,1)} %shard_map.86.after), channel_id=1, source_target_pairs={{0,32},{32,0},{1,33},{33,1},{2,34},{34,2},{3,35},{35,3},{4,36},{36... | collective-permute-start | bytes 4718600 | tf_op jit(solution)/shard_map/ppermute | solution.py:47
  67.4 1.1 copy-start.2
  68.5 3.8 %copy-start.1 = (bf16[384,1024]{1,0:T(8,128)(2,1)S(1)}, bf16[384,1024]{1,0:T(8,128)(2,1)}, u32[]{:S(2)}) copy-start(bf16[384,1024]{1,0:T(8,128)(2,1)} %copy-done) | copy-start | bytes 2359300
  68.5 20.3 %all-to-all-start.2 = ((bf16[4,384,384]{2,1,0:T(8,128)(2,1)}), bf16[4,384,384]{2,1,0:T(8,128)(2,1)S(1)}, u32[]{:S(2)}, u32[]{:S(2)}) async-start(bf16[4,384,384]{2,1,0:T(8,128)(2,1)} %bitcast.27), calls=%async_computation.2 | async-start | bytes 2359296 | tf_op jit(solution)/shard_map/all_to_all | solution.py:191
  75.9 20.4 %collective-permute-start.1 = (bf16[384,1024]{1,0:T(8,128)(2,1)}, bf16[384,1024]{1,0:T(8,128)(2,1)S(1)}, u32[]{:S(2)}, u32[]{:S(2)}) collective-permute-start(bf16[384,1024]{1,0:T(8,128)(2,1)} %get-tuple-element.12.after), channel_id=1, source_target_pairs={{0,64},{32,224},{64,0},{96,160},{128,192},{160,96},{192,128},{224,... | collective-permute-start | bytes 2359304 | tf_op jit(solution)/shard_map/ppermute | solution.py:43
  89.6 52.7 %all-to-all-start.3 = ((bf16[8,48,384]{2,1,0:T(8,128)(2,1)}), bf16[8,48,384]{2,1,0:T(8,128)(2,1)S(1)}, u32[]{:S(2)}, u32[]{:S(2)}) async-start(bf16[8,48,384]{2,1,0:T(8,128)(2,1)} %bitcast.16), calls=%async_computation.3 | async-start | bytes 589824 | tf_op jit(solution)/shard_map/all_to_all | solution.py:201
  96.6 8.8 %collective-permute-start.2 = (bf16[192,1024]{1,0:T(8,128)(2,1)S(1)}, bf16[192,1024]{1,0:T(8,128)(2,1)S(1)}, u32[]{:S(2)}, u32[]{:S(2)}) collective-permute-start(bf16[192,1024]{1,0:T(8,128)(2,1)S(1)} %slice.44), channel_id=1, source_target_pairs={{0,192},{32,96},{64,128},{96,32},{128,64},{160,224},{192,0},{224,1... | collective-permute-start | bytes 1179656 | tf_op jit(solution)/shard_map/ppermute | solution.py:43
  105.6 36.7 %collective-permute-start.3 = (bf16[96,1024]{1,0:T(8,128)(2,1)S(1)}, bf16[96,1024]{1,0:T(8,128)(2,1)S(1)}, u32[]{:S(2)}, u32[]{:S(2)}) collective-permute-start(bf16[96,1024]{1,0:T(8,128)(2,1)S(1)} %slice.45), channel_id=1, source_target_pairs={{0,256},{1,769},{2,258},{3,771},{4,260},{5,773},{6,262},{7,775},{2... | collective-permute-start | bytes 589832 | tf_op jit(solution)/shard_map/ppermute | solution.py:43
  142.4 20.7 %collective-permute-start.4 = (bf16[48,1024]{1,0:T(8,128)(2,1)S(1)}, bf16[48,1024]{1,0:T(8,128)(2,1)S(1)}, u32[]{:S(2)}, u32[]{:S(2)}) collective-permute-start(bf16[48,1024]{1,0:T(8,128)(2,1)S(1)} %slice.46), channel_id=1, source_target_pairs={{0,768},{1,257},{2,770},{3,259},{4,772},{5,261},{6,774},{7,263},{2... | collective-permute-start | bytes 294920 | tf_op jit(solution)/shard_map/ppermute | solution.py:43

commit v5 on v4

--- a/solution.py
+++ b/solution.py
@@ -56,7 +56,15 @@
     return block
 
 
-def attend_kernel(keys, counts, lat, weight, query, grad, token, attended, dflat, kv):
+def pick_blocks(depth, blocks, lat, picked):
+    for i in range(picked.shape[0] // depth):
+        start = pl.multiple_of(blocks[i] * depth, 16)
+        picked[i * depth : (i + 1) * depth, :] = lat[pl.ds(start, depth), :]
+
+
+def main_kernel(
+    keys, depth, counts, blocks, lat, weight, query, grad, token, attended, dflat, sent, lat_term, kv, picked
+):
     samples, _, width = query.shape
     scale = HEAD ** (-0.5)
     kv[...] = dot(lat[...], weight[...], TRANS_A).astype(bf16)
@@ -79,28 +87,18 @@
             dscore = prob * (dprob - jnp.sum(dprob * prob, axis=0, keepdims=True)) * scale
             dflat[rows, low] = dot(dscore.astype(bf16), q).astype(bf16)
             dflat[rows, high] = dot(prob_bf, g).astype(bf16)
-
-
-def latent_kernel(weight, dflat, after, out):
-    out[...] = dot(weight[...], dflat[...], TRANS_B).astype(bf16)
-
-
-def pick_blocks(depth, blocks, lat, picked):
-    for i in range(picked.shape[0] // depth):
-        start = pl.multiple_of(blocks[i] * depth, 16)
-        picked[i * depth : (i + 1) * depth, :] = lat[pl.ds(start, depth), :]
-
-
-def send_kernel(depth, blocks, lat, dflat, out, picked):
     pick_blocks(depth, blocks, lat, picked)
-    out[...] = dot(picked[...], dflat[...]).astype(bf16)
-
-
-def keep_kernel(depth, blocks, lat, dflat, other, keep, send, picked):
+    sent[...] = dot(picked[...], dflat[...]).astype(bf16)
+    lat_term[...] = dot(weight[...], dflat[...], TRANS_B).astype(bf16)
+
+
+def keep_kernel(depth, blocks, lat, dflat, other, keep_k, keep_v, send_k, send_v, picked):
     pick_blocks(depth, blocks, lat, picked)
-    half = keep.shape[0]
-    keep[...] = dot(picked[:half], dflat[...]) + other[:half].astype(f32)
-    send[...] = (dot(picked[half:], dflat[...]) + other[half:].astype(f32)).astype(bf16)
+    half, cols = keep_k.shape
+    for at, send, keep in ((0, send_k, keep_k), (cols, send_v, keep_v)):
+        part = slice(at, at + cols)
+        send[...] = (dot(picked[half:], dflat[:, part]) + other[half:, part].astype(f32)).astype(bf16)
+        keep[...] = dot(picked[:half], dflat[:, part]) + other[:half, part].astype(f32)
 
 
 def sum_kernel(parts, after, out):
@@ -131,56 +129,38 @@
     core = lax.axis_index("core")
     lat = gather_latents(latents.reshape(rows, depth).T)
 
-    attended, dflat = call(
-        functools.partial(attend_kernel, keys),
-        [SMEM] + [VMEM] * 5,
+    half, cols = width // 4, 2 * local
+    zs = jnp.stack(relative("zh"))
+
+    def blocks(at_core, ys):
+        return (zs[None, :] * 8 + jnp.stack(ys)[:, None] * 2 + at_core).reshape(-1).astype(jnp.int32)
+
+    mine, second, first, both = relative("y")
+    picked = pltpu.VMEM((2 * half, rows), bf16)
+    attended, dflat, grad_send, lat_term = call(
+        functools.partial(main_kernel, keys, depth),
+        [SMEM] * 2 + [VMEM] * 5,
         (
             jax.ShapeDtypeStruct(queries.shape[1:], bf16),
-            jax.ShapeDtypeStruct((rows, 2 * local), bf16),
+            jax.ShapeDtypeStruct((rows, cols), bf16),
+            jax.ShapeDtypeStruct((2 * half, cols), bf16),
+            jax.ShapeDtypeStruct((width, rows), bf16),
         ),
-        [pltpu.VMEM((rows, 2 * local), bf16)],
-        2 * rows * width * 2 * local,
+        [pltpu.VMEM((rows, cols), bf16), picked],
+        5 * rows * width * cols,
         image_counts,
+        blocks(1 - core, [mine, first, second, both]),
         lat,
         weight,
         queries[0],
         out_grad[0],
         token_image.reshape(samples, 1, -1),
     )
-
-    half, cols = width // 4, 2 * local
-    zs = jnp.stack(relative("zh"))
-
-    def blocks(at_core, ys):
-        return (zs[None, :] * 8 + jnp.stack(ys)[:, None] * 2 + at_core).reshape(-1).astype(jnp.int32)
-
-    mine, second, first, both = relative("y")
-    picked = [pltpu.VMEM((2 * half, rows), bf16)]
-    grad_send = call(
-        functools.partial(send_kernel, depth),
-        [SMEM, VMEM, VMEM],
-        jax.ShapeDtypeStruct((2 * half, cols), bf16),
-        picked,
-        width * rows * cols,
-        blocks(1 - core, [mine, first, second, both]),
-        lat,
-        dflat,
-    )
-    lat_term = call(
-        latent_kernel,
-        [VMEM, VMEM, pl.BlockSpec(memory_space=pl.ANY)],
-        jax.ShapeDtypeStruct((width, rows), bf16),
-        [],
-        2 * width * rows * cols,
-        weight,
-        dflat,
-        grad_send,
-    )
-    keep, send = call(
+    keep_k, keep_v, send_k, send_v = call(
         functools.partial(keep_kernel, depth),
         [SMEM, VMEM, VMEM, VMEM],
-        (jax.ShapeDtypeStruct((half, cols), f32), jax.ShapeDtypeStruct((half, cols), bf16)),
-        picked,
+        (jax.ShapeDtypeStruct((half, local), f32),) * 2 + (jax.ShapeDtypeStruct((half, local), bf16),) * 2,
+        [picked],
         width * rows * cols,
         blocks(core, [mine, second, first, both]),
         lat,
@@ -196,18 +176,25 @@
         [],
         4 * half * rows,
         lat_parts,
-        send,
+        send_v,
     )
     lat_parts = lax.all_to_all(lat_sum.reshape(8, depth, rows), "mp", 0, 0, tiled=True)
 
-    grad = (keep + paired(send, "y", True).astype(f32)).reshape(2, -1, cols)
-    grad = grad[0] + paired(grad[1].astype(bf16), "y", False).astype(f32)
-    grad = grad.reshape(2, -1, cols)
-    grad = grad[0] + paired(grad[1].astype(bf16), "zh", True).astype(f32)
     lat_sum = jnp.sum(lat_parts.astype(f32), axis=0)
-    grad, lat_sum = lax.optimization_barrier((grad, lat_sum))
-    grad = grad.reshape(2, -1, cols)
-    kv_grad = grad[0] + paired(grad[1].astype(bf16), "zh", False).astype(f32)
+
+    def split(x):
+        return x.reshape(2, -1, local)
+
+    key = split(keep_k + paired(send_k, "y", True).astype(f32))
+    value = split(keep_v + paired(send_v, "y", True).astype(f32))
+    key = split(key[0] + paired(key[1].astype(bf16), "y", False).astype(f32))
+    value = split(value[0] + paired(value[1].astype(bf16), "y", False).astype(f32))
+    key = split(key[0] + paired(key[1].astype(bf16), "zh", True).astype(f32))
+    value = split(value[0] + paired(value[1].astype(bf16), "zh", True).astype(f32))
+    value, lat_sum = lax.optimization_barrier((value, lat_sum))
+    key = key[0] + paired(key[1].astype(bf16), "zh", False).astype(f32)
+    value = value[0] + paired(value[1].astype(bf16), "zh", False).astype(f32)
+    kv_grad = jnp.stack([key, value], axis=1)
     return (
         attended[None],
         kv_grad.reshape(1, depth, 2, local),

time: 165 us -> 174 us (1.055)
  the two profiles are of different devices: /device:TPU:9 before, /device:TPU:224 now
where the time goes in v5:
time: 174 us; the launch traced here: 173 us
  starting transfers between devices  75.5 us (43%)
  waiting for transfers between devices  47.3 us (27%)
  blocking collectives  23 us (13%)
  local copies, waits for them, and re-layouts  14 us (8%)
  Pallas kernels  11.9 us (7%)
    ppermute x8, starting transfers between devices, paired(): return lax.ppermute(x, axes, pairs)  55.9 us
    ppermute x8, waiting for transfers between devices, paired(): return lax.ppermute(x, axes, pairs)  23.5 us
    all_to_all x1, blocking collectives, gather_latents(): block = lax.all_to_all(copies, axis, 0, 0, tiled=True)  23 us
    unnamed x26, local copies, waits for them, and re-layouts  12.3 us
    all_to_all x1, waiting for transfers between devices, body(): lax.all_to_all(lat_term.reshape(4, half, rows), 'section', 0, 0, tiled=True)  12 us
    pallas_call x3, Pallas kernels, call(): pl.pallas_call(kernel, out_shape=shapes, in_specs=specs, out_specs=jax.tr...  11.9 us
    all_to_all x1, waiting for transfers between devices, gather_latents(): block = lax.all_to_all(copies, axis, 0, 0, tiled=True)  11.6 us
    all_to_all x1, starting transfers between devices, body(): lax.all_to_all(lat_sum.reshape(8, depth, rows), 'mp', 0, 0, tiled=True)  9.9 us
  transfers between devices with their start and end apart: 12, of which 7 were waited for; matrix products, arithmetic and copies ran while one was open for 4% of the time, Pallas kernels for 1%

profile of v5, /device:TPU:224, one launch (start us, length us, event | category | flops | bytes accessed | tf_op | source)
XLA Modules:
  0.0 173.2 jit_solution(10643822185215525925)
XLA Ops:
  0.6 0.8 copy.10
  1.6 23.0 %all_to_all.20 = bf16[8,48,384]{2,1,0:T(8,128)(2,1)S(1)} all-to-all(bf16[8,48,384]{2,1,0:T(8,128)(2,1)S(1)} %broadcast_in_dim.6), channel_id=1, replica_groups=mesh['zh'=4,'y'=4,'core'=2,'section'=4,'mp'=8] {'mp'}, dimensions={0} | all-to-all | bytes 589824 | tf_op jit(solution)/shard_map/all_to_all | solution.py:54
  24.6 1.1 broadcast_in_dim.14
  25.7 4.3 %all-to-all-start.1 = ((bf16[4,384,384]{2,1,0:T(8,128)(2,1)}), bf16[4,384,384]{2,1,0:T(8,128)(2,1)S(1)}, u32[]{:S(2)}, u32[]{:S(2)}) async-start(bf16[4,384,384]{2,1,0:T(8,128)(2,1)} %broadcast_in_dim.14), calls=%async_computation.1 | async-start | bytes 2359296 | tf_op jit(solution)/shard_map/all_to_all | solution.py:54
  30.3 4.4 %copy.13 = bf16[192,8,2,512]{3,1,2,0:T(8,128)(2,1)} copy(bf16[192,8,2,512]{3,2,1,0:T(2,128)(2,1)} %bitcast.44) | data formatting | bytes 6291456
  34.7 11.6 %all-to-all-done.1 = bf16[4,384,384]{2,1,0:T(8,128)(2,1)S(1)} async-done(((bf16[4,384,384]{2,1,0:T(8,128)(2,1)}), bf16[4,384,384]{2,1,0:T(8,128)(2,1)S(1)}, u32[]{:S(2)}, u32[]{:S(2)}) %all-to-all-start.1) | async-done | bytes 1179680 | tf_op jit(solution)/shard_map/all_to_all | solution.py:54
  46.4 1.9 %copy-done = bf16[192,8,2,512]{3,1,2,0:T(8,128)(2,1)S(1)} copy-done((bf16[192,8,2,512]{3,1,2,0:T(8,128)(2,1)S(1)}, bf16[192,8,2,512]{3,1,2,0:T(8,128)(2,1)}, u32[]{:S(2)}) %copy-start) | copy-done | bytes 3145752
  48.3 8.6 %shard_map.85 = (bf16[2,128,512]{2,1,0:T(8,128)(2,1)}, bf16[384,1024]{1,0:T(8,128)(2,1)S(1)}, bf16[768,1024]{1,0:T(8,128)(2,1)}, bf16[1536,384]{1,0:T(8,128)(2,1)}) custom-call(s32[2]{0:T(128)S(1)} %copy-done.10, s32[16]{0:T(128)S(1)} %add.94.blocks, bf16[1536,384]{1,0:T(8,128)(2,1)S(1)} %bitcast.38, bf16[1536,1024]{1,0:T(8,128)(2,1)S(1)} %bitcast.40, ...), custom_call_target="tpu_custom_call" | custom-call | flops 3019898880 | bytes 4850760 | tf_op jit(solution)/shard_map/pallas_call | solution.py:113
  56.9 0.9 copy-done.3
  57.7 1.9 %collective-permute-start = (bf16[768,1024]{1,0:T(8,128)(2,1)}, bf16[768,1024]{1,0:T(8,128)(2,1)}, u32[]{:S(2)}, u32[]{:S(2)}) collective-permute-start(bf16[768,1024]{1,0:T(8,128)(2,1)} %get-tuple-element.15), channel_id=1, source_target_pairs={{0,32},{32,0},{1,33},{33,1},{2,34},{34,2},{3,35},{35,3},{4,36},{36... | collective-permute-start | bytes 4718600 | tf_op jit(solution)/shard_map/ppermute | solution.py:47
  59.7 3.5 %all-to-all-start.2 = ((bf16[4,384,384]{2,1,0:T(8,128)(2,1)}), bf16[4,384,384]{2,1,0:T(8,128)(2,1)S(1)}, u32[]{:S(2)}, u32[]{:S(2)}) async-start(bf16[4,384,384]{2,1,0:T(8,128)(2,1)} %bitcast.17), calls=%async_computation.2 | async-start | bytes 2359296 | tf_op jit(solution)/shard_map/all_to_all | solution.py:171
  63.4 1.1 copy-done.4
  64.5 2.4 %shard_map.86 = (f32[384,512]{1,0:T(8,128)S(1)}, f32[384,512]{1,0:T(8,128)S(1)}, bf16[384,512]{1,0:T(8,128)(2,1)S(1)}, bf16[384,512]{1,0:T(8,128)(2,1)S(1)}) custom-call(s32[16]{0:T(128)S(1)} %add.99.blocks, bf16[1536,384]{1,0:T(8,128)(2,1)S(1)} %bitcast.39, bf16[384,1024]{1,0:T(8,128)(2,1)S(1)} %copy-done.4, bf16[768,1024]{1,0:T(8,128)(2,1)} %collective-permute-done.other), custom_call_target="tpu_custom_call" | custom-call | flops 603979776 | bytes 3539008 | tf_op jit(solution)/shard_map/pallas_call | solution.py:113
  66.9 0.9 copy-done.1
  67.8 0.8 copy-done.5
  68.6 12.0 %all-to-all-done.2.parts = bf16[4,384,384]{2,1,0:T(8,128)(2,1)S(1)} async-done(((bf16[4,384,384]{2,1,0:T(8,128)(2,1)}), bf16[4,384,384]{2,1,0:T(8,128)(2,1)S(1)}, u32[]{:S(2)}, u32[]{:S(2)}) %all-to-all-start.2) | async-done | bytes 1179680 | tf_op jit(solution)/shard_map/all_to_all | solution.py:171
  80.6 0.9 shard_map.87
  81.5 9.9 %all-to-all-start.3 = ((bf16[8,48,384]{2,1,0:T(8,128)(2,1)}), bf16[8,48,384]{2,1,0:T(8,128)(2,1)S(1)}, u32[]{:S(2)}, u32[]{:S(2)}) async-start(bf16[8,48,384]{2,1,0:T(8,128)(2,1)} %bitcast.18), calls=%async_computation.3 | async-start | bytes 589824 | tf_op jit(solution)/shard_map/all_to_all | solution.py:181
  91.4 3.5 %collective-permute-start.1 = (bf16[384,512]{1,0:T(8,128)(2,1)S(1)}, bf16[384,512]{1,0:T(8,128)(2,1)S(1)}, u32[]{:S(2)}, u32[]{:S(2)}) collective-permute-start(bf16[384,512]{1,0:T(8,128)(2,1)S(1)} %copy-done.6), channel_id=1, source_target_pairs={{0,64},{32,224},{64,0},{96,160},{128,192},{160,96},{192,128},{224,... | collective-permute-start | bytes 1179656 | tf_op jit(solution)/shard_map/ppermute | solution.py:43
  94.9 2.4 %collective-permute-start.5 = (bf16[384,512]{1,0:T(8,128)(2,1)S(1)}, bf16[384,512]{1,0:T(8,128)(2,1)S(1)}, u32[]{:S(2)}, u32[]{:S(2)}) collective-permute-start(bf16[384,512]{1,0:T(8,128)(2,1)S(1)} %get-tuple-element.19.after), channel_id=1, source_target_pairs={{0,64},{32,224},{64,0},{96,160},{128,192},{160,96},{192,128},{224,... | collective-permute-start | bytes 1179656 | tf_op jit(solution)/shard_map/ppermute | solution.py:43
  97.2 3.8 %collective-permute-done.1 = bf16[384,512]{1,0:T(8,128)(2,1)S(1)} collective-permute-done((bf16[384,512]{1,0:T(8,128)(2,1)S(1)}, bf16[384,512]{1,0:T(8,128)(2,1)S(1)}, u32[]{:S(2)}, u32[]{:S(2)}) %collective-permute-start.1) | collective-permute-done | bytes 393248 | tf_op jit(solution)/shard_map/ppermute | solution.py:43
  101.2 4.9 %collective-permute-start.2 = (bf16[192,512]{1,0:T(8,128)(2,1)S(1)}, bf16[192,512]{1,0:T(8,128)(2,1)S(1)}, u32[]{:S(2)}, u32[]{:S(2)}) collective-permute-start(bf16[192,512]{1,0:T(8,128)(2,1)S(1)} %slice.92), channel_id=1, source_target_pairs={{0,192},{32,96},{64,128},{96,32},{128,64},{160,224},{192,0},{224,1... | collective-permute-start | bytes 589832 | tf_op jit(solution)/shard_map/ppermute | solution.py:43
  106.3 4.3 %collective-permute-start.6 = (bf16[192,512]{1,0:T(8,128)(2,1)S(1)}, bf16[192,512]{1,0:T(8,128)(2,1)S(1)}, u32[]{:S(2)}, u32[]{:S(2)}) collective-permute-start(bf16[192,512]{1,0:T(8,128)(2,1)S(1)} %slice.91), channel_id=1, source_target_pairs={{0,192},{32,96},{64,128},{96,32},{128,64},{160,224},{192,0},{224,1... | collective-permute-start | bytes 589832 | tf_op jit(solution)/shard_map/ppermute | solution.py:43
  110.7 15.5 %collective-permute-start.3 = (bf16[96,512]{1,0:T(8,128)(2,1)S(1)}, bf16[96,512]{1,0:T(8,128)(2,1)S(1)}, u32[]{:S(2)}, u32[]{:S(2)}) collective-permute-start(bf16[96,512]{1,0:T(8,128)(2,1)S(1)} %slice.94), channel_id=1, source_target_pairs={{0,256},{1,769},{2,258},{3,771},{4,260},{5,773},{6,262},{7,775},{2... | collective-permute-start | bytes 294920 | tf_op jit(solution)/shard_map/ppermute | solution.py:43
  126.3 4.3 %collective-permute-start.7 = (bf16[96,512]{1,0:T(8,128)(2,1)S(1)}, bf16[96,512]{1,0:T(8,128)(2,1)S(1)}, u32[]{:S(2)}, u32[]{:S(2)}) collective-permute-start(bf16[96,512]{1,0:T(8,128)(2,1)S(1)} %slice.93), channel_id=1, source_target_pairs={{0,256},{1,769},{2,258},{3,771},{4,260},{5,773},{6,262},{7,775},{2... | collective-permute-start | bytes 294920 | tf_op jit(solution)/shard_map/ppermute | solution.py:43
  130.6 7.2 %collective-permute-done.3 = bf16[96,512]{1,0:T(8,128)(2,1)S(1)} collective-permute-done((bf16[96,512]{1,0:T(8,128)(2,1)S(1)}, bf16[96,512]{1,0:T(8,128)(2,1)S(1)}, u32[]{:S(2)}, u32[]{:S(2)}) %collective-permute-start.3) | collective-permute-done | bytes 98336 | tf_op jit(solution)/shard_map/ppermute | solution.py:43
  137.9 19.1 %collective-permute-start.4 = (bf16[48,512]{1,0:T(8,128)(2,1)S(1)}, bf16[48,512]{1,0:T(8,128)(2,1)S(1)}, u32[]{:S(2)}, u32[]{:S(2)}) collective-permute-start(bf16[48,512]{1,0:T(8,128)(2,1)S(1)} %slice.95), channel_id=1, source_target_pairs={{0,768},{1,257},{2,770},{3,259},{4,772},{5,261},{6,774},{7,263},{2... | collective-permute-start | bytes 147464 | tf_op jit(solution)/shard_map/ppermute | solution.py:43
  157.1 1.9 %collective-permute-start.8 = (bf16[48,512]{1,0:T(8,128)(2,1)S(1)}, bf16[48,512]{1,0:T(8,128)(2,1)S(1)}, u32[]{:S(2)}, u32[]{:S(2)}) collective-permute-start(bf16[48,512]{1,0:T(8,128)(2,1)S(1)} %fusion.2), channel_id=1, source_target_pairs={{0,768},{1,257},{2,770},{3,259},{4,772},{5,261},{6,774},{7,263},{2... | collective-permute-start | bytes 147464 | tf_op jit(solution)/shard_map/ppermute | solution.py:43
  159.0 0.8 collective-permute-done.4
  159.9 0.6 copy.12
  160.6 11.7 %collective-permute-done.8 = bf16[48,512]{1,0:T(8,128)(2,1)S(1)} collective-permute-done((bf16[48,512]{1,0:T(8,128)(2,1)S(1)}, bf16[48,512]{1,0:T(8,128)(2,1)S(1)}, u32[]{:S(2)}, u32[]{:S(2)}) %collective-permute-start.8) | collective-permute-done | bytes 49184 | tf_op jit(solution)/shard_map/ppermute | solution.py:43
  172.3 0.8 copy.11
  (47 shorter events, 1.3 us)
Async XLA Ops:
  25.7 20.7 %all-to-all-start.1 = ((bf16[4,384,384]{2,1,0:T(8,128)(2,1)}), bf16[4,384,384]{2,1,0:T(8,128)(2,1)S(1)}, u32[]{:S(2)}, u32[]{:S(2)}) async-start(bf16[4,384,384]{2,1,0:T(8,128)(2,1)} %broadcast_in_dim.14), calls=%async_computation.1 | async-start | bytes 2359296 | tf_op jit(solution)/shard_map/all_to_all | solution.py:54
  30.3 16.1 %copy-start.7 = (bf16[1,2,128,512]{3,2,1,0:T(8,128)(2,1)S(1)}, bf16[1,2,128,512]{3,2,1,0:T(8,128)(2,1)}, u32[]{:S(2)}) copy-start(bf16[1,2,128,512]{3,2,1,0:T(8,128)(2,1)} %param.6) | copy-start | bytes 786436
  30.3 16.1 %copy-start.8 = (bf16[1,2,128,512]{3,2,1,0:T(8,128)(2,1)S(1)}, bf16[1,2,128,512]{3,2,1,0:T(8,128)(2,1)}, u32[]{:S(2)}) copy-start(bf16[1,2,128,512]{3,2,1,0:T(8,128)(2,1)} %param.11) | copy-start | bytes 786436
  30.3 16.1 %copy-start.9 = (s32[2,128]{1,0:T(2,128)S(1)}, s32[2,128]{1,0:T(2,128)}, u32[]{:S(2)}) copy-start(s32[2,128]{1,0:T(2,128)} %param.9) | copy-start | bytes 3076
  30.3 16.1 %copy-start.10 = (s32[2]{0:T(128)S(1)}, s32[2]{0:T(128)}, u32[]{:S(2)}) copy-start(s32[2]{0:T(128)} %counts.1) | copy-start | bytes 28
  46.4 1.9 %copy-start = (bf16[192,8,2,512]{3,1,2,0:T(8,128)(2,1)S(1)}, bf16[192,8,2,512]{3,1,2,0:T(8,128)(2,1)}, u32[]{:S(2)}) copy-start(bf16[192,8,2,512]{3,1,2,0:T(8,128)(2,1)} %copy.13) | copy-start | bytes 9437188
  56.8 0.9 copy-start.3
  57.7 5.6 %collective-permute-start = (bf16[768,1024]{1,0:T(8,128)(2,1)}, bf16[768,1024]{1,0:T(8,128)(2,1)}, u32[]{:S(2)}, u32[]{:S(2)}) collective-permute-start(bf16[768,1024]{1,0:T(8,128)(2,1)} %get-tuple-element.15), channel_id=1, source_target_pairs={{0,32},{32,0},{1,33},{33,1},{2,34},{34,2},{3,35},{35,3},{4,36},{36... | collective-permute-start | bytes 4718600 | tf_op jit(solution)/shard_map/ppermute | solution.py:47
  59.7 21.0 %all-to-all-start.2 = ((bf16[4,384,384]{2,1,0:T(8,128)(2,1)}), bf16[4,384,384]{2,1,0:T(8,128)(2,1)S(1)}, u32[]{:S(2)}, u32[]{:S(2)}) async-start(bf16[4,384,384]{2,1,0:T(8,128)(2,1)} %bitcast.17), calls=%async_computation.2 | async-start | bytes 2359296 | tf_op jit(solution)/shard_map/all_to_all | solution.py:171
  63.4 1.1 copy-start.4
  66.9 0.9 copy-start.1
  67.8 0.8 copy-start.5
  80.6 10.8 %copy-start.6 = (bf16[384,512]{1,0:T(8,128)(2,1)S(1)}, bf16[384,512]{1,0:T(8,128)(2,1)}, u32[]{:S(2)}) copy-start(bf16[384,512]{1,0:T(8,128)(2,1)} %copy-done.5) | copy-start | bytes 1179652
  80.6 20.4 %copy-start.2 = (f32[384,512]{1,0:T(8,128)S(1)}, f32[384,512]{1,0:T(8,128)}, u32[]{:S(2)}) copy-start(f32[384,512]{1,0:T(8,128)} %copy-done.1) | copy-start | bytes 2359300
  81.5 75.5 %all-to-all-start.3 = ((bf16[8,48,384]{2,1,0:T(8,128)(2,1)}), bf16[8,48,384]{2,1,0:T(8,128)(2,1)S(1)}, u32[]{:S(2)}, u32[]{:S(2)}) async-start(bf16[8,48,384]{2,1,0:T(8,128)(2,1)} %bitcast.18), calls=%async_computation.3 | async-start | bytes 589824 | tf_op jit(solution)/shard_map/all_to_all | solution.py:181
  91.4 9.7 %collective-permute-start.1 = (bf16[384,512]{1,0:T(8,128)(2,1)S(1)}, bf16[384,512]{1,0:T(8,128)(2,1)S(1)}, u32[]{:S(2)}, u32[]{:S(2)}) collective-permute-start(bf16[384,512]{1,0:T(8,128)(2,1)S(1)} %copy-done.6), channel_id=1, source_target_pairs={{0,64},{32,224},{64,0},{96,160},{128,192},{160,96},{192,128},{224,... | collective-permute-start | bytes 1179656 | tf_op jit(solution)/shard_map/ppermute | solution.py:43
  94.9 11.3 %collective-permute-start.5 = (bf16[384,512]{1,0:T(8,128)(2,1)S(1)}, bf16[384,512]{1,0:T(8,128)(2,1)S(1)}, u32[]{:S(2)}, u32[]{:S(2)}) collective-permute-start(bf16[384,512]{1,0:T(8,128)(2,1)S(1)} %get-tuple-element.19.after), channel_id=1, source_target_pairs={{0,64},{32,224},{64,0},{96,160},{128,192},{160,96},{192,128},{224,... | collective-permute-start | bytes 1179656 | tf_op jit(solution)/shard_map/ppermute | solution.py:43
  101.2 9.4 %collective-permute-start.2 = (bf16[192,512]{1,0:T(8,128)(2,1)S(1)}, bf16[192,512]{1,0:T(8,128)(2,1)S(1)}, u32[]{:S(2)}, u32[]{:S(2)}) collective-permute-start(bf16[192,512]{1,0:T(8,128)(2,1)S(1)} %slice.92), channel_id=1, source_target_pairs={{0,192},{32,96},{64,128},{96,32},{128,64},{160,224},{192,0},{224,1... | collective-permute-start | bytes 589832 | tf_op jit(solution)/shard_map/ppermute | solution.py:43
  106.3 19.9 %collective-permute-start.6 = (bf16[192,512]{1,0:T(8,128)(2,1)S(1)}, bf16[192,512]{1,0:T(8,128)(2,1)S(1)}, u32[]{:S(2)}, u32[]{:S(2)}) collective-permute-start(bf16[192,512]{1,0:T(8,128)(2,1)S(1)} %slice.91), channel_id=1, source_target_pairs={{0,192},{32,96},{64,128},{96,32},{128,64},{160,224},{192,0},{224,1... | collective-permute-start | bytes 589832 | tf_op jit(solution)/shard_map/ppermute | solution.py:43
  110.7 27.1 %collective-permute-start.3 = (bf16[96,512]{1,0:T(8,128)(2,1)S(1)}, bf16[96,512]{1,0:T(8,128)(2,1)S(1)}, u32[]{:S(2)}, u32[]{:S(2)}) collective-permute-start(bf16[96,512]{1,0:T(8,128)(2,1)S(1)} %slice.94), channel_id=1, source_target_pairs={{0,256},{1,769},{2,258},{3,771},{4,260},{5,773},{6,262},{7,775},{2... | collective-permute-start | bytes 294920 | tf_op jit(solution)/shard_map/ppermute | solution.py:43
  126.3 30.7 %collective-permute-start.7 = (bf16[96,512]{1,0:T(8,128)(2,1)S(1)}, bf16[96,512]{1,0:T(8,128)(2,1)S(1)}, u32[]{:S(2)}, u32[]{:S(2)}) collective-permute-start(bf16[96,512]{1,0:T(8,128)(2,1)S(1)} %slice.93), channel_id=1, source_target_pairs={{0,256},{1,769},{2,258},{3,771},{4,260},{5,773},{6,262},{7,775},{2... | collective-permute-start | bytes 294920 | tf_op jit(solution)/shard_map/ppermute | solution.py:43
  137.9 21.9 %collective-permute-start.4 = (bf16[48,512]{1,0:T(8,128)(2,1)S(1)}, bf16[48,512]{1,0:T(8,128)(2,1)S(1)}, u32[]{:S(2)}, u32[]{:S(2)}) collective-permute-start(bf16[48,512]{1,0:T(8,128)(2,1)S(1)} %slice.95), channel_id=1, source_target_pairs={{0,768},{1,257},{2,770},{3,259},{4,772},{5,261},{6,774},{7,263},{2... | collective-permute-start | bytes 147464 | tf_op jit(solution)/shard_map/ppermute | solution.py:43
  157.1 15.2 %collective-permute-start.8 = (bf16[48,512]{1,0:T(8,128)(2,1)S(1)}, bf16[48,512]{1,0:T(8,128)(2,1)S(1)}, u32[]{:S(2)}, u32[]{:S(2)}) collective-permute-start(bf16[48,512]{1,0:T(8,128)(2,1)S(1)} %fusion.2), channel_id=1, source_target_pairs={{0,768},{1,257},{2,770},{3,259},{4,772},{5,261},{6,774},{7,263},{2... | collective-permute-start | bytes 147464 | tf_op jit(solution)/shard_map/ppermute | solution.py:43

commit v6 on v5

--- a/solution.py
+++ b/solution.py
@@ -101,11 +101,13 @@
         keep[...] = dot(picked[:half], dflat[:, part]) + other[:half, part].astype(f32)
 
 
-def sum_kernel(parts, after, out):
+def sum_kernel(depth, place, parts, after, out):
     total = parts[0].astype(f32)
     for i in range(1, parts.shape[0]):
         total += parts[i].astype(f32)
-    out[...] = total.astype(bf16)
+    for m in range(out.shape[0] // depth):
+        at = pl.multiple_of(place[m] * depth, 16)
+        out[pl.ds(at, depth), :] = total[m * depth : (m + 1) * depth]
 
 
 def call(kernel, specs, shapes, scratch, flops, *args):
@@ -168,33 +170,42 @@
         swap(grad_send, "core", 1),
     )
 
+    def split(x):
+        return x.reshape(2, -1, local)
+
     lat_parts = lax.all_to_all(lat_term.reshape(4, half, rows), "section", 0, 0, tiled=True)
+    key = split(keep_k + paired(send_k, "y", True).astype(f32))
+    value = split(keep_v + paired(send_v, "y", True).astype(f32))
+    last = value[1].astype(bf16)
+    grad = jnp.concatenate(
+        [
+            key[0] + paired(key[1].astype(bf16), "y", False).astype(f32),
+            value[0] + paired(last, "y", False).astype(f32),
+        ],
+        axis=-1,
+    ).reshape(2, -1, cols)
+    send = grad[1].astype(bf16)
+
+    to = jnp.arange(8, dtype=jnp.int32) ^ lax.axis_index("mp")
     lat_sum = call(
-        sum_kernel,
-        [VMEM, pl.BlockSpec(memory_space=pl.ANY)],
-        jax.ShapeDtypeStruct((half, rows), bf16),
+        functools.partial(sum_kernel, depth),
+        [SMEM, VMEM, pl.BlockSpec(memory_space=pl.ANY)],
+        jax.ShapeDtypeStruct((half, rows), f32),
         [],
         4 * half * rows,
+        (to % 2) * 4 + (to // 2 % 2) * 2 + to // 4,
         lat_parts,
-        send_v,
-    )
-    lat_parts = lax.all_to_all(lat_sum.reshape(8, depth, rows), "mp", 0, 0, tiled=True)
-
-    lat_sum = jnp.sum(lat_parts.astype(f32), axis=0)
-
-    def split(x):
-        return x.reshape(2, -1, local)
-
-    key = split(keep_k + paired(send_k, "y", True).astype(f32))
-    value = split(keep_v + paired(send_v, "y", True).astype(f32))
-    key = split(key[0] + paired(key[1].astype(bf16), "y", False).astype(f32))
-    value = split(value[0] + paired(value[1].astype(bf16), "y", False).astype(f32))
-    key = split(key[0] + paired(key[1].astype(bf16), "zh", True).astype(f32))
-    value = split(value[0] + paired(value[1].astype(bf16), "zh", True).astype(f32))
-    value, lat_sum = lax.optimization_barrier((value, lat_sum))
-    key = key[0] + paired(key[1].astype(bf16), "zh", False).astype(f32)
-    value = value[0] + paired(value[1].astype(bf16), "zh", False).astype(f32)
-    kv_grad = jnp.stack([key, value], axis=1)
+        last,
+    ).reshape(8, depth, rows)
+    lat_sum = lat_sum[:4] + swap(lat_sum[4:].astype(bf16), "mp", 1).astype(f32)
+
+    lat_send = lat_sum[2:].astype(bf16)
+    send, lat_send = lax.optimization_barrier((send, lat_send))
+
+    grad = (grad[0] + paired(send, "zh", True).astype(f32)).reshape(2, -1, cols)
+    kv_grad = grad[0] + paired(grad[1].astype(bf16), "zh", False).astype(f32)
+    lat_sum = lat_sum[:2] + swap(lat_send, "mp", 2).astype(f32)
+    lat_sum = lat_sum[0] + swap(lat_sum[1].astype(bf16), "mp", 4).astype(f32)
     return (
         attended[None],
         kv_grad.reshape(1, depth, 2, local),

time: 174 us -> 162 us (0.931)
  the two profiles are of different devices: /device:TPU:224 before, /device:TPU:2 now
where the time goes in v6:
time: 162 us
  starting transfers between devices  70.9 us (44%)
  waiting for transfers between devices  32.8 us (20%)
  blocking collectives  31.2 us (19%)
  local copies, waits for them, and re-layouts  12.4 us (8%)
  Pallas kernels  11.7 us (7%)
  other arithmetic  1.71 us (1%)
    ppermute x6, starting transfers between devices, paired(): return lax.ppermute(x, axes, pairs)  46.6 us
    all_to_all x1, blocking collectives, gather_latents(): block = lax.all_to_all(copies, axis, 0, 0, tiled=True)  31.2 us
    ppermute x6, waiting for transfers between devices, paired(): return lax.ppermute(x, axes, pairs)  22.9 us
    ppermute x4, starting transfers between devices, swap(): return lax.ppermute(x, axis, [(i, i ^ bit) for i in range(SIZE[axis])])  14.5 us
    pallas_call x3, Pallas kernels, call(): pl.pallas_call(kernel, out_shape=shapes, in_specs=specs, out_specs=jax.tr...  11.7 us
    unnamed x17, local copies, waits for them, and re-layouts  9.87 us
    all_to_all x1, waiting for transfers between devices, gather_latents(): block = lax.all_to_all(copies, axis, 0, 0, tiled=True)  7.4 us
    all_to_all x1, starting transfers between devices, body(): lax.all_to_all(lat_term.reshape(4, half, rows), 'section', 0, 0, tiled=True)  4.97 us
  transfers between devices with their start and end apart: 12, of which 6 were waited for; matrix products, arithmetic and copies ran while one was open for 4% of the time, Pallas kernels for 2%

profile of v6, /device:TPU:2, one launch (start us, length us, event | category | flops | bytes accessed | tf_op | source)
XLA Modules:
  0.0 161.7 jit_solution(3057132321337067772)
XLA Ops:
  0.6 0.8 copy.9
  1.6 31.2 %all_to_all.15 = bf16[8,48,384]{2,1,0:T(8,128)(2,1)S(1)} all-to-all(bf16[8,48,384]{2,1,0:T(8,128)(2,1)S(1)} %broadcast_in_dim.6), channel_id=1, replica_groups=mesh['zh'=4,'y'=4,'core'=2,'section'=4,'mp'=8] {'mp'}, dimensions={0} | all-to-all | bytes 589824 | tf_op jit(solution)/shard_map/all_to_all | solution.py:54
  32.8 1.1 broadcast_in_dim.14
  34.0 4.8 %all-to-all-start.1 = ((bf16[4,384,384]{2,1,0:T(8,128)(2,1)}), bf16[4,384,384]{2,1,0:T(8,128)(2,1)S(1)}, u32[]{:S(2)}, u32[]{:S(2)}) async-start(bf16[4,384,384]{2,1,0:T(8,128)(2,1)} %broadcast_in_dim.14), calls=%async_computation.1 | async-start | bytes 2359296 | tf_op jit(solution)/shard_map/all_to_all | solution.py:54
  39.1 4.4 %copy.11 = bf16[192,8,2,512]{3,1,2,0:T(8,128)(2,1)} copy(bf16[192,8,2,512]{3,2,1,0:T(2,128)(2,1)} %bitcast.41) | data formatting | bytes 6291456
  43.6 7.4 %all-to-all-done.1 = bf16[4,384,384]{2,1,0:T(8,128)(2,1)S(1)} async-done(((bf16[4,384,384]{2,1,0:T(8,128)(2,1)}), bf16[4,384,384]{2,1,0:T(8,128)(2,1)S(1)}, u32[]{:S(2)}, u32[]{:S(2)}) %all-to-all-start.1) | async-done | bytes 1179680 | tf_op jit(solution)/shard_map/all_to_all | solution.py:54
  51.0 1.9 %copy-done = bf16[192,8,2,512]{3,1,2,0:T(8,128)(2,1)S(1)} copy-done((bf16[192,8,2,512]{3,1,2,0:T(8,128)(2,1)S(1)}, bf16[192,8,2,512]{3,1,2,0:T(8,128)(2,1)}, u32[]{:S(2)}) %copy-start) | copy-done | bytes 3145752
  52.9 8.6 %shard_map.85 = (bf16[2,128,512]{2,1,0:T(8,128)(2,1)}, bf16[384,1024]{1,0:T(8,128)(2,1)S(1)}, bf16[768,1024]{1,0:T(8,128)(2,1)}, bf16[1536,384]{1,0:T(8,128)(2,1)}) custom-call(s32[2]{0:T(128)S(1)} %copy-done.6, s32[16]{0:T(128)S(1)} %add.115.blocks, bf16[1536,384]{1,0:T(8,128)(2,1)S(1)} %bitcast.35, bf16[1536,1024]{1,0:T(8,128)(2,1)S(1)} %bitcast.37, ...), custom_call_target="tpu_custom_call" | custom-call | flops 3019898880 | bytes 4850760 | tf_op jit(solution)/shard_map/pallas_call | solution.py:115
  61.5 0.9 copy-done.1
  62.4 1.9 %collective-permute-start = (bf16[768,1024]{1,0:T(8,128)(2,1)}, bf16[768,1024]{1,0:T(8,128)(2,1)}, u32[]{:S(2)}, u32[]{:S(2)}) collective-permute-start(bf16[768,1024]{1,0:T(8,128)(2,1)} %get-tuple-element.15), channel_id=1, source_target_pairs={{0,32},{32,0},{1,33},{33,1},{2,34},{34,2},{3,35},{35,3},{4,36},{36... | collective-permute-start | bytes 4718600 | tf_op jit(solution)/shard_map/ppermute | solution.py:47
  64.3 5.0 %all-to-all-start.2 = ((bf16[4,384,384]{2,1,0:T(8,128)(2,1)}), bf16[4,384,384]{2,1,0:T(8,128)(2,1)S(1)}, u32[]{:S(2)}, u32[]{:S(2)}) async-start(bf16[4,384,384]{2,1,0:T(8,128)(2,1)} %bitcast.15), calls=%async_computation.2 | async-start | bytes 2359296 | tf_op jit(solution)/shard_map/all_to_all | solution.py:176
  69.4 1.1 copy-done.2
  70.5 2.4 %shard_map.86 = (f32[384,512]{1,0:T(8,128)S(1)}, f32[384,512]{1,0:T(8,128)S(1)}, bf16[384,512]{1,0:T(8,128)(2,1)S(1)}, bf16[384,512]{1,0:T(8,128)(2,1)S(1)}) custom-call(s32[16]{0:T(128)S(1)} %add.120.blocks, bf16[1536,384]{1,0:T(8,128)(2,1)S(1)} %bitcast.36, bf16[384,1024]{1,0:T(8,128)(2,1)S(1)} %copy-done.2, bf16[768,1024]{1,0:T(8,128)(2,1)} %collective-permute-done.other), custom_call_target="tpu_custom_call" | custom-call | flops 603979776 | bytes 3539008 | tf_op jit(solution)/shard_map/pallas_call | solution.py:115
  72.9 3.5 %collective-permute-start.3 = (bf16[384,512]{1,0:T(8,128)(2,1)S(1)}, bf16[384,512]{1,0:T(8,128)(2,1)S(1)}, u32[]{:S(2)}, u32[]{:S(2)}) collective-permute-start(bf16[384,512]{1,0:T(8,128)(2,1)S(1)} %get-tuple-element.19), channel_id=1, source_target_pairs={{0,64},{32,224},{64,0},{96,160},{128,192},{160,96},{192,128},{224,... | collective-permute-start | bytes 1179656 | tf_op jit(solution)/shard_map/ppermute | solution.py:43
  76.4 2.4 %collective-permute-start.1 = (bf16[384,512]{1,0:T(8,128)(2,1)S(1)}, bf16[384,512]{1,0:T(8,128)(2,1)}, u32[]{:S(2)}, u32[]{:S(2)}) collective-permute-start(bf16[384,512]{1,0:T(8,128)(2,1)S(1)} %get-tuple-element.17), channel_id=1, source_target_pairs={{0,64},{32,224},{64,0},{96,160},{128,192},{160,96},{192,128},{224,... | collective-permute-start | bytes 1179656 | tf_op jit(solution)/shard_map/ppermute | solution.py:43
  78.8 3.8 %collective-permute-done.3 = bf16[384,512]{1,0:T(8,128)(2,1)S(1)} collective-permute-done((bf16[384,512]{1,0:T(8,128)(2,1)S(1)}, bf16[384,512]{1,0:T(8,128)(2,1)S(1)}, u32[]{:S(2)}, u32[]{:S(2)}) %collective-permute-start.3) | collective-permute-done | bytes 393248 | tf_op jit(solution)/shard_map/ppermute | solution.py:43
  82.7 2.5 %all-to-all-done.2.parts = bf16[4,384,384]{2,1,0:T(8,128)(2,1)S(1)} async-done(((bf16[4,384,384]{2,1,0:T(8,128)(2,1)}), bf16[4,384,384]{2,1,0:T(8,128)(2,1)S(1)}, u32[]{:S(2)}, u32[]{:S(2)}) %all-to-all-start.2) | async-done | bytes 1179680 | tf_op jit(solution)/shard_map/all_to_all | solution.py:176
  85.3 0.7 shard_map.87
  86.0 4.9 %collective-permute-start.4 = (bf16[192,512]{1,0:T(8,128)(2,1)S(1)}, bf16[192,512]{1,0:T(8,128)(2,1)S(1)}, u32[]{:S(2)}, u32[]{:S(2)}) collective-permute-start(bf16[192,512]{1,0:T(8,128)(2,1)S(1)} %slice.115.after), channel_id=1, source_target_pairs={{0,192},{32,96},{64,128},{96,32},{128,64},{160,224},{192,0},{224,1... | collective-permute-start | bytes 589832 | tf_op jit(solution)/shard_map/ppermute | solution.py:43
  90.9 4.1 %collective-permute-start.5 = (bf16[4,48,384]{2,1,0:T(8,128)(2,1)S(1)}, bf16[4,48,384]{2,1,0:T(8,128)(2,1)S(1)}, u32[]{:S(2)}, u32[]{:S(2)}) collective-permute-start(bf16[4,48,384]{2,1,0:T(8,128)(2,1)S(1)} %bitcast.44), channel_id=1, source_target_pairs={{0,1},{1,0},{2,3},{3,2},{4,5},{5,4},{6,7},{7,6},{8,9},{9,8},{10,11... | collective-permute-start | bytes 442376 | tf_op jit(solution)/shard_map/ppermute | solution.py:47
  95.1 1.1 convert_add_fusion.1
  96.2 2.1 %collective-permute-start.2 = (bf16[192,512]{1,0:T(8,128)(2,1)S(1)}, bf16[192,512]{1,0:T(8,128)(2,1)S(1)}, u32[]{:S(2)}, u32[]{:S(2)}) collective-permute-start(bf16[192,512]{1,0:T(8,128)(2,1)S(1)} %slice.116), channel_id=1, source_target_pairs={{0,192},{32,96},{64,128},{96,32},{128,64},{160,224},{192,0},{224,1... | collective-permute-start | bytes 589832 | tf_op jit(solution)/shard_map/ppermute | solution.py:43
  98.4 6.6 %collective-permute-done.2 = bf16[192,512]{1,0:T(8,128)(2,1)S(1)} collective-permute-done((bf16[192,512]{1,0:T(8,128)(2,1)S(1)}, bf16[192,512]{1,0:T(8,128)(2,1)S(1)}, u32[]{:S(2)}, u32[]{:S(2)}) %collective-permute-start.2) | collective-permute-done | bytes 196640 | tf_op jit(solution)/shard_map/ppermute | solution.py:43
  105.2 1.9 %collective-permute-start.8 = (bf16[2,48,384]{2,1,0:T(8,128)(2,1)S(1)}, bf16[2,48,384]{2,1,0:T(8,128)(2,1)S(1)}, u32[]{:S(2)}, u32[]{:S(2)}) collective-permute-start(bf16[2,48,384]{2,1,0:T(8,128)(2,1)S(1)} %slice.119), channel_id=1, source_target_pairs={{0,2},{1,3},{2,0},{3,1},{4,6},{5,7},{6,4},{7,5},{8,10},{9,11},{10,... | collective-permute-start | bytes 221192 | tf_op jit(solution)/shard_map/ppermute | solution.py:47
  107.1 15.7 %collective-permute-start.6 = (bf16[96,1024]{1,0:T(8,128)(2,1)S(1)}, bf16[96,1024]{1,0:T(8,128)(2,1)S(1)}, u32[]{:S(2)}, u32[]{:S(2)}) collective-permute-start(bf16[96,1024]{1,0:T(8,128)(2,1)S(1)} %fusion.2), channel_id=1, source_target_pairs={{0,256},{1,769},{2,258},{3,771},{4,260},{5,773},{6,262},{7,775},{2... | collective-permute-start | bytes 589832 | tf_op jit(solution)/shard_map/ppermute | solution.py:43
  122.9 6.5 %collective-permute-start.9 = (bf16[48,384]{1,0:T(8,128)(2,1)S(1)}, bf16[48,384]{1,0:T(8,128)(2,1)S(1)}, u32[]{:S(2)}, u32[]{:S(2)}) collective-permute-start(bf16[48,384]{1,0:T(8,128)(2,1)S(1)} %fusion.5), channel_id=1, source_target_pairs={{0,4},{1,5},{2,6},{3,7},{4,0},{5,1},{6,2},{7,3},{8,12},{9,13},{10,... | collective-permute-start | bytes 110600 | tf_op jit(solution)/shard_map/ppermute | solution.py:47
  129.4 5.6 %collective-permute-done.6 = bf16[96,1024]{1,0:T(8,128)(2,1)S(1)} collective-permute-done((bf16[96,1024]{1,0:T(8,128)(2,1)S(1)}, bf16[96,1024]{1,0:T(8,128)(2,1)S(1)}, u32[]{:S(2)}, u32[]{:S(2)}) %collective-permute-start.6) | collective-permute-done | bytes 196640 | tf_op jit(solution)/shard_map/ppermute | solution.py:43
  135.0 18.0 %collective-permute-start.7 = (bf16[48,1024]{1,0:T(8,128)(2,1)S(1)}, bf16[48,1024]{1,0:T(8,128)(2,1)S(1)}, u32[]{:S(2)}, u32[]{:S(2)}) collective-permute-start(bf16[48,1024]{1,0:T(8,128)(2,1)S(1)} %slice.118), channel_id=1, source_target_pairs={{0,768},{1,257},{2,770},{3,259},{4,772},{5,261},{6,774},{7,263},{2... | collective-permute-start | bytes 294920 | tf_op jit(solution)/shard_map/ppermute | solution.py:43
  153.1 0.1 reshape.176
  153.2 0.6 copy.10
  153.9 6.9 %collective-permute-done.7 = bf16[48,1024]{1,0:T(8,128)(2,1)S(1)} collective-permute-done((bf16[48,1024]{1,0:T(8,128)(2,1)S(1)}, bf16[48,1024]{1,0:T(8,128)(2,1)S(1)}, u32[]{:S(2)}, u32[]{:S(2)}) %collective-permute-start.7) | collective-permute-done | bytes 98336 | tf_op jit(solution)/shard_map/ppermute | solution.py:43
  160.8 0.8 reshape.175
  (41 shorter events, 1.1 us)
Async XLA Ops:
  34.0 17.0 %all-to-all-start.1 = ((bf16[4,384,384]{2,1,0:T(8,128)(2,1)}), bf16[4,384,384]{2,1,0:T(8,128)(2,1)S(1)}, u32[]{:S(2)}, u32[]{:S(2)}) async-start(bf16[4,384,384]{2,1,0:T(8,128)(2,1)} %broadcast_in_dim.14), calls=%async_computation.1 | async-start | bytes 2359296 | tf_op jit(solution)/shard_map/all_to_all | solution.py:54
  39.1 11.9 %copy-start.3 = (bf16[1,2,128,512]{3,2,1,0:T(8,128)(2,1)S(1)}, bf16[1,2,128,512]{3,2,1,0:T(8,128)(2,1)}, u32[]{:S(2)}) copy-start(bf16[1,2,128,512]{3,2,1,0:T(8,128)(2,1)} %param.6) | copy-start | bytes 786436
  39.1 11.9 %copy-start.4 = (bf16[1,2,128,512]{3,2,1,0:T(8,128)(2,1)S(1)}, bf16[1,2,128,512]{3,2,1,0:T(8,128)(2,1)}, u32[]{:S(2)}) copy-start(bf16[1,2,128,512]{3,2,1,0:T(8,128)(2,1)} %param.11) | copy-start | bytes 786436
  39.1 11.9 %copy-start.5 = (s32[2,128]{1,0:T(2,128)S(1)}, s32[2,128]{1,0:T(2,128)}, u32[]{:S(2)}) copy-start(s32[2,128]{1,0:T(2,128)} %param.9) | copy-start | bytes 3076
  39.1 11.9 %copy-start.6 = (s32[2]{0:T(128)S(1)}, s32[2]{0:T(128)}, u32[]{:S(2)}) copy-start(s32[2]{0:T(128)} %counts.1) | copy-start | bytes 28
  51.0 1.9 %copy-start = (bf16[192,8,2,512]{3,1,2,0:T(8,128)(2,1)S(1)}, bf16[192,8,2,512]{3,1,2,0:T(8,128)(2,1)}, u32[]{:S(2)}) copy-start(bf16[192,8,2,512]{3,1,2,0:T(8,128)(2,1)} %copy.11) | copy-start | bytes 9437188
  61.5 0.9 copy-start.1
  62.4 7.0 %collective-permute-start = (bf16[768,1024]{1,0:T(8,128)(2,1)}, bf16[768,1024]{1,0:T(8,128)(2,1)}, u32[]{:S(2)}, u32[]{:S(2)}) collective-permute-start(bf16[768,1024]{1,0:T(8,128)(2,1)} %get-tuple-element.15), channel_id=1, source_target_pairs={{0,32},{32,0},{1,33},{33,1},{2,34},{34,2},{3,35},{35,3},{4,36},{36... | collective-permute-start | bytes 4718600 | tf_op jit(solution)/shard_map/ppermute | solution.py:47
  64.3 21.0 %all-to-all-start.2 = ((bf16[4,384,384]{2,1,0:T(8,128)(2,1)}), bf16[4,384,384]{2,1,0:T(8,128)(2,1)S(1)}, u32[]{:S(2)}, u32[]{:S(2)}) async-start(bf16[4,384,384]{2,1,0:T(8,128)(2,1)} %bitcast.15), calls=%async_computation.2 | async-start | bytes 2359296 | tf_op jit(solution)/shard_map/all_to_all | solution.py:176
  69.4 1.1 copy-start.2
  72.9 9.7 %collective-permute-start.3 = (bf16[384,512]{1,0:T(8,128)(2,1)S(1)}, bf16[384,512]{1,0:T(8,128)(2,1)S(1)}, u32[]{:S(2)}, u32[]{:S(2)}) collective-permute-start(bf16[384,512]{1,0:T(8,128)(2,1)S(1)} %get-tuple-element.19), channel_id=1, source_target_pairs={{0,64},{32,224},{64,0},{96,160},{128,192},{160,96},{192,128},{224,... | collective-permute-start | bytes 1179656 | tf_op jit(solution)/shard_map/ppermute | solution.py:43
  76.4 18.7 %collective-permute-start.1 = (bf16[384,512]{1,0:T(8,128)(2,1)S(1)}, bf16[384,512]{1,0:T(8,128)(2,1)}, u32[]{:S(2)}, u32[]{:S(2)}) collective-permute-start(bf16[384,512]{1,0:T(8,128)(2,1)S(1)} %get-tuple-element.17), channel_id=1, source_target_pairs={{0,64},{32,224},{64,0},{96,160},{128,192},{160,96},{192,128},{224,... | collective-permute-start | bytes 1179656 | tf_op jit(solution)/shard_map/ppermute | solution.py:43
  86.0 19.1 %collective-permute-start.4 = (bf16[192,512]{1,0:T(8,128)(2,1)S(1)}, bf16[192,512]{1,0:T(8,128)(2,1)S(1)}, u32[]{:S(2)}, u32[]{:S(2)}) collective-permute-start(bf16[192,512]{1,0:T(8,128)(2,1)S(1)} %slice.115.after), channel_id=1, source_target_pairs={{0,192},{32,96},{64,128},{96,32},{128,64},{160,224},{192,0},{224,1... | collective-permute-start | bytes 589832 | tf_op jit(solution)/shard_map/ppermute | solution.py:43
  90.9 7.4 %collective-permute-start.5 = (bf16[4,48,384]{2,1,0:T(8,128)(2,1)S(1)}, bf16[4,48,384]{2,1,0:T(8,128)(2,1)S(1)}, u32[]{:S(2)}, u32[]{:S(2)}) collective-permute-start(bf16[4,48,384]{2,1,0:T(8,128)(2,1)S(1)} %bitcast.44), channel_id=1, source_target_pairs={{0,1},{1,0},{2,3},{3,2},{4,5},{5,4},{6,7},{7,6},{8,9},{9,8},{10,11... | collective-permute-start | bytes 442376 | tf_op jit(solution)/shard_map/ppermute | solution.py:47
  96.2 8.8 %collective-permute-start.2 = (bf16[192,512]{1,0:T(8,128)(2,1)S(1)}, bf16[192,512]{1,0:T(8,128)(2,1)S(1)}, u32[]{:S(2)}, u32[]{:S(2)}) collective-permute-start(bf16[192,512]{1,0:T(8,128)(2,1)S(1)} %slice.116), channel_id=1, source_target_pairs={{0,192},{32,96},{64,128},{96,32},{128,64},{160,224},{192,0},{224,1... | collective-permute-start | bytes 589832 | tf_op jit(solution)/shard_map/ppermute | solution.py:43
  105.2 17.7 %collective-permute-start.8 = (bf16[2,48,384]{2,1,0:T(8,128)(2,1)S(1)}, bf16[2,48,384]{2,1,0:T(8,128)(2,1)S(1)}, u32[]{:S(2)}, u32[]{:S(2)}) collective-permute-start(bf16[2,48,384]{2,1,0:T(8,128)(2,1)S(1)} %slice.119), channel_id=1, source_target_pairs={{0,2},{1,3},{2,0},{3,1},{4,6},{5,7},{6,4},{7,5},{8,10},{9,11},{10,... | collective-permute-start | bytes 221192 | tf_op jit(solution)/shard_map/ppermute | solution.py:47
  107.1 27.9 %collective-permute-start.6 = (bf16[96,1024]{1,0:T(8,128)(2,1)S(1)}, bf16[96,1024]{1,0:T(8,128)(2,1)S(1)}, u32[]{:S(2)}, u32[]{:S(2)}) collective-permute-start(bf16[96,1024]{1,0:T(8,128)(2,1)S(1)} %fusion.2), channel_id=1, source_target_pairs={{0,256},{1,769},{2,258},{3,771},{4,260},{5,773},{6,262},{7,775},{2... | collective-permute-start | bytes 589832 | tf_op jit(solution)/shard_map/ppermute | solution.py:43
  122.9 30.2 %collective-permute-start.9 = (bf16[48,384]{1,0:T(8,128)(2,1)S(1)}, bf16[48,384]{1,0:T(8,128)(2,1)S(1)}, u32[]{:S(2)}, u32[]{:S(2)}) collective-permute-start(bf16[48,384]{1,0:T(8,128)(2,1)S(1)} %fusion.5), channel_id=1, source_target_pairs={{0,4},{1,5},{2,6},{3,7},{4,0},{5,1},{6,2},{7,3},{8,12},{9,13},{10,... | collective-permute-start | bytes 110600 | tf_op jit(solution)/shard_map/ppermute | solution.py:47
  135.0 25.8 %collective-permute-start.7 = (bf16[48,1024]{1,0:T(8,128)(2,1)S(1)}, bf16[48,1024]{1,0:T(8,128)(2,1)S(1)}, u32[]{:S(2)}, u32[]{:S(2)}) collective-permute-start(bf16[48,1024]{1,0:T(8,128)(2,1)S(1)} %slice.118), channel_id=1, source_target_pairs={{0,768},{1,257},{2,770},{3,259},{4,772},{5,261},{6,774},{7,263},{2... | collective-permute-start | bytes 294920 | tf_op jit(solution)/shard_map/ppermute | solution.py:43

commit v7 on v6

--- a/solution.py
+++ b/solution.py
@@ -92,16 +92,16 @@
     lat_term[...] = dot(weight[...], dflat[...], TRANS_B).astype(bf16)
 
 
-def keep_kernel(depth, blocks, lat, dflat, other, keep_k, keep_v, send_k, send_v, picked):
+def keep_kernel(depth, blocks, lat, dflat, other, keep, send, picked):
     pick_blocks(depth, blocks, lat, picked)
-    half, cols = keep_k.shape
-    for at, send, keep in ((0, send_k, keep_k), (cols, send_v, keep_v)):
+    half, cols = keep.shape[0], keep.shape[1] // 2
+    for at in (0, cols):
         part = slice(at, at + cols)
-        send[...] = (dot(picked[half:], dflat[:, part]) + other[half:, part].astype(f32)).astype(bf16)
-        keep[...] = dot(picked[:half], dflat[:, part]) + other[:half, part].astype(f32)
-
-
-def sum_kernel(depth, place, parts, after, out):
+        send[:, part] = (dot(picked[half:], dflat[:, part]) + other[half:, part].astype(f32)).astype(bf16)
+        keep[:, part] = dot(picked[:half], dflat[:, part]) + other[:half, part].astype(f32)
+
+
+def sum_kernel(depth, place, parts, out):
     total = parts[0].astype(f32)
     for i in range(1, parts.shape[0]):
         total += parts[i].astype(f32)
@@ -158,10 +158,10 @@
         out_grad[0],
         token_image.reshape(samples, 1, -1),
     )
-    keep_k, keep_v, send_k, send_v = call(
+    keep, send = call(
         functools.partial(keep_kernel, depth),
         [SMEM, VMEM, VMEM, VMEM],
-        (jax.ShapeDtypeStruct((half, local), f32),) * 2 + (jax.ShapeDtypeStruct((half, local), bf16),) * 2,
+        (jax.ShapeDtypeStruct((half, cols), f32), jax.ShapeDtypeStruct((half, cols), bf16)),
         [picked],
         width * rows * cols,
         blocks(core, [mine, second, first, both]),
@@ -170,42 +170,30 @@
         swap(grad_send, "core", 1),
     )
 
-    def split(x):
-        return x.reshape(2, -1, local)
-
     lat_parts = lax.all_to_all(lat_term.reshape(4, half, rows), "section", 0, 0, tiled=True)
-    key = split(keep_k + paired(send_k, "y", True).astype(f32))
-    value = split(keep_v + paired(send_v, "y", True).astype(f32))
-    last = value[1].astype(bf16)
-    grad = jnp.concatenate(
-        [
-            key[0] + paired(key[1].astype(bf16), "y", False).astype(f32),
-            value[0] + paired(last, "y", False).astype(f32),
-        ],
-        axis=-1,
-    ).reshape(2, -1, cols)
+    grad = (keep + paired(send, "y", True).astype(f32)).reshape(2, -1, cols)
+    last = grad[1].astype(bf16)
+    grad = (grad[0] + paired(last, "y", False).astype(f32)).reshape(2, -1, cols)
     send = grad[1].astype(bf16)
 
     to = jnp.arange(8, dtype=jnp.int32) ^ lax.axis_index("mp")
     lat_sum = call(
         functools.partial(sum_kernel, depth),
-        [SMEM, VMEM, pl.BlockSpec(memory_space=pl.ANY)],
+        [SMEM, VMEM],
         jax.ShapeDtypeStruct((half, rows), f32),
         [],
         4 * half * rows,
         (to % 2) * 4 + (to // 2 % 2) * 2 + to // 4,
         lat_parts,
-        last,
     ).reshape(8, depth, rows)
     lat_sum = lat_sum[:4] + swap(lat_sum[4:].astype(bf16), "mp", 1).astype(f32)
 
-    lat_send = lat_sum[2:].astype(bf16)
-    send, lat_send = lax.optimization_barrier((send, lat_send))
-
     grad = (grad[0] + paired(send, "zh", True).astype(f32)).reshape(2, -1, cols)
-    kv_grad = grad[0] + paired(grad[1].astype(bf16), "zh", False).astype(f32)
-    lat_sum = lat_sum[:2] + swap(lat_send, "mp", 2).astype(f32)
-    lat_sum = lat_sum[0] + swap(lat_sum[1].astype(bf16), "mp", 4).astype(f32)
+    lat_sum = lat_sum[:2] + swap(lat_sum[2:].astype(bf16), "mp", 2).astype(f32)
+    last = lat_sum[1].astype(bf16)
+    send, last = lax.optimization_barrier((grad[1].astype(bf16), last))
+    kv_grad = grad[0] + paired(send, "zh", False).astype(f32)
+    lat_sum = lat_sum[0] + swap(last, "mp", 4).astype(f32)
     return (
         attended[None],
         kv_grad.reshape(1, depth, 2, local),

time: 162 us -> 163 us (level)
  the two profiles are of different devices: /device:TPU:2 before, /device:TPU:120 now
where the time goes in v7:
time: 163 us; the launch traced here: 162 us
  starting transfers between devices  69 us (42%)
  waiting for transfers between devices  40.2 us (25%)
  blocking collectives  27.2 us (17%)
  Pallas kernels  12.3 us (8%)
  local copies, waits for them, and re-layouts  11.5 us (7%)
    ppermute x4, starting transfers between devices, paired(): return lax.ppermute(x, axes, pairs)  38 us
    all_to_all x1, blocking collectives, gather_latents(): block = lax.all_to_all(copies, axis, 0, 0, tiled=True)  27.2 us
    ppermute x4, starting transfers between devices, swap(): return lax.ppermute(x, axis, [(i, i ^ bit) for i in range(SIZE[axis])])  23.1 us
    ppermute x4, waiting for transfers between devices, paired(): return lax.ppermute(x, axes, pairs)  16.6 us
    pallas_call x3, Pallas kernels, call(): pl.pallas_call(kernel, out_shape=shapes, in_specs=specs, out_specs=jax.tr...  12.3 us
    all_to_all x1, waiting for transfers between devices, body(): lax.all_to_all(lat_term.reshape(4, half, rows), 'section', 0, 0, tiled=True)  10.2 us
    unnamed x17, local copies, waits for them, and re-layouts  8.98 us
    all_to_all x1, waiting for transfers between devices, gather_latents(): block = lax.all_to_all(copies, axis, 0, 0, tiled=True)  8.92 us
  transfers between devices with their start and end apart: 10, of which 7 were waited for; matrix products, arithmetic and copies ran while one was open for 4% of the time, Pallas kernels for 2%

profile of v7, /device:TPU:120, one launch (start us, length us, event | category | flops | bytes accessed | tf_op | source)
XLA Modules:
  0.0 161.9 jit_solution(17810204110105459694)
XLA Ops:
  0.6 0.8 copy.9
  1.5 0.1 reshape.164
  1.6 27.2 %all_to_all.15 = bf16[8,48,384]{2,1,0:T(8,128)(2,1)S(1)} all-to-all(bf16[8,48,384]{2,1,0:T(8,128)(2,1)S(1)} %broadcast_in_dim.6), channel_id=1, replica_groups=mesh['zh'=4,'y'=4,'core'=2,'section'=4,'mp'=8] {'mp'}, dimensions={0} | all-to-all | bytes 589824 | tf_op jit(solution)/shard_map/all_to_all | solution.py:54
  28.8 1.1 broadcast_in_dim.14
  30.0 4.3 %all-to-all-start.1 = ((bf16[4,384,384]{2,1,0:T(8,128)(2,1)}), bf16[4,384,384]{2,1,0:T(8,128)(2,1)S(1)}, u32[]{:S(2)}, u32[]{:S(2)}) async-start(bf16[4,384,384]{2,1,0:T(8,128)(2,1)} %broadcast_in_dim.14), calls=%async_computation.1 | async-start | bytes 2359296 | tf_op jit(solution)/shard_map/all_to_all | solution.py:54
  34.6 4.4 %copy.11 = bf16[192,8,2,512]{3,1,2,0:T(8,128)(2,1)} copy(bf16[192,8,2,512]{3,2,1,0:T(2,128)(2,1)} %bitcast.41) | data formatting | bytes 6291456
  39.0 8.9 %all-to-all-done.1 = bf16[4,384,384]{2,1,0:T(8,128)(2,1)S(1)} async-done(((bf16[4,384,384]{2,1,0:T(8,128)(2,1)}), bf16[4,384,384]{2,1,0:T(8,128)(2,1)S(1)}, u32[]{:S(2)}, u32[]{:S(2)}) %all-to-all-start.1) | async-done | bytes 1179680 | tf_op jit(solution)/shard_map/all_to_all | solution.py:54
  48.0 1.9 %copy-done = bf16[192,8,2,512]{3,1,2,0:T(8,128)(2,1)S(1)} copy-done((bf16[192,8,2,512]{3,1,2,0:T(8,128)(2,1)S(1)}, bf16[192,8,2,512]{3,1,2,0:T(8,128)(2,1)}, u32[]{:S(2)}) %copy-start) | copy-done | bytes 3145752
  49.9 8.6 %shard_map.85 = (bf16[2,128,512]{2,1,0:T(8,128)(2,1)}, bf16[384,1024]{1,0:T(8,128)(2,1)S(1)}, bf16[768,1024]{1,0:T(8,128)(2,1)}, bf16[1536,384]{1,0:T(8,128)(2,1)}) custom-call(s32[2]{0:T(128)S(1)} %copy-done.6, s32[16]{0:T(128)S(1)} %add.109.blocks, bf16[1536,384]{1,0:T(8,128)(2,1)S(1)} %bitcast.35, bf16[1536,1024]{1,0:T(8,128)(2,1)S(1)} %bitcast.37, ...), custom_call_target="tpu_custom_call" | custom-call | flops 3019898880 | bytes 4850760 | tf_op jit(solution)/shard_map/pallas_call | solution.py:115
  58.4 1.9 %collective-permute-start = (bf16[768,1024]{1,0:T(8,128)(2,1)}, bf16[768,1024]{1,0:T(8,128)(2,1)}, u32[]{:S(2)}, u32[]{:S(2)}) collective-permute-start(bf16[768,1024]{1,0:T(8,128)(2,1)} %get-tuple-element.13), channel_id=1, source_target_pairs={{0,32},{32,0},{1,33},{33,1},{2,34},{34,2},{3,35},{35,3},{4,36},{36... | collective-permute-start | bytes 4718600 | tf_op jit(solution)/shard_map/ppermute | solution.py:47
  60.3 3.5 %all-to-all-start.2 = ((bf16[4,384,384]{2,1,0:T(8,128)(2,1)}), bf16[4,384,384]{2,1,0:T(8,128)(2,1)S(1)}, u32[]{:S(2)}, u32[]{:S(2)}) async-start(bf16[4,384,384]{2,1,0:T(8,128)(2,1)} %bitcast.15), calls=%async_computation.2 | async-start | bytes 2359296 | tf_op jit(solution)/shard_map/all_to_all | solution.py:173
  64.0 0.1 collective-permute-done.other
  64.1 3.1 %shard_map.86 = (f32[384,1024]{1,0:T(8,128)S(1)}, bf16[384,1024]{1,0:T(8,128)(2,1)}) custom-call(s32[16]{0:T(128)S(1)} %add.114.blocks, bf16[1536,384]{1,0:T(8,128)(2,1)S(1)} %bitcast.36, bf16[384,1024]{1,0:T(8,128)(2,1)S(1)} %get-tuple-element.12.dflat, bf16[768,1024]{1,0:T(8,128)(2,1)} %collective-permute-done.other), custom_call_target="tpu_custom_call" | custom-call | flops 603979776 | bytes 3539008 | tf_op jit(solution)/shard_map/pallas_call | solution.py:115
  67.1 1.2 copy-done.1
  68.3 2.8 %collective-permute-start.1 = (bf16[384,1024]{1,0:T(8,128)(2,1)}, bf16[384,1024]{1,0:T(8,128)(2,1)S(1)}, u32[]{:S(2)}, u32[]{:S(2)}) collective-permute-start(bf16[384,1024]{1,0:T(8,128)(2,1)} %get-tuple-element.15), channel_id=1, source_target_pairs={{0,64},{32,224},{64,0},{96,160},{128,192},{160,96},{192,128},{224,... | collective-permute-start | bytes 2359304 | tf_op jit(solution)/shard_map/ppermute | solution.py:43
  71.1 10.2 %all-to-all-done.2.parts = bf16[4,384,384]{2,1,0:T(8,128)(2,1)S(1)} async-done(((bf16[4,384,384]{2,1,0:T(8,128)(2,1)}), bf16[4,384,384]{2,1,0:T(8,128)(2,1)S(1)}, u32[]{:S(2)}, u32[]{:S(2)}) %all-to-all-start.2) | async-done | bytes 1179680 | tf_op jit(solution)/shard_map/all_to_all | solution.py:173
  81.3 0.7 shard_map.87
  82.0 3.4 %collective-permute-start.4 = (bf16[4,48,384]{2,1,0:T(8,128)(2,1)S(1)}, bf16[4,48,384]{2,1,0:T(8,128)(2,1)S(1)}, u32[]{:S(2)}, u32[]{:S(2)}) collective-permute-start(bf16[4,48,384]{2,1,0:T(8,128)(2,1)S(1)} %bitcast.44), channel_id=1, source_target_pairs={{0,1},{1,0},{2,3},{3,2},{4,5},{5,4},{6,7},{7,6},{8,9},{9,8},{10,11... | collective-permute-start | bytes 442376 | tf_op jit(solution)/shard_map/ppermute | solution.py:47
  85.5 0.2 convert_add_fusion
  85.8 2.1 %collective-permute-start.2 = (bf16[192,1024]{1,0:T(8,128)(2,1)S(1)}, bf16[192,1024]{1,0:T(8,128)(2,1)S(1)}, u32[]{:S(2)}, u32[]{:S(2)}) collective-permute-start(bf16[192,1024]{1,0:T(8,128)(2,1)S(1)} %slice.94), channel_id=1, source_target_pairs={{0,192},{32,96},{64,128},{96,32},{128,64},{160,224},{192,0},{224,1... | collective-permute-start | bytes 1179656 | tf_op jit(solution)/shard_map/ppermute | solution.py:43
  88.0 1.4 collective-permute-done.4
  89.4 5.8 %collective-permute-start.5 = (bf16[2,48,384]{2,1,0:T(8,128)(2,1)S(1)}, bf16[2,48,384]{2,1,0:T(8,128)(2,1)S(1)}, u32[]{:S(2)}, u32[]{:S(2)}) collective-permute-start(bf16[2,48,384]{2,1,0:T(8,128)(2,1)S(1)} %slice.98), channel_id=1, source_target_pairs={{0,2},{1,3},{2,0},{3,1},{4,6},{5,7},{6,4},{7,5},{8,10},{9,11},{10,... | collective-permute-start | bytes 221192 | tf_op jit(solution)/shard_map/ppermute | solution.py:47
  95.3 3.1 %collective-permute-done.5 = bf16[2,48,384]{2,1,0:T(8,128)(2,1)S(1)} collective-permute-done((bf16[2,48,384]{2,1,0:T(8,128)(2,1)S(1)}, bf16[2,48,384]{2,1,0:T(8,128)(2,1)S(1)}, u32[]{:S(2)}, u32[]{:S(2)}) %collective-permute-start.5) | collective-permute-done | bytes 73760 | tf_op jit(solution)/shard_map/ppermute | solution.py:47
  98.4 0.1 slice_add_fusion
  98.5 15.5 %collective-permute-start.3 = (bf16[96,1024]{1,0:T(8,128)(2,1)S(1)}, bf16[96,1024]{1,0:T(8,128)(2,1)S(1)}, u32[]{:S(2)}, u32[]{:S(2)}) collective-permute-start(bf16[96,1024]{1,0:T(8,128)(2,1)S(1)} %slice.95), channel_id=1, source_target_pairs={{0,256},{1,769},{2,258},{3,771},{4,260},{5,773},{6,262},{7,775},{2... | collective-permute-start | bytes 589832 | tf_op jit(solution)/shard_map/ppermute | solution.py:43
  114.1 9.3 %collective-permute-done.3 = bf16[96,1024]{1,0:T(8,128)(2,1)S(1)} collective-permute-done((bf16[96,1024]{1,0:T(8,128)(2,1)S(1)}, bf16[96,1024]{1,0:T(8,128)(2,1)S(1)}, u32[]{:S(2)}, u32[]{:S(2)}) %collective-permute-start.3) | collective-permute-done | bytes 196640 | tf_op jit(solution)/shard_map/ppermute | solution.py:43
  123.4 11.9 %collective-permute-start.7 = (bf16[48,384]{1,0:T(8,128)(2,1)S(1)}, bf16[48,384]{1,0:T(8,128)(2,1)S(1)}, u32[]{:S(2)}, u32[]{:S(2)}) collective-permute-start(bf16[48,384]{1,0:T(8,128)(2,1)S(1)} %fusion.2), channel_id=1, source_target_pairs={{0,4},{1,5},{2,6},{3,7},{4,0},{5,1},{6,2},{7,3},{8,12},{9,13},{10,... | collective-permute-start | bytes 110600 | tf_op jit(solution)/shard_map/ppermute | solution.py:47
  135.4 17.6 %collective-permute-start.6 = (bf16[48,1024]{1,0:T(8,128)(2,1)S(1)}, bf16[48,1024]{1,0:T(8,128)(2,1)S(1)}, u32[]{:S(2)}, u32[]{:S(2)}) collective-permute-start(bf16[48,1024]{1,0:T(8,128)(2,1)S(1)} %slice.97), channel_id=1, source_target_pairs={{0,768},{1,257},{2,770},{3,259},{4,772},{5,261},{6,774},{7,263},{2... | collective-permute-start | bytes 294920 | tf_op jit(solution)/shard_map/ppermute | solution.py:43
  153.0 0.1 reshape.171
  153.1 0.6 copy.10
  153.8 7.3 %collective-permute-done.6 = bf16[48,1024]{1,0:T(8,128)(2,1)S(1)} collective-permute-done((bf16[48,1024]{1,0:T(8,128)(2,1)S(1)}, bf16[48,1024]{1,0:T(8,128)(2,1)S(1)}, u32[]{:S(2)}, u32[]{:S(2)}) %collective-permute-start.6) | collective-permute-done | bytes 98336 | tf_op jit(solution)/shard_map/ppermute | solution.py:43
  161.1 0.8 reshape.170
  (34 shorter events, 0.8 us)
Async XLA Ops:
  30.0 18.0 %all-to-all-start.1 = ((bf16[4,384,384]{2,1,0:T(8,128)(2,1)}), bf16[4,384,384]{2,1,0:T(8,128)(2,1)S(1)}, u32[]{:S(2)}, u32[]{:S(2)}) async-start(bf16[4,384,384]{2,1,0:T(8,128)(2,1)} %broadcast_in_dim.14), calls=%async_computation.1 | async-start | bytes 2359296 | tf_op jit(solution)/shard_map/all_to_all | solution.py:54
  34.6 13.4 %copy-start.3 = (bf16[1,2,128,512]{3,2,1,0:T(8,128)(2,1)S(1)}, bf16[1,2,128,512]{3,2,1,0:T(8,128)(2,1)}, u32[]{:S(2)}) copy-start(bf16[1,2,128,512]{3,2,1,0:T(8,128)(2,1)} %param.6) | copy-start | bytes 786436
  34.6 13.4 %copy-start.4 = (bf16[1,2,128,512]{3,2,1,0:T(8,128)(2,1)S(1)}, bf16[1,2,128,512]{3,2,1,0:T(8,128)(2,1)}, u32[]{:S(2)}) copy-start(bf16[1,2,128,512]{3,2,1,0:T(8,128)(2,1)} %param.11) | copy-start | bytes 786436
  34.6 13.4 %copy-start.5 = (s32[2,128]{1,0:T(2,128)S(1)}, s32[2,128]{1,0:T(2,128)}, u32[]{:S(2)}) copy-start(s32[2,128]{1,0:T(2,128)} %param.9) | copy-start | bytes 3076
  34.6 13.4 %copy-start.6 = (s32[2]{0:T(128)S(1)}, s32[2]{0:T(128)}, u32[]{:S(2)}) copy-start(s32[2]{0:T(128)} %counts.1) | copy-start | bytes 28
  48.0 1.9 %copy-start = (bf16[192,8,2,512]{3,1,2,0:T(8,128)(2,1)S(1)}, bf16[192,8,2,512]{3,1,2,0:T(8,128)(2,1)}, u32[]{:S(2)}) copy-start(bf16[192,8,2,512]{3,1,2,0:T(8,128)(2,1)} %copy.11) | copy-start | bytes 9437188
  58.4 5.6 %collective-permute-start = (bf16[768,1024]{1,0:T(8,128)(2,1)}, bf16[768,1024]{1,0:T(8,128)(2,1)}, u32[]{:S(2)}, u32[]{:S(2)}) collective-permute-start(bf16[768,1024]{1,0:T(8,128)(2,1)} %get-tuple-element.13), channel_id=1, source_target_pairs={{0,32},{32,0},{1,33},{33,1},{2,34},{34,2},{3,35},{35,3},{4,36},{36... | collective-permute-start | bytes 4718600 | tf_op jit(solution)/shard_map/ppermute | solution.py:47
  60.3 21.0 %all-to-all-start.2 = ((bf16[4,384,384]{2,1,0:T(8,128)(2,1)}), bf16[4,384,384]{2,1,0:T(8,128)(2,1)S(1)}, u32[]{:S(2)}, u32[]{:S(2)}) async-start(bf16[4,384,384]{2,1,0:T(8,128)(2,1)} %bitcast.15), calls=%async_computation.2 | async-start | bytes 2359296 | tf_op jit(solution)/shard_map/all_to_all | solution.py:173
  67.1 1.2 copy-start.1
  68.3 17.2 %copy-start.2 = (f32[384,1024]{1,0:T(8,128)S(1)}, f32[384,1024]{1,0:T(8,128)}, u32[]{:S(2)}) copy-start(f32[384,1024]{1,0:T(8,128)} %copy-done.1) | copy-start | bytes 4718596
  68.3 17.2 %collective-permute-start.1 = (bf16[384,1024]{1,0:T(8,128)(2,1)}, bf16[384,1024]{1,0:T(8,128)(2,1)S(1)}, u32[]{:S(2)}, u32[]{:S(2)}) collective-permute-start(bf16[384,1024]{1,0:T(8,128)(2,1)} %get-tuple-element.15), channel_id=1, source_target_pairs={{0,64},{32,224},{64,0},{96,160},{128,192},{160,96},{192,128},{224,... | collective-permute-start | bytes 2359304 | tf_op jit(solution)/shard_map/ppermute | solution.py:43
  82.0 7.4 %collective-permute-start.4 = (bf16[4,48,384]{2,1,0:T(8,128)(2,1)S(1)}, bf16[4,48,384]{2,1,0:T(8,128)(2,1)S(1)}, u32[]{:S(2)}, u32[]{:S(2)}) collective-permute-start(bf16[4,48,384]{2,1,0:T(8,128)(2,1)S(1)} %bitcast.44), channel_id=1, source_target_pairs={{0,1},{1,0},{2,3},{3,2},{4,5},{5,4},{6,7},{7,6},{8,9},{9,8},{10,11... | collective-permute-start | bytes 442376 | tf_op jit(solution)/shard_map/ppermute | solution.py:47
  85.8 12.6 %collective-permute-start.2 = (bf16[192,1024]{1,0:T(8,128)(2,1)S(1)}, bf16[192,1024]{1,0:T(8,128)(2,1)S(1)}, u32[]{:S(2)}, u32[]{:S(2)}) collective-permute-start(bf16[192,1024]{1,0:T(8,128)(2,1)S(1)} %slice.94), channel_id=1, source_target_pairs={{0,192},{32,96},{64,128},{96,32},{128,64},{160,224},{192,0},{224,1... | collective-permute-start | bytes 1179656 | tf_op jit(solution)/shard_map/ppermute | solution.py:43
  89.4 8.9 %collective-permute-start.5 = (bf16[2,48,384]{2,1,0:T(8,128)(2,1)S(1)}, bf16[2,48,384]{2,1,0:T(8,128)(2,1)S(1)}, u32[]{:S(2)}, u32[]{:S(2)}) collective-permute-start(bf16[2,48,384]{2,1,0:T(8,128)(2,1)S(1)} %slice.98), channel_id=1, source_target_pairs={{0,2},{1,3},{2,0},{3,1},{4,6},{5,7},{6,4},{7,5},{8,10},{9,11},{10,... | collective-permute-start | bytes 221192 | tf_op jit(solution)/shard_map/ppermute | solution.py:47
  98.5 24.8 %collective-permute-start.3 = (bf16[96,1024]{1,0:T(8,128)(2,1)S(1)}, bf16[96,1024]{1,0:T(8,128)(2,1)S(1)}, u32[]{:S(2)}, u32[]{:S(2)}) collective-permute-start(bf16[96,1024]{1,0:T(8,128)(2,1)S(1)} %slice.95), channel_id=1, source_target_pairs={{0,256},{1,769},{2,258},{3,771},{4,260},{5,773},{6,262},{7,775},{2... | collective-permute-start | bytes 589832 | tf_op jit(solution)/shard_map/ppermute | solution.py:43
  123.4 29.6 %collective-permute-start.7 = (bf16[48,384]{1,0:T(8,128)(2,1)S(1)}, bf16[48,384]{1,0:T(8,128)(2,1)S(1)}, u32[]{:S(2)}, u32[]{:S(2)}) collective-permute-start(bf16[48,384]{1,0:T(8,128)(2,1)S(1)} %fusion.2), channel_id=1, source_target_pairs={{0,4},{1,5},{2,6},{3,7},{4,0},{5,1},{6,2},{7,3},{8,12},{9,13},{10,... | collective-permute-start | bytes 110600 | tf_op jit(solution)/shard_map/ppermute | solution.py:47
  135.4 25.7 %collective-permute-start.6 = (bf16[48,1024]{1,0:T(8,128)(2,1)S(1)}, bf16[48,1024]{1,0:T(8,128)(2,1)S(1)}, u32[]{:S(2)}, u32[]{:S(2)}) collective-permute-start(bf16[48,1024]{1,0:T(8,128)(2,1)S(1)} %slice.97), channel_id=1, source_target_pairs={{0,768},{1,257},{2,770},{3,259},{4,772},{5,261},{6,774},{7,263},{2... | collective-permute-start | bytes 294920 | tf_op jit(solution)/shard_map/ppermute | solution.py:43

commit v8 on v7

--- a/solution.py
+++ b/solution.py
@@ -24,7 +24,7 @@
     return lax.dot_general(a, b, dims, preferred_element_type=f32)
 
 
-PARITY = {"y": "core", "section": "core", "zh": "mp"}
+PARITY = {"y": "core", "section": "core", "zh": "core"}
 
 
 def relative(axis):
@@ -132,12 +132,13 @@
     lat = gather_latents(latents.reshape(rows, depth).T)
 
     half, cols = width // 4, 2 * local
-    zs = jnp.stack(relative("zh"))
-
-    def blocks(at_core, ys):
-        return (zs[None, :] * 8 + jnp.stack(ys)[:, None] * 2 + at_core).reshape(-1).astype(jnp.int32)
-
-    mine, second, first, both = relative("y")
+
+    def blocks(at_core, zs, ys):
+        zs, ys = jnp.stack(zs), jnp.stack(ys)
+        return (zs[None, :] * 8 + ys[:, None] * 2 + at_core).reshape(-1).astype(jnp.int32)
+
+    own_order = relative("zh"), relative("y")
+    other_order = [[mine, first, second, both] for mine, second, first, both in own_order]
     picked = pltpu.VMEM((2 * half, rows), bf16)
     attended, dflat, grad_send, lat_term = call(
         functools.partial(main_kernel, keys, depth),
@@ -151,7 +152,7 @@
         [pltpu.VMEM((rows, cols), bf16), picked],
         5 * rows * width * cols,
         image_counts,
-        blocks(1 - core, [mine, first, second, both]),
+        blocks(1 - core, *other_order),
         lat,
         weight,
         queries[0],
@@ -164,7 +165,7 @@
         (jax.ShapeDtypeStruct((half, cols), f32), jax.ShapeDtypeStruct((half, cols), bf16)),
         [picked],
         width * rows * cols,
-        blocks(core, [mine, second, first, both]),
+        blocks(core, *own_order),
         lat,
         dflat,
         swap(grad_send, "core", 1),

time: 163 us -> 160 us (0.982)
  the two profiles are of different devices: /device:TPU:120 before, /device:TPU:16 now
where the time goes in v8:
time: 160 us; the launch traced here: 159 us
  waiting for transfers between devices  52.9 us (33%)
  starting transfers between devices  49.5 us (31%)
  blocking collectives  31.2 us (20%)
  Pallas kernels  12.3 us (8%)
  local copies, waits for them, and re-layouts  11.5 us (7%)
    all_to_all x1, blocking collectives, gather_latents(): block = lax.all_to_all(copies, axis, 0, 0, tiled=True)  31.2 us
    ppermute x4, starting transfers between devices, paired(): return lax.ppermute(x, axes, pairs)  29.1 us
    ppermute x4, waiting for transfers between devices, paired(): return lax.ppermute(x, axes, pairs)  28.3 us
    ppermute x4, starting transfers between devices, swap(): return lax.ppermute(x, axis, [(i, i ^ bit) for i in range(SIZE[axis])])  12.6 us
    pallas_call x3, Pallas kernels, call(): pl.pallas_call(kernel, out_shape=shapes, in_specs=specs, out_specs=jax.tr...  12.3 us
    all_to_all x1, waiting for transfers between devices, body(): lax.all_to_all(lat_term.reshape(4, half, rows), 'section', 0, 0, tiled=True)  9.64 us
    unnamed x17, local copies, waits for them, and re-layouts  8.98 us
    all_to_all x1, waiting for transfers between devices, gather_latents(): block = lax.all_to_all(copies, axis, 0, 0, tiled=True)  8.88 us
  transfers between devices with their start and end apart: 10, of which 6 were waited for; matrix products, arithmetic and copies ran while one was open for 4% of the time, Pallas kernels for 2%

profile of v8, /device:TPU:16, one launch (start us, length us, event | category | flops | bytes accessed | tf_op | source)
XLA Modules:
  0.0 159.1 jit_solution(13748789644219090585)
XLA Ops:
  0.6 0.8 copy.9
  1.5 0.1 reshape.198
  1.6 31.2 %all_to_all.15 = bf16[8,48,384]{2,1,0:T(8,128)(2,1)S(1)} all-to-all(bf16[8,48,384]{2,1,0:T(8,128)(2,1)S(1)} %broadcast_in_dim.6), channel_id=1, replica_groups=mesh['zh'=4,'y'=4,'core'=2,'section'=4,'mp'=8] {'mp'}, dimensions={0} | all-to-all | bytes 589824 | tf_op jit(solution)/shard_map/all_to_all | solution.py:54
  32.8 1.1 broadcast_in_dim.14
  34.0 4.3 %all-to-all-start.1 = ((bf16[4,384,384]{2,1,0:T(8,128)(2,1)}), bf16[4,384,384]{2,1,0:T(8,128)(2,1)S(1)}, u32[]{:S(2)}, u32[]{:S(2)}) async-start(bf16[4,384,384]{2,1,0:T(8,128)(2,1)} %broadcast_in_dim.14), calls=%async_computation.1 | async-start | bytes 2359296 | tf_op jit(solution)/shard_map/all_to_all | solution.py:54
  38.5 0.1 add.105.blocks
  38.6 4.4 %copy.11 = bf16[192,8,2,512]{3,1,2,0:T(8,128)(2,1)} copy(bf16[192,8,2,512]{3,2,1,0:T(2,128)(2,1)} %bitcast.41) | data formatting | bytes 6291456
  43.0 8.9 %all-to-all-done.1 = bf16[4,384,384]{2,1,0:T(8,128)(2,1)S(1)} async-done(((bf16[4,384,384]{2,1,0:T(8,128)(2,1)}), bf16[4,384,384]{2,1,0:T(8,128)(2,1)S(1)}, u32[]{:S(2)}, u32[]{:S(2)}) %all-to-all-start.1) | async-done | bytes 1179680 | tf_op jit(solution)/shard_map/all_to_all | solution.py:54
  52.0 1.9 %copy-done = bf16[192,8,2,512]{3,1,2,0:T(8,128)(2,1)S(1)} copy-done((bf16[192,8,2,512]{3,1,2,0:T(8,128)(2,1)S(1)}, bf16[192,8,2,512]{3,1,2,0:T(8,128)(2,1)}, u32[]{:S(2)}) %copy-start) | copy-done | bytes 3145752
  53.8 8.6 %shard_map.85 = (bf16[2,128,512]{2,1,0:T(8,128)(2,1)}, bf16[384,1024]{1,0:T(8,128)(2,1)S(1)}, bf16[768,1024]{1,0:T(8,128)(2,1)}, bf16[1536,384]{1,0:T(8,128)(2,1)}) custom-call(s32[2]{0:T(128)S(1)} %copy-done.6, s32[16]{0:T(128)S(1)} %add.105.blocks, bf16[1536,384]{1,0:T(8,128)(2,1)S(1)} %bitcast.35, bf16[1536,1024]{1,0:T(8,128)(2,1)S(1)} %bitcast.37, ...), custom_call_target="tpu_custom_call" | custom-call | flops 3019898880 | bytes 4850760 | tf_op jit(solution)/shard_map/pallas_call | solution.py:115
  62.4 1.9 %collective-permute-start = (bf16[768,1024]{1,0:T(8,128)(2,1)}, bf16[768,1024]{1,0:T(8,128)(2,1)}, u32[]{:S(2)}, u32[]{:S(2)}) collective-permute-start(bf16[768,1024]{1,0:T(8,128)(2,1)} %get-tuple-element.13), channel_id=1, source_target_pairs={{0,32},{32,0},{1,33},{33,1},{2,34},{34,2},{3,35},{35,3},{4,36},{36... | collective-permute-start | bytes 4718600 | tf_op jit(solution)/shard_map/ppermute | solution.py:47
  64.3 3.5 %all-to-all-start.2 = ((bf16[4,384,384]{2,1,0:T(8,128)(2,1)}), bf16[4,384,384]{2,1,0:T(8,128)(2,1)S(1)}, u32[]{:S(2)}, u32[]{:S(2)}) async-start(bf16[4,384,384]{2,1,0:T(8,128)(2,1)} %bitcast.15), calls=%async_computation.2 | async-start | bytes 2359296 | tf_op jit(solution)/shard_map/all_to_all | solution.py:174
  68.0 3.1 %shard_map.86 = (f32[384,1024]{1,0:T(8,128)S(1)}, bf16[384,1024]{1,0:T(8,128)(2,1)}) custom-call(s32[16]{0:T(128)S(1)} %add.111.blocks, bf16[1536,384]{1,0:T(8,128)(2,1)S(1)} %bitcast.36, bf16[384,1024]{1,0:T(8,128)(2,1)S(1)} %get-tuple-element.12.dflat, bf16[768,1024]{1,0:T(8,128)(2,1)} %collective-permute-done.other), custom_call_target="tpu_custom_call" | custom-call | flops 603979776 | bytes 3539008 | tf_op jit(solution)/shard_map/pallas_call | solution.py:115
  71.1 1.2 copy-done.1
  72.3 3.3 %collective-permute-start.1 = (bf16[384,1024]{1,0:T(8,128)(2,1)}, bf16[384,1024]{1,0:T(8,128)(2,1)S(1)}, u32[]{:S(2)}, u32[]{:S(2)}) collective-permute-start(bf16[384,1024]{1,0:T(8,128)(2,1)} %get-tuple-element.15), channel_id=1, source_target_pairs={{0,64},{32,224},{64,0},{96,160},{128,192},{160,96},{192,128},{224,... | collective-permute-start | bytes 2359304 | tf_op jit(solution)/shard_map/ppermute | solution.py:43
  75.6 9.6 %all-to-all-done.2.parts = bf16[4,384,384]{2,1,0:T(8,128)(2,1)S(1)} async-done(((bf16[4,384,384]{2,1,0:T(8,128)(2,1)}), bf16[4,384,384]{2,1,0:T(8,128)(2,1)S(1)}, u32[]{:S(2)}, u32[]{:S(2)}) %all-to-all-start.2) | async-done | bytes 1179680 | tf_op jit(solution)/shard_map/all_to_all | solution.py:174
  85.3 0.7 shard_map.87
  86.0 4.1 %collective-permute-start.4 = (bf16[4,48,384]{2,1,0:T(8,128)(2,1)S(1)}, bf16[4,48,384]{2,1,0:T(8,128)(2,1)S(1)}, u32[]{:S(2)}, u32[]{:S(2)}) collective-permute-start(bf16[4,48,384]{2,1,0:T(8,128)(2,1)S(1)} %bitcast.44), channel_id=1, source_target_pairs={{0,1},{1,0},{2,3},{3,2},{4,5},{5,4},{6,7},{7,6},{8,9},{9,8},{10,11... | collective-permute-start | bytes 442376 | tf_op jit(solution)/shard_map/ppermute | solution.py:47
  90.2 0.2 convert_add_fusion
  90.5 2.4 %collective-permute-start.2 = (bf16[192,1024]{1,0:T(8,128)(2,1)S(1)}, bf16[192,1024]{1,0:T(8,128)(2,1)S(1)}, u32[]{:S(2)}, u32[]{:S(2)}) collective-permute-start(bf16[192,1024]{1,0:T(8,128)(2,1)S(1)} %slice.94), channel_id=1, source_target_pairs={{0,192},{32,96},{64,128},{96,32},{128,64},{160,224},{192,0},{224,1... | collective-permute-start | bytes 1179656 | tf_op jit(solution)/shard_map/ppermute | solution.py:43
  92.8 1.0 collective-permute-done.4
  93.9 2.1 %collective-permute-start.5 = (bf16[2,48,384]{2,1,0:T(8,128)(2,1)S(1)}, bf16[2,48,384]{2,1,0:T(8,128)(2,1)S(1)}, u32[]{:S(2)}, u32[]{:S(2)}) collective-permute-start(bf16[2,48,384]{2,1,0:T(8,128)(2,1)S(1)} %slice.98), channel_id=1, source_target_pairs={{0,2},{1,3},{2,0},{3,1},{4,6},{5,7},{6,4},{7,5},{8,10},{9,11},{10,... | collective-permute-start | bytes 221192 | tf_op jit(solution)/shard_map/ppermute | solution.py:47
  96.1 5.0 %collective-permute-done.5 = bf16[2,48,384]{2,1,0:T(8,128)(2,1)S(1)} collective-permute-done((bf16[2,48,384]{2,1,0:T(8,128)(2,1)S(1)}, bf16[2,48,384]{2,1,0:T(8,128)(2,1)S(1)}, u32[]{:S(2)}, u32[]{:S(2)}) %collective-permute-start.5) | collective-permute-done | bytes 73760 | tf_op jit(solution)/shard_map/ppermute | solution.py:47
  101.1 0.1 slice_add_fusion
  101.2 15.7 %collective-permute-start.3 = (bf16[96,1024]{1,0:T(8,128)(2,1)S(1)}, bf16[96,1024]{1,0:T(8,128)(2,1)S(1)}, u32[]{:S(2)}, u32[]{:S(2)}) collective-permute-start(bf16[96,1024]{1,0:T(8,128)(2,1)S(1)} %slice.95), channel_id=1, source_target_pairs={{0,256},{32,800},{256,0},{288,544},{512,768},{544,288},{768,512},{... | collective-permute-start | bytes 589832 | tf_op jit(solution)/shard_map/ppermute | solution.py:43
  117.0 18.3 %collective-permute-done.3 = bf16[96,1024]{1,0:T(8,128)(2,1)S(1)} collective-permute-done((bf16[96,1024]{1,0:T(8,128)(2,1)S(1)}, bf16[96,1024]{1,0:T(8,128)(2,1)S(1)}, u32[]{:S(2)}, u32[]{:S(2)}) %collective-permute-start.3) | collective-permute-done | bytes 196640 | tf_op jit(solution)/shard_map/ppermute | solution.py:43
  135.4 4.4 %collective-permute-start.7 = (bf16[48,384]{1,0:T(8,128)(2,1)S(1)}, bf16[48,384]{1,0:T(8,128)(2,1)S(1)}, u32[]{:S(2)}, u32[]{:S(2)}) collective-permute-start(bf16[48,384]{1,0:T(8,128)(2,1)S(1)} %fusion.2), channel_id=1, source_target_pairs={{0,4},{1,5},{2,6},{3,7},{4,0},{5,1},{6,2},{7,3},{8,12},{9,13},{10,... | collective-permute-start | bytes 110600 | tf_op jit(solution)/shard_map/ppermute | solution.py:47
  139.8 7.7 %collective-permute-start.6 = (bf16[48,1024]{1,0:T(8,128)(2,1)S(1)}, bf16[48,1024]{1,0:T(8,128)(2,1)S(1)}, u32[]{:S(2)}, u32[]{:S(2)}) collective-permute-start(bf16[48,1024]{1,0:T(8,128)(2,1)S(1)} %slice.97), channel_id=1, source_target_pairs={{0,768},{32,288},{256,512},{288,32},{512,256},{544,800},{768,0},{8... | collective-permute-start | bytes 294920 | tf_op jit(solution)/shard_map/ppermute | solution.py:43
  147.5 0.1 reshape.205
  147.6 0.6 copy.10
  148.2 10.0 %collective-permute-done.6 = bf16[48,1024]{1,0:T(8,128)(2,1)S(1)} collective-permute-done((bf16[48,1024]{1,0:T(8,128)(2,1)S(1)}, bf16[48,1024]{1,0:T(8,128)(2,1)S(1)}, u32[]{:S(2)}, u32[]{:S(2)}) %collective-permute-start.6) | collective-permute-done | bytes 98336 | tf_op jit(solution)/shard_map/ppermute | solution.py:43
  158.3 0.8 reshape.204
  (35 shorter events, 0.8 us)
Async XLA Ops:
  34.0 17.9 %all-to-all-start.1 = ((bf16[4,384,384]{2,1,0:T(8,128)(2,1)}), bf16[4,384,384]{2,1,0:T(8,128)(2,1)S(1)}, u32[]{:S(2)}, u32[]{:S(2)}) async-start(bf16[4,384,384]{2,1,0:T(8,128)(2,1)} %broadcast_in_dim.14), calls=%async_computation.1 | async-start | bytes 2359296 | tf_op jit(solution)/shard_map/all_to_all | solution.py:54
  38.6 13.3 %copy-start.3 = (bf16[1,2,128,512]{3,2,1,0:T(8,128)(2,1)S(1)}, bf16[1,2,128,512]{3,2,1,0:T(8,128)(2,1)}, u32[]{:S(2)}) copy-start(bf16[1,2,128,512]{3,2,1,0:T(8,128)(2,1)} %param.6) | copy-start | bytes 786436
  38.6 13.3 %copy-start.4 = (bf16[1,2,128,512]{3,2,1,0:T(8,128)(2,1)S(1)}, bf16[1,2,128,512]{3,2,1,0:T(8,128)(2,1)}, u32[]{:S(2)}) copy-start(bf16[1,2,128,512]{3,2,1,0:T(8,128)(2,1)} %param.11) | copy-start | bytes 786436
  38.6 13.3 %copy-start.5 = (s32[2,128]{1,0:T(2,128)S(1)}, s32[2,128]{1,0:T(2,128)}, u32[]{:S(2)}) copy-start(s32[2,128]{1,0:T(2,128)} %param.9) | copy-start | bytes 3076
  38.6 13.3 %copy-start.6 = (s32[2]{0:T(128)S(1)}, s32[2]{0:T(128)}, u32[]{:S(2)}) copy-start(s32[2]{0:T(128)} %counts.1) | copy-start | bytes 28
  51.9 1.9 %copy-start = (bf16[192,8,2,512]{3,1,2,0:T(8,128)(2,1)S(1)}, bf16[192,8,2,512]{3,1,2,0:T(8,128)(2,1)}, u32[]{:S(2)}) copy-start(bf16[192,8,2,512]{3,1,2,0:T(8,128)(2,1)} %copy.11) | copy-start | bytes 9437188
  62.4 5.6 %collective-permute-start = (bf16[768,1024]{1,0:T(8,128)(2,1)}, bf16[768,1024]{1,0:T(8,128)(2,1)}, u32[]{:S(2)}, u32[]{:S(2)}) collective-permute-start(bf16[768,1024]{1,0:T(8,128)(2,1)} %get-tuple-element.13), channel_id=1, source_target_pairs={{0,32},{32,0},{1,33},{33,1},{2,34},{34,2},{3,35},{35,3},{4,36},{36... | collective-permute-start | bytes 4718600 | tf_op jit(solution)/shard_map/ppermute | solution.py:47
  64.3 21.0 %all-to-all-start.2 = ((bf16[4,384,384]{2,1,0:T(8,128)(2,1)}), bf16[4,384,384]{2,1,0:T(8,128)(2,1)S(1)}, u32[]{:S(2)}, u32[]{:S(2)}) async-start(bf16[4,384,384]{2,1,0:T(8,128)(2,1)} %bitcast.15), calls=%async_computation.2 | async-start | bytes 2359296 | tf_op jit(solution)/shard_map/all_to_all | solution.py:174
  71.1 1.2 copy-start.1
  72.3 17.9 %copy-start.2 = (f32[384,1024]{1,0:T(8,128)S(1)}, f32[384,1024]{1,0:T(8,128)}, u32[]{:S(2)}) copy-start(f32[384,1024]{1,0:T(8,128)} %copy-done.1) | copy-start | bytes 4718596
  72.3 17.9 %collective-permute-start.1 = (bf16[384,1024]{1,0:T(8,128)(2,1)}, bf16[384,1024]{1,0:T(8,128)(2,1)S(1)}, u32[]{:S(2)}, u32[]{:S(2)}) collective-permute-start(bf16[384,1024]{1,0:T(8,128)(2,1)} %get-tuple-element.15), channel_id=1, source_target_pairs={{0,64},{32,224},{64,0},{96,160},{128,192},{160,96},{192,128},{224,... | collective-permute-start | bytes 2359304 | tf_op jit(solution)/shard_map/ppermute | solution.py:43
  86.0 7.9 %collective-permute-start.4 = (bf16[4,48,384]{2,1,0:T(8,128)(2,1)S(1)}, bf16[4,48,384]{2,1,0:T(8,128)(2,1)S(1)}, u32[]{:S(2)}, u32[]{:S(2)}) collective-permute-start(bf16[4,48,384]{2,1,0:T(8,128)(2,1)S(1)} %bitcast.44), channel_id=1, source_target_pairs={{0,1},{1,0},{2,3},{3,2},{4,5},{5,4},{6,7},{7,6},{8,9},{9,8},{10,11... | collective-permute-start | bytes 442376 | tf_op jit(solution)/shard_map/ppermute | solution.py:47
  90.5 10.6 %collective-permute-start.2 = (bf16[192,1024]{1,0:T(8,128)(2,1)S(1)}, bf16[192,1024]{1,0:T(8,128)(2,1)S(1)}, u32[]{:S(2)}, u32[]{:S(2)}) collective-permute-start(bf16[192,1024]{1,0:T(8,128)(2,1)S(1)} %slice.94), channel_id=1, source_target_pairs={{0,192},{32,96},{64,128},{96,32},{128,64},{160,224},{192,0},{224,1... | collective-permute-start | bytes 1179656 | tf_op jit(solution)/shard_map/ppermute | solution.py:43
  93.9 7.1 %collective-permute-start.5 = (bf16[2,48,384]{2,1,0:T(8,128)(2,1)S(1)}, bf16[2,48,384]{2,1,0:T(8,128)(2,1)S(1)}, u32[]{:S(2)}, u32[]{:S(2)}) collective-permute-start(bf16[2,48,384]{2,1,0:T(8,128)(2,1)S(1)} %slice.98), channel_id=1, source_target_pairs={{0,2},{1,3},{2,0},{3,1},{4,6},{5,7},{6,4},{7,5},{8,10},{9,11},{10,... | collective-permute-start | bytes 221192 | tf_op jit(solution)/shard_map/ppermute | solution.py:47
  101.2 34.0 %collective-permute-start.3 = (bf16[96,1024]{1,0:T(8,128)(2,1)S(1)}, bf16[96,1024]{1,0:T(8,128)(2,1)S(1)}, u32[]{:S(2)}, u32[]{:S(2)}) collective-permute-start(bf16[96,1024]{1,0:T(8,128)(2,1)S(1)} %slice.95), channel_id=1, source_target_pairs={{0,256},{32,800},{256,0},{288,544},{512,768},{544,288},{768,512},{... | collective-permute-start | bytes 589832 | tf_op jit(solution)/shard_map/ppermute | solution.py:43
  135.4 12.1 %collective-permute-start.7 = (bf16[48,384]{1,0:T(8,128)(2,1)S(1)}, bf16[48,384]{1,0:T(8,128)(2,1)S(1)}, u32[]{:S(2)}, u32[]{:S(2)}) collective-permute-start(bf16[48,384]{1,0:T(8,128)(2,1)S(1)} %fusion.2), channel_id=1, source_target_pairs={{0,4},{1,5},{2,6},{3,7},{4,0},{5,1},{6,2},{7,3},{8,12},{9,13},{10,... | collective-permute-start | bytes 110600 | tf_op jit(solution)/shard_map/ppermute | solution.py:47
  139.8 18.5 %collective-permute-start.6 = (bf16[48,1024]{1,0:T(8,128)(2,1)S(1)}, bf16[48,1024]{1,0:T(8,128)(2,1)S(1)}, u32[]{:S(2)}, u32[]{:S(2)}) collective-permute-start(bf16[48,1024]{1,0:T(8,128)(2,1)S(1)} %slice.97), channel_id=1, source_target_pairs={{0,768},{32,288},{256,512},{288,32},{512,256},{544,800},{768,0},{8... | collective-permute-start | bytes 294920 | tf_op jit(solution)/shard_map/ppermute | solution.py:43

commit v9 on v8

--- a/solution.py
+++ b/solution.py
@@ -191,10 +191,8 @@
 
     grad = (grad[0] + paired(send, "zh", True).astype(f32)).reshape(2, -1, cols)
     lat_sum = lat_sum[:2] + swap(lat_sum[2:].astype(bf16), "mp", 2).astype(f32)
-    last = lat_sum[1].astype(bf16)
-    send, last = lax.optimization_barrier((grad[1].astype(bf16), last))
-    kv_grad = grad[0] + paired(send, "zh", False).astype(f32)
-    lat_sum = lat_sum[0] + swap(last, "mp", 4).astype(f32)
+    kv_grad = grad[0] + paired(grad[1].astype(bf16), "zh", False).astype(f32)
+    lat_sum = lat_sum[0] + swap(lat_sum[1].astype(bf16), "mp", 4).astype(f32)
     return (
         attended[None],
         kv_grad.reshape(1, depth, 2, local),

time: 160 us -> 156 us (0.975)
  the two profiles are of different devices: /device:TPU:16 before, /device:TPU:68 now
where the time goes in v9:
time: 156 us
  starting transfers between devices  53.1 us (34%)
  waiting for transfers between devices  48.4 us (31%)
  blocking collectives  28.6 us (18%)
  Pallas kernels  12.3 us (8%)
  local copies, waits for them, and re-layouts  11.5 us (7%)
    ppermute x4, waiting for transfers between devices, paired(): return lax.ppermute(x, axes, pairs)  33.6 us
    all_to_all x1, blocking collectives, gather_latents(): block = lax.all_to_all(copies, axis, 0, 0, tiled=True)  28.6 us
    ppermute x4, starting transfers between devices, paired(): return lax.ppermute(x, axes, pairs)  26.2 us
    ppermute x4, starting transfers between devices, swap(): return lax.ppermute(x, axis, [(i, i ^ bit) for i in range(SIZE[axis])])  15.6 us
    pallas_call x3, Pallas kernels, call(): pl.pallas_call(kernel, out_shape=shapes, in_specs=specs, out_specs=jax.tr...  12.3 us
    unnamed x17, local copies, waits for them, and re-layouts  8.98 us
    all_to_all x1, starting transfers between devices, body(): lax.all_to_all(lat_term.reshape(4, half, rows), 'section', 0, 0, tiled=True)  6.47 us
    all_to_all x1, waiting for transfers between devices, body(): lax.all_to_all(lat_term.reshape(4, half, rows), 'section', 0, 0, tiled=True)  6.43 us
  transfers between devices with their start and end apart: 10, of which 6 were waited for; matrix products, arithmetic and copies ran while one was open for 4% of the time, Pallas kernels for 2%

profile of v9, /device:TPU:68, one launch (start us, length us, event | category | flops | bytes accessed | tf_op | source)
XLA Modules:
  0.0 155.6 jit_solution(1064970240970529597)
XLA Ops:
  0.6 0.8 copy.9
  1.5 0.1 reshape.198
  1.6 28.6 %all_to_all.15 = bf16[8,48,384]{2,1,0:T(8,128)(2,1)S(1)} all-to-all(bf16[8,48,384]{2,1,0:T(8,128)(2,1)S(1)} %broadcast_in_dim.6), channel_id=1, replica_groups=mesh['zh'=4,'y'=4,'core'=2,'section'=4,'mp'=8] {'mp'}, dimensions={0} | all-to-all | bytes 589824 | tf_op jit(solution)/shard_map/all_to_all | solution.py:54
  30.2 1.1 broadcast_in_dim.14
  31.4 4.8 %all-to-all-start.1 = ((bf16[4,384,384]{2,1,0:T(8,128)(2,1)}), bf16[4,384,384]{2,1,0:T(8,128)(2,1)S(1)}, u32[]{:S(2)}, u32[]{:S(2)}) async-start(bf16[4,384,384]{2,1,0:T(8,128)(2,1)} %broadcast_in_dim.14), calls=%async_computation.1 | async-start | bytes 2359296 | tf_op jit(solution)/shard_map/all_to_all | solution.py:54
  36.4 0.1 add.105.blocks
  36.5 4.4 %copy.11 = bf16[192,8,2,512]{3,1,2,0:T(8,128)(2,1)} copy(bf16[192,8,2,512]{3,2,1,0:T(2,128)(2,1)} %bitcast.41) | data formatting | bytes 6291456
  40.9 6.0 %all-to-all-done.1 = bf16[4,384,384]{2,1,0:T(8,128)(2,1)S(1)} async-done(((bf16[4,384,384]{2,1,0:T(8,128)(2,1)}), bf16[4,384,384]{2,1,0:T(8,128)(2,1)S(1)}, u32[]{:S(2)}, u32[]{:S(2)}) %all-to-all-start.1) | async-done | bytes 1179680 | tf_op jit(solution)/shard_map/all_to_all | solution.py:54
  47.0 1.9 %copy-done = bf16[192,8,2,512]{3,1,2,0:T(8,128)(2,1)S(1)} copy-done((bf16[192,8,2,512]{3,1,2,0:T(8,128)(2,1)S(1)}, bf16[192,8,2,512]{3,1,2,0:T(8,128)(2,1)}, u32[]{:S(2)}) %copy-start) | copy-done | bytes 3145752
  48.8 8.6 %shard_map.85 = (bf16[2,128,512]{2,1,0:T(8,128)(2,1)}, bf16[384,1024]{1,0:T(8,128)(2,1)S(1)}, bf16[768,1024]{1,0:T(8,128)(2,1)}, bf16[1536,384]{1,0:T(8,128)(2,1)}) custom-call(s32[2]{0:T(128)S(1)} %copy-done.6, s32[16]{0:T(128)S(1)} %add.105.blocks, bf16[1536,384]{1,0:T(8,128)(2,1)S(1)} %bitcast.35, bf16[1536,1024]{1,0:T(8,128)(2,1)S(1)} %bitcast.37, ...), custom_call_target="tpu_custom_call" | custom-call | flops 3019898880 | bytes 4850760 | tf_op jit(solution)/shard_map/pallas_call | solution.py:115
  57.4 1.9 %collective-permute-start = (bf16[768,1024]{1,0:T(8,128)(2,1)}, bf16[768,1024]{1,0:T(8,128)(2,1)}, u32[]{:S(2)}, u32[]{:S(2)}) collective-permute-start(bf16[768,1024]{1,0:T(8,128)(2,1)} %get-tuple-element.11), channel_id=1, source_target_pairs={{0,32},{32,0},{1,33},{33,1},{2,34},{34,2},{3,35},{35,3},{4,36},{36... | collective-permute-start | bytes 4718600 | tf_op jit(solution)/shard_map/ppermute | solution.py:47
  59.3 6.5 %all-to-all-start.2 = ((bf16[4,384,384]{2,1,0:T(8,128)(2,1)}), bf16[4,384,384]{2,1,0:T(8,128)(2,1)S(1)}, u32[]{:S(2)}, u32[]{:S(2)}) async-start(bf16[4,384,384]{2,1,0:T(8,128)(2,1)} %bitcast.15), calls=%async_computation.2 | async-start | bytes 2359296 | tf_op jit(solution)/shard_map/all_to_all | solution.py:174
  65.9 3.1 %shard_map.86 = (f32[384,1024]{1,0:T(8,128)S(1)}, bf16[384,1024]{1,0:T(8,128)(2,1)}) custom-call(s32[16]{0:T(128)S(1)} %add.111.blocks, bf16[1536,384]{1,0:T(8,128)(2,1)S(1)} %bitcast.36, bf16[384,1024]{1,0:T(8,128)(2,1)S(1)} %get-tuple-element.10.dflat, bf16[768,1024]{1,0:T(8,128)(2,1)} %collective-permute-done.other), custom_call_target="tpu_custom_call" | custom-call | flops 603979776 | bytes 3539008 | tf_op jit(solution)/shard_map/pallas_call | solution.py:115
  69.0 1.2 copy-done.1
  70.2 3.6 %collective-permute-start.1 = (bf16[384,1024]{1,0:T(8,128)(2,1)}, bf16[384,1024]{1,0:T(8,128)(2,1)S(1)}, u32[]{:S(2)}, u32[]{:S(2)}) collective-permute-start(bf16[384,1024]{1,0:T(8,128)(2,1)} %get-tuple-element.13), channel_id=1, source_target_pairs={{0,64},{32,224},{64,0},{96,160},{128,192},{160,96},{192,128},{224,... | collective-permute-start | bytes 2359304 | tf_op jit(solution)/shard_map/ppermute | solution.py:43
  73.8 6.4 %all-to-all-done.2.parts = bf16[4,384,384]{2,1,0:T(8,128)(2,1)S(1)} async-done(((bf16[4,384,384]{2,1,0:T(8,128)(2,1)}), bf16[4,384,384]{2,1,0:T(8,128)(2,1)S(1)}, u32[]{:S(2)}, u32[]{:S(2)}) %all-to-all-start.2) | async-done | bytes 1179680 | tf_op jit(solution)/shard_map/all_to_all | solution.py:174
  80.3 0.7 shard_map.87
  81.0 2.4 %collective-permute-start.5 = (bf16[4,48,384]{2,1,0:T(8,128)(2,1)S(1)}, bf16[4,48,384]{2,1,0:T(8,128)(2,1)S(1)}, u32[]{:S(2)}, u32[]{:S(2)}) collective-permute-start(bf16[4,48,384]{2,1,0:T(8,128)(2,1)S(1)} %bitcast.44), channel_id=1, source_target_pairs={{0,1},{1,0},{2,3},{3,2},{4,5},{5,4},{6,7},{7,6},{8,9},{9,8},{10,11... | collective-permute-start | bytes 442376 | tf_op jit(solution)/shard_map/ppermute | solution.py:47
  83.4 1.0 collective-permute-done.1
  84.4 0.2 convert_add_fusion
  84.7 4.9 %collective-permute-start.2 = (bf16[192,1024]{1,0:T(8,128)(2,1)S(1)}, bf16[192,1024]{1,0:T(8,128)(2,1)S(1)}, u32[]{:S(2)}, u32[]{:S(2)}) collective-permute-start(bf16[192,1024]{1,0:T(8,128)(2,1)S(1)} %slice.94), channel_id=1, source_target_pairs={{0,192},{32,96},{64,128},{96,32},{128,64},{160,224},{192,0},{224,1... | collective-permute-start | bytes 1179656 | tf_op jit(solution)/shard_map/ppermute | solution.py:43
  89.7 4.9 %collective-permute-start.6 = (bf16[2,48,384]{2,1,0:T(8,128)(2,1)S(1)}, bf16[2,48,384]{2,1,0:T(8,128)(2,1)S(1)}, u32[]{:S(2)}, u32[]{:S(2)}) collective-permute-start(bf16[2,48,384]{2,1,0:T(8,128)(2,1)S(1)} %slice.98), channel_id=1, source_target_pairs={{0,2},{1,3},{2,0},{3,1},{4,6},{5,7},{6,4},{7,5},{8,10},{9,11},{10,... | collective-permute-start | bytes 221192 | tf_op jit(solution)/shard_map/ppermute | solution.py:47
  94.6 2.4 %collective-permute-done.6 = bf16[2,48,384]{2,1,0:T(8,128)(2,1)S(1)} collective-permute-done((bf16[2,48,384]{2,1,0:T(8,128)(2,1)S(1)}, bf16[2,48,384]{2,1,0:T(8,128)(2,1)S(1)}, u32[]{:S(2)}, u32[]{:S(2)}) %collective-permute-start.6) | collective-permute-done | bytes 73760 | tf_op jit(solution)/shard_map/ppermute | solution.py:47
  97.0 0.1 slice_add_fusion
  97.2 15.7 %collective-permute-start.3 = (bf16[96,1024]{1,0:T(8,128)(2,1)S(1)}, bf16[96,1024]{1,0:T(8,128)(2,1)S(1)}, u32[]{:S(2)}, u32[]{:S(2)}) collective-permute-start(bf16[96,1024]{1,0:T(8,128)(2,1)S(1)} %slice.95), channel_id=1, source_target_pairs={{0,256},{32,800},{256,0},{288,544},{512,768},{544,288},{768,512},{... | collective-permute-start | bytes 589832 | tf_op jit(solution)/shard_map/ppermute | solution.py:43
  112.9 6.5 %collective-permute-start.7 = (bf16[48,384]{1,0:T(8,128)(2,1)S(1)}, bf16[48,384]{1,0:T(8,128)(2,1)S(1)}, u32[]{:S(2)}, u32[]{:S(2)}) collective-permute-start(bf16[48,384]{1,0:T(8,128)(2,1)S(1)} %fusion.2), channel_id=1, source_target_pairs={{0,4},{1,5},{2,6},{3,7},{4,0},{5,1},{6,2},{7,3},{8,12},{9,13},{10,... | collective-permute-start | bytes 110600 | tf_op jit(solution)/shard_map/ppermute | solution.py:47
  119.4 11.7 %collective-permute-done.3 = bf16[96,1024]{1,0:T(8,128)(2,1)S(1)} collective-permute-done((bf16[96,1024]{1,0:T(8,128)(2,1)S(1)}, bf16[96,1024]{1,0:T(8,128)(2,1)S(1)}, u32[]{:S(2)}, u32[]{:S(2)}) %collective-permute-start.3) | collective-permute-done | bytes 196640 | tf_op jit(solution)/shard_map/ppermute | solution.py:43
  131.2 1.9 %collective-permute-start.4 = (bf16[48,1024]{1,0:T(8,128)(2,1)S(1)}, bf16[48,1024]{1,0:T(8,128)(2,1)S(1)}, u32[]{:S(2)}, u32[]{:S(2)}) collective-permute-start(bf16[48,1024]{1,0:T(8,128)(2,1)S(1)} %slice.97), channel_id=1, source_target_pairs={{0,768},{32,288},{256,512},{288,32},{512,256},{544,800},{768,0},{8... | collective-permute-start | bytes 294920 | tf_op jit(solution)/shard_map/ppermute | solution.py:43
  133.1 0.1 reshape.205
  133.2 0.6 copy.10
  133.9 20.9 %collective-permute-done.4 = bf16[48,1024]{1,0:T(8,128)(2,1)S(1)} collective-permute-done((bf16[48,1024]{1,0:T(8,128)(2,1)S(1)}, bf16[48,1024]{1,0:T(8,128)(2,1)S(1)}, u32[]{:S(2)}, u32[]{:S(2)}) %collective-permute-start.4) | collective-permute-done | bytes 98336 | tf_op jit(solution)/shard_map/ppermute | solution.py:43
  154.8 0.8 reshape.203
  (35 shorter events, 0.7 us)
Async XLA Ops:
  31.4 15.6 %all-to-all-start.1 = ((bf16[4,384,384]{2,1,0:T(8,128)(2,1)}), bf16[4,384,384]{2,1,0:T(8,128)(2,1)S(1)}, u32[]{:S(2)}, u32[]{:S(2)}) async-start(bf16[4,384,384]{2,1,0:T(8,128)(2,1)} %broadcast_in_dim.14), calls=%async_computation.1 | async-start | bytes 2359296 | tf_op jit(solution)/shard_map/all_to_all | solution.py:54
  36.5 10.4 %copy-start.3 = (bf16[1,2,128,512]{3,2,1,0:T(8,128)(2,1)S(1)}, bf16[1,2,128,512]{3,2,1,0:T(8,128)(2,1)}, u32[]{:S(2)}) copy-start(bf16[1,2,128,512]{3,2,1,0:T(8,128)(2,1)} %param.6) | copy-start | bytes 786436
  36.5 10.4 %copy-start.4 = (bf16[1,2,128,512]{3,2,1,0:T(8,128)(2,1)S(1)}, bf16[1,2,128,512]{3,2,1,0:T(8,128)(2,1)}, u32[]{:S(2)}) copy-start(bf16[1,2,128,512]{3,2,1,0:T(8,128)(2,1)} %param.11) | copy-start | bytes 786436
  36.5 10.4 %copy-start.5 = (s32[2,128]{1,0:T(2,128)S(1)}, s32[2,128]{1,0:T(2,128)}, u32[]{:S(2)}) copy-start(s32[2,128]{1,0:T(2,128)} %param.9) | copy-start | bytes 3076
  36.5 10.4 %copy-start.6 = (s32[2]{0:T(128)S(1)}, s32[2]{0:T(128)}, u32[]{:S(2)}) copy-start(s32[2]{0:T(128)} %counts.1) | copy-start | bytes 28
  46.9 1.9 %copy-start = (bf16[192,8,2,512]{3,1,2,0:T(8,128)(2,1)S(1)}, bf16[192,8,2,512]{3,1,2,0:T(8,128)(2,1)}, u32[]{:S(2)}) copy-start(bf16[192,8,2,512]{3,1,2,0:T(8,128)(2,1)} %copy.11) | copy-start | bytes 9437188
  57.4 8.6 %collective-permute-start = (bf16[768,1024]{1,0:T(8,128)(2,1)}, bf16[768,1024]{1,0:T(8,128)(2,1)}, u32[]{:S(2)}, u32[]{:S(2)}) collective-permute-start(bf16[768,1024]{1,0:T(8,128)(2,1)} %get-tuple-element.11), channel_id=1, source_target_pairs={{0,32},{32,0},{1,33},{33,1},{2,34},{34,2},{3,35},{35,3},{4,36},{36... | collective-permute-start | bytes 4718600 | tf_op jit(solution)/shard_map/ppermute | solution.py:47
  59.3 20.9 %all-to-all-start.2 = ((bf16[4,384,384]{2,1,0:T(8,128)(2,1)}), bf16[4,384,384]{2,1,0:T(8,128)(2,1)S(1)}, u32[]{:S(2)}, u32[]{:S(2)}) async-start(bf16[4,384,384]{2,1,0:T(8,128)(2,1)} %bitcast.15), calls=%async_computation.2 | async-start | bytes 2359296 | tf_op jit(solution)/shard_map/all_to_all | solution.py:174
  69.0 1.2 copy-start.1
  70.2 14.2 %copy-start.2 = (f32[384,1024]{1,0:T(8,128)S(1)}, f32[384,1024]{1,0:T(8,128)}, u32[]{:S(2)}) copy-start(f32[384,1024]{1,0:T(8,128)} %copy-done.1) | copy-start | bytes 4718596
  70.2 14.2 %collective-permute-start.1 = (bf16[384,1024]{1,0:T(8,128)(2,1)}, bf16[384,1024]{1,0:T(8,128)(2,1)S(1)}, u32[]{:S(2)}, u32[]{:S(2)}) collective-permute-start(bf16[384,1024]{1,0:T(8,128)(2,1)} %get-tuple-element.13), channel_id=1, source_target_pairs={{0,64},{32,224},{64,0},{96,160},{128,192},{160,96},{192,128},{224,... | collective-permute-start | bytes 2359304 | tf_op jit(solution)/shard_map/ppermute | solution.py:43
  81.0 8.6 %collective-permute-start.5 = (bf16[4,48,384]{2,1,0:T(8,128)(2,1)S(1)}, bf16[4,48,384]{2,1,0:T(8,128)(2,1)S(1)}, u32[]{:S(2)}, u32[]{:S(2)}) collective-permute-start(bf16[4,48,384]{2,1,0:T(8,128)(2,1)S(1)} %bitcast.44), channel_id=1, source_target_pairs={{0,1},{1,0},{2,3},{3,2},{4,5},{5,4},{6,7},{7,6},{8,9},{9,8},{10,11... | collective-permute-start | bytes 442376 | tf_op jit(solution)/shard_map/ppermute | solution.py:47
  84.7 12.3 %collective-permute-start.2 = (bf16[192,1024]{1,0:T(8,128)(2,1)S(1)}, bf16[192,1024]{1,0:T(8,128)(2,1)S(1)}, u32[]{:S(2)}, u32[]{:S(2)}) collective-permute-start(bf16[192,1024]{1,0:T(8,128)(2,1)S(1)} %slice.94), channel_id=1, source_target_pairs={{0,192},{32,96},{64,128},{96,32},{128,64},{160,224},{192,0},{224,1... | collective-permute-start | bytes 1179656 | tf_op jit(solution)/shard_map/ppermute | solution.py:43
  89.7 7.3 %collective-permute-start.6 = (bf16[2,48,384]{2,1,0:T(8,128)(2,1)S(1)}, bf16[2,48,384]{2,1,0:T(8,128)(2,1)S(1)}, u32[]{:S(2)}, u32[]{:S(2)}) collective-permute-start(bf16[2,48,384]{2,1,0:T(8,128)(2,1)S(1)} %slice.98), channel_id=1, source_target_pairs={{0,2},{1,3},{2,0},{3,1},{4,6},{5,7},{6,4},{7,5},{8,10},{9,11},{10,... | collective-permute-start | bytes 221192 | tf_op jit(solution)/shard_map/ppermute | solution.py:47
  97.2 33.9 %collective-permute-start.3 = (bf16[96,1024]{1,0:T(8,128)(2,1)S(1)}, bf16[96,1024]{1,0:T(8,128)(2,1)S(1)}, u32[]{:S(2)}, u32[]{:S(2)}) collective-permute-start(bf16[96,1024]{1,0:T(8,128)(2,1)S(1)} %slice.95), channel_id=1, source_target_pairs={{0,256},{32,800},{256,0},{288,544},{512,768},{544,288},{768,512},{... | collective-permute-start | bytes 589832 | tf_op jit(solution)/shard_map/ppermute | solution.py:43
  112.9 20.2 %collective-permute-start.7 = (bf16[48,384]{1,0:T(8,128)(2,1)S(1)}, bf16[48,384]{1,0:T(8,128)(2,1)S(1)}, u32[]{:S(2)}, u32[]{:S(2)}) collective-permute-start(bf16[48,384]{1,0:T(8,128)(2,1)S(1)} %fusion.2), channel_id=1, source_target_pairs={{0,4},{1,5},{2,6},{3,7},{4,0},{5,1},{6,2},{7,3},{8,12},{9,13},{10,... | collective-permute-start | bytes 110600 | tf_op jit(solution)/shard_map/ppermute | solution.py:47
  131.2 23.6 %collective-permute-start.4 = (bf16[48,1024]{1,0:T(8,128)(2,1)S(1)}, bf16[48,1024]{1,0:T(8,128)(2,1)S(1)}, u32[]{:S(2)}, u32[]{:S(2)}) collective-permute-start(bf16[48,1024]{1,0:T(8,128)(2,1)S(1)} %slice.97), channel_id=1, source_target_pairs={{0,768},{32,288},{256,512},{288,32},{512,256},{544,800},{768,0},{8... | collective-permute-start | bytes 294920 | tf_op jit(solution)/shard_map/ppermute | solution.py:43
